TPU v7x, 512 devices: a whole 4x4x16 slice. The times are simulated.
512 devices in a mesh: rep: 4 (over z_lo), tab: 8 (over z_hi, core), fsdp: 16 (over y, x).
Axes of the slice: x: 4, y: 4, z: 16 (z_hi: 4, z_lo: 4; z = z_hi * 4 + z_lo), core: 2. Of those that a mesh axis runs over, the one named last changes fastest.
Arguments:
- pooled: bfloat16 [16384, 128, 192], P(('rep', 'tab', 'fsdp')), may hold values from -6 to 6
- projection: bfloat16 [128, 16], replicated, may hold values from -0.0390625 to 0.0390625
- w_inner: bfloat16 [2048, 1024], P('fsdp'), may hold values from -0.125 to 0.125
- w_outer: bfloat16 [1024, 1536], P(None, 'fsdp'), may hold values from -0.1875 to 0.1875
- upstream: bfloat16 [16384, 1536], P(('rep', 'tab', 'fsdp')), may hold values from -24 to 24
- feature_order: int32 [128], replicated, may hold values from 0 to 127, each once
- bag_slots: int32 [4, 8, 512, 128, 4], P('rep', None, 'fsdp', 'tab'), may hold values from 0 to 1023
- bag_lengths: int32 [4, 8, 512, 128], P('rep', None, 'fsdp', 'tab'), may hold values from 1 to 4
Outputs:
- grad_inner: float32 [2048, 1024], P('fsdp')
- grad_outer: float32 [1024, 1536], P(None, 'fsdp')
- grad_proj: float32 [128, 16], replicated
- row_grads: float32 [8, 16, 1024, 192], P('tab', 'fsdp', 'rep')
Inputs may be any that keep to these rules, and one draw needn't show every extreme that they name: `bag_slots`: index into the deduplicated row list of the owning table shard; all replica groups share that list. `bag_lengths`: slots of a bag past its length are ignored. `feature_order`: each feature once.
All inputs are finite; a program needn't handle non-finite values.
Results may differ from a plain program's by a relative error of at most 0.03.
Values may be sent and summed in bfloat16 or wider, within the bound.
No kernel may reach another device: no remote copies, remote signals or barrier semaphores. Data moves between devices by JAX's collectives and lax.ppermute only.
A program may use at most 64 MiB of HBM per device.

v0:
```python
import math

import jax
import jax.numpy as jnp
from jax import lax
from jax.sharding import PartitionSpec as P

DEDUP = 1024


def rounded(values):
    return lax.optimization_barrier(values.astype(jnp.bfloat16)).astype(jnp.float32)


def body(pooled, projection, w_inner, w_outer, upstream, feature_order, bag_slots, bag_lengths):
    samples, features, emb_width = pooled.shape
    comp_rank = projection.shape[1]
    inner_full = lax.all_gather(w_inner, "fsdp", axis=0, tiled=True)
    compress = jnp.einsum(
        "bfe,fk->bek", pooled, projection, preferred_element_type=jnp.float32
    ).astype(jnp.bfloat16)
    zed = jnp.einsum("bfe,bek->bfk", pooled, compress, preferred_element_type=jnp.float32).astype(
        jnp.bfloat16
    )
    flattened = zed.reshape(samples, features * comp_rank)
    zed_cols, upper_cols = (
        lax.all_to_all(flattened, "fsdp", split_axis=1, concat_axis=0, tiled=True),
        lax.all_to_all(upstream, "fsdp", split_axis=1, concat_axis=0, tiled=True),
    )
    preact = jnp.dot(flattened, inner_full, preferred_element_type=jnp.float32)
    logistic = jax.nn.sigmoid(preact)
    activated = (preact * logistic).astype(jnp.bfloat16)
    grad_act = lax.dot_general(
        upstream,
        lax.all_gather(w_outer, "fsdp", axis=1, tiled=True),
        (((1,), (1,)), ((), ())),
        preferred_element_type=jnp.float32,
    )
    grad_pre = (grad_act * (logistic * (1.0 + preact * (1.0 - logistic)))).astype(jnp.bfloat16)
    grad_flat = lax.dot_general(
        grad_pre, inner_full, (((1,), (1,)), ((), ())), preferred_element_type=jnp.float32
    ).astype(jnp.bfloat16)
    grad_zed = grad_flat.reshape(samples, features, comp_rank)
    grad_comp = jnp.einsum(
        "bfe,bfk->bek", pooled, grad_zed, preferred_element_type=jnp.float32
    ).astype(jnp.bfloat16)
    pooled_grad = (
        jnp.einsum("bfk,bek->bfe", grad_zed, compress, preferred_element_type=jnp.float32)
        + jnp.einsum("fk,bek->bfe", projection, grad_comp, preferred_element_type=jnp.float32)
    ).astype(jnp.bfloat16)
    reordered = jnp.take(pooled_grad, feature_order, axis=1)
    owned = lax.all_to_all(reordered, "tab", split_axis=1, concat_axis=0, tiled=True)
    values = owned.astype(jnp.float32).reshape(-1, emb_width)
    bag_depth = bag_slots.shape[-1]
    slot_table = bag_slots.reshape(-1, bag_depth)
    live_counts = bag_lengths.reshape(-1)
    running = jnp.zeros((DEDUP, emb_width), jnp.float32)
    for slot_index in range(bag_depth):
        row_ids = jnp.where(slot_index < live_counts, slot_table[:, slot_index], DEDUP)
        running = running + jax.ops.segment_sum(values, row_ids, num_segments=DEDUP)
    row_share = lax.psum_scatter(
        running.astype(jnp.bfloat16), "rep", scatter_dimension=0, tiled=True
    ).astype(jnp.float32)
    act_all, pre_all = (
        lax.all_gather(activated, "fsdp", axis=0, tiled=True),
        lax.all_gather(grad_pre, "fsdp", axis=0, tiled=True),
    )
    part_inner = rounded(
        lax.dot_general(
            zed_cols, pre_all, (((0,), (0,)), ((), ())), preferred_element_type=jnp.float32
        )
    )
    part_outer = rounded(
        lax.dot_general(
            act_all, upper_cols, (((0,), (0,)), ((), ())), preferred_element_type=jnp.float32
        )
    )
    part_proj = jnp.einsum("bfe,bek->fk", pooled, grad_comp, preferred_element_type=jnp.float32)
    proj_sum = lax.psum(part_proj, ("rep", "tab", "fsdp"))
    share_inner, share_outer = (
        lax.psum(part_inner.astype(jnp.bfloat16), ("rep", "tab")).astype(jnp.float32),
        lax.psum(part_outer.astype(jnp.bfloat16), ("rep", "tab")).astype(jnp.float32),
    )
    all_samples = samples * lax.axis_size("rep") * lax.axis_size("tab") * lax.axis_size("fsdp")
    loss_scale = 1.0 / math.sqrt(all_samples)
    grad_inner = share_inner * loss_scale
    grad_outer = share_outer * loss_scale
    grad_proj = proj_sum * loss_scale
    row_grads = row_share.reshape(1, 1, row_share.shape[0], emb_width)
    return (grad_inner, grad_outer, grad_proj, row_grads)


def solution(mesh):
    in_specs = (
        P(("rep", "tab", "fsdp"), None, None),
        P(),
        P("fsdp", None),
        P(None, "fsdp"),
        P(("rep", "tab", "fsdp"), None),
        P(),
        P("rep", None, "fsdp", "tab", None),
        P("rep", None, "fsdp", "tab"),
    )
    out_specs = (P("fsdp", None), P(None, "fsdp"), P(), P("tab", "fsdp", "rep", None))
    return jax.shard_map(body, mesh=mesh, in_specs=in_specs, out_specs=out_specs, check_vma=False)
```

profile of v0, /device:TPU:1, one launch (start us, length us, event | category | flops | bytes accessed | tf_op | source)
XLA Modules:
  0.0 558.1 jit_solution(9252963438397087237)
XLA Ops:
  8.7 1.0 all_to_all.39
  10.4 7.6 %all-to-all-start.1 = ((bf16[32,16,96]{2,0,1:T(8,128)(2,1)}), bf16[32,16,96]{2,0,1:T(8,128)(2,1)}, u32[]{:S(2)}, u32[]{:S(2)}) async-start(bf16[32,16,96]{2,0,1:T(8,128)(2,1)} %copy.67), calls=%async_computation.1 | async-start | bytes 262144 | tf_op jit(solution)/shard_map/all_to_all | solution.py:28
  18.1 1.6 convolution_convert_fusion.3
  21.6 61.6 %all-gather.7.cloned.1.call-done = bf16[2048,1024]{1,0:T(8,128)(2,1)} async-done(((bf16[128,1024]{1,0:T(8,128)(2,1)}), bf16[2048,1024]{1,0:T(8,128)(2,1)}) %all-gather.7.cloned.1.call-update) | async-done | bytes 4194320 | tf_op jit(solution)/shard_map/all_gather | solution.py:18
  83.2 3.7 multiply_convert_fusion
  86.9 62.1 %all-gather.5.cloned.1.call-done = bf16[1024,1536]{0,1:T(8,128)(2,1)} async-done(((bf16[1024,96]{0,1:T(8,128)(2,1)}), bf16[1024,1536]{0,1:T(8,128)(2,1)}) %all-gather.5.cloned.1.call-update) | async-done | bytes 3145744 | tf_op jit(solution)/shard_map/all_gather | solution.py:35
  149.0 2.5 fusion.3
  151.5 3.5 convolution_convert_fusion
  158.1 3.0 copy.73
  161.1 3.6 gather_fusion
  164.7 4.1 all-to-all-start
  168.8 3.2 select_bitcast_fusion
  172.0 3.7 all-to-all-done
  175.7 14.7 %all-to-all-start.2 = ((bf16[32,128,192]{2,0,1:T(8,128)(2,1)}), bf16[32,128,192]{2,0,1:T(8,128)(2,1)}, u32[]{:S(2)}, u32[]{:S(2)}) async-start(bf16[32,128,192]{2,0,1:T(8,128)(2,1)} %select_bitcast_fusion), calls=%async_computation.2 | async-start | bytes 4194304 | tf_op jit(solution)/shard_map/all_to_all | solution.py:52
  193.4 54.6 %all-gather.9.cloned.1.call-done = bf16[512,1024]{1,0:T(8,128)(2,1)} async-done(((bf16[32,1024]{1,0:T(8,128)(2,1)}), bf16[512,1024]{1,0:T(8,128)(2,1)}) %all-gather.9.cloned.1.call-update) | async-done | bytes 1048592 | tf_op jit(solution)/shard_map/all_gather | solution.py:66
  248.1 2.3 convolution_convert_fusion.2
  250.4 58.3 %all-gather.11.cloned.1.call-done = bf16[512,1024]{1,0:T(8,128)(2,1)} async-done(((bf16[32,1024]{1,0:T(8,128)(2,1)}), bf16[512,1024]{1,0:T(8,128)(2,1)}) %all-gather.11.cloned.1.call-update) | async-done | bytes 1048592 | tf_op jit(solution)/shard_map/all_gather | solution.py:65
  308.6 2.3 convolution_convert_fusion.4
  311.2 3.5 copy.74
  314.6 3.1 copy.75
  317.7 4.8 copy.76
  322.5 23.9 %scatter_custom_fusion.1 = f32[1024,192]{1,0:T(8,128)} fusion(s32[4096]{0:T(1024)S(1)} %bitcast.83, f32[4096,192]{1,0:T(8,128)} %bitcast.71, f32[]{:T(128)} %constant.13.clone.1), kind=kCustom, calls=%fused_computation.22 | custom fusion | flops 786432 | bytes 786944 | tf_op jit(solution)/shard_map/scatter-add | solution.py:60
  346.4 23.9 %scatter_custom_fusion = f32[1024,192]{1,0:T(8,128)} fusion(s32[4096]{0:T(1024)S(1)} %bitcast.82, f32[4096,192]{1,0:T(8,128)} %bitcast.72, f32[]{:T(128)} %constant.13.clone.1), kind=kCustom, calls=%fused_computation.24 | custom fusion | flops 786432 | bytes 786944 | tf_op jit(solution)/shard_map/scatter-add | solution.py:60
  370.2 23.8 %scatter_custom_fusion.3 = f32[1024,192]{1,0:T(8,128)} fusion(s32[4096]{0:T(1024)S(1)} %bitcast.81, f32[4096,192]{1,0:T(8,128)} %bitcast.73, f32[]{:T(128)} %constant.13.clone.1), kind=kCustom, calls=%fused_computation.20 | custom fusion | flops 786432 | bytes 786944 | tf_op jit(solution)/shard_map/scatter-add | solution.py:60
  394.1 1.7 add.46
  395.7 23.3 %scatter_fusion = f32[1024,192]{1,0:T(8,128)S(1)} fusion(f32[1024,192]{1,0:T(8,128)S(1)} %add.46, s32[4096]{0:T(1024)S(1)} %bitcast.80, f32[4096,192]{1,0:T(8,128)} %bitcast.74), kind=kCustom, calls=%fused_computation.3 | custom fusion | flops 786432 | bytes 9453568 | tf_op jit(solution)/shard_map/scatter-add | solution.py:60
  419.0 2.1 add_convert_fusion
  421.5 105.3 %psum.23 = f32[128,16]{0,1:T(8,128)S(1)} all-reduce(f32[128,16]{0,1:T(8,128)S(1)} %convolution_bitcast_fusion), channel_id=1, replica_groups=mesh['rep'=4,'tab'=8,'fsdp'=16] {'rep','tab','fsdp'}, use_global_device_ids=true, to_apply=%region_2.3 | all-reduce | flops 2048 | bytes 16384 | tf_op jit(solution)/shard_map/psum | solution.py:79
  527.4 1.7 convert_multiply_fusion.1
  529.1 1.8 convert_multiply_fusion
  530.9 18.6 %reduce-scatter.2.cloned.1.call-done = bf16[256,192]{1,0:T(8,128)(2,1)} async-done(((bf16[1024,192]{1,0:T(8,128)(2,1)}), bf16[256,192]{1,0:T(8,128)(2,1)}) %reduce-scatter.2.cloned.1.call-update) | async-done | bytes 98320 | tf_op jit(solution)/shard_map/reduce_scatter | solution.py:61
  549.6 0.9 bitcast_convert_fusion
  (56 shorter events, 12.0 us)
Async XLA Ops:
  7.2 10.9 %copy-start = (bf16[32,128,192]{1,2,0:T(8,128)(2,1)S(1)}, bf16[32,128,192]{1,2,0:T(8,128)(2,1)}, u32[]{:S(2)}) copy-start(bf16[32,128,192]{1,2,0:T(8,128)(2,1)} %param.8) | copy-start | bytes 4718596
  7.2 14.4 %copy-start.6 = (s32[128]{0:T(128)S(1)}, s32[128]{0:T(128)}, u32[]{:S(2)}) copy-start(s32[128]{0:T(128)} %param.13) | copy-start | bytes 1540
  7.2 76.0 %all-gather.7.cloned.1.call-start = ((), (), s32[]{:S(2)}) async-start(), calls=%async_computation.5 | async-start | bytes 4456448 | tf_op jit(solution)/shard_map/all_gather | solution.py:18
  7.9 141.1 %all-gather.5.cloned.1.call-start = ((), (), s32[]{:S(2)}) async-start(), calls=%async_computation.4 | async-start | bytes 3342336 | tf_op jit(solution)/shard_map/all_gather | solution.py:35
  10.4 154.3 %all-to-all-start.1 = ((bf16[32,16,96]{2,0,1:T(8,128)(2,1)}), bf16[32,16,96]{2,0,1:T(8,128)(2,1)}, u32[]{:S(2)}, u32[]{:S(2)}) async-start(bf16[32,16,96]{2,0,1:T(8,128)(2,1)} %copy.67), calls=%async_computation.1 | async-start | bytes 262144 | tf_op jit(solution)/shard_map/all_to_all | solution.py:28
  20.2 128.8 %copy-start.2 = (bf16[32,1536]{1,0:T(8,128)(2,1)S(1)}, bf16[32,1536]{1,0:T(8,128)(2,1)}, u32[]{:S(2)}) copy-start(bf16[32,1536]{1,0:T(8,128)(2,1)} %param.12) | copy-start | bytes 294916
  151.5 5.0 copy-start.1
  155.4 2.1 copy-start.5
  164.7 11.0 %all-to-all-start = ((bf16[32,16,128]{2,0,1:T(8,128)(2,1)}), bf16[32,16,128]{2,0,1:T(8,128)(2,1)S(1)}, u32[]{:S(2)}, u32[]{:S(2)}) async-start(bf16[32,16,128]{2,0,1:T(8,128)(2,1)} %copy.65), calls=%async_computation | async-start | bytes 262144 | tf_op jit(solution)/shard_map/all_to_all | solution.py:27
  172.0 19.8 %copy-start.4 = (s32[1,8,32,16]{2,3,1,0:T(8,128)S(1)}, s32[1,8,32,16]{2,3,1,0:T(8,128)}, u32[]{:S(2)}) copy-start(s32[1,8,32,16]{2,3,1,0:T(8,128)} %param.15) | copy-start | bytes 49156
  172.0 20.8 %copy-start.3 = (s32[1,8,32,16,4]{2,4,3,1,0:T(4,128)S(1)}, s32[1,8,32,16,4]{2,4,3,1,0:T(4,128)}, u32[]{:S(2)}) copy-start(s32[1,8,32,16,4]{2,4,3,1,0:T(4,128)} %param.14) | copy-start | bytes 196612
  175.7 135.5 %all-to-all-start.2 = ((bf16[32,128,192]{2,0,1:T(8,128)(2,1)}), bf16[32,128,192]{2,0,1:T(8,128)(2,1)}, u32[]{:S(2)}, u32[]{:S(2)}) async-start(bf16[32,128,192]{2,0,1:T(8,128)(2,1)} %select_bitcast_fusion), calls=%async_computation.2 | async-start | bytes 4194304 | tf_op jit(solution)/shard_map/all_to_all | solution.py:52
  190.4 57.7 %all-gather.9.cloned.1.call-start = ((), (), s32[]{:S(2)}) async-start(), calls=%async_computation.6 | async-start | bytes 1114112 | tf_op jit(solution)/shard_map/all_gather | solution.py:66
  191.1 117.5 %all-gather.11.cloned.1.call-start = ((), (), s32[]{:S(2)}) async-start(), calls=%async_computation.7 | async-start | bytes 1114112 | tf_op jit(solution)/shard_map/all_gather | solution.py:65
  191.7 335.7 %all-reduce.3.cloned.1.call-start = ((), (), s32[]{:S(2)}) async-start(), calls=%async_computation.9 | async-start | bytes 917504 | tf_op jit(solution)/shard_map/psum | solution.py:81
  310.9 238.6 %reduce-scatter.2.cloned.1.call-start = ((), (), s32[]{:S(2)}) async-start(), calls=%async_computation.8 | async-start | bytes 655360 | tf_op jit(solution)/shard_map/reduce_scatter | solution.py:61
Sparse Core Ops, SparseCore 0:
  11.0 72.1 all-gather.6
  86.2 62.7 all-gather.4
  194.2 53.8 all-gather.8
  251.5 57.0 all-gather.10
  311.5 205.2 all-reduce.2
  519.7 29.8 reduce-scatter.1
where the time goes:
time: 560 us; the launch traced here: 558 us
  waiting for transfers between devices  262 us (47%)
  other arithmetic  107 us (19%)
  blocking collectives  105 us (19%)
  starting transfers between devices  26.8 us (5%)
  local copies, waits for them, and re-layouts  24.1 us (4%)
  matrix products  19 us (3%)
  between operations  14.4 us (3%)
    psum x1, blocking collectives, body(): proj_sum = lax.psum(part_proj, ('rep', 'tab', 'fsdp'))  105 us
    scatter-add x4, other arithmetic, body(): running = running + jax.ops.segment_sum(values, row_ids, num_segments=DEDUP)  94.8 us
    all_gather x1, waiting for transfers between devices, body(): lax.all_gather(w_outer, 'fsdp', axis=1, tiled=True)  62.1 us
    all_gather x1, waiting for transfers between devices, body(): inner_full = lax.all_gather(w_inner, 'fsdp', axis=0, tiled=True)  61.6 us
    all_gather x1, waiting for transfers between devices, body(): lax.all_gather(activated, 'fsdp', axis=0, tiled=True)  58.3 us
    all_gather x1, waiting for transfers between devices, body(): lax.all_gather(grad_pre, 'fsdp', axis=0, tiled=True)  54.6 us
    reduce_scatter x1, waiting for transfers between devices, body(): lax.psum_scatter(running.astype(jnp.bfloat16), 'rep', scatter_dimension=0...  18.6 us
    all_to_all x1, starting transfers between devices, body(): lax.all_to_all(reordered, 'tab', split_axis=1, concat_axis=0, tiled=True)  14.7 us
  transfers between devices with their start and end apart: 9, of which 6 were waited for; matrix products, arithmetic and copies ran while one was open for 26% of the time, Pallas kernels for 0%

commit v1 on v0

v1 whole, which is shorter than its diff:
```python
import math

import jax
import jax.numpy as jnp
from jax import lax
from jax.experimental import pallas as pl
from jax.experimental.pallas import tpu as pltpu
from jax.sharding import PartitionSpec as P

DEDUP = 1024
BF = jnp.bfloat16
F32 = jnp.float32
ZT = ("rep", "tab")
N_REP, N_TAB = 4, 8
TEAM = [[(2 * a + b) * 8 + 2 * h + c for b in range(2) for c in range(2)] for a in range(2) for h in range(4)]
PEERS = [[(2 * a + b) * 8 + 2 * h + c for a in range(2) for h in range(4)] for b in range(2) for c in range(2)]


def exchange(pieces, axis, groups=None):
    return lax.all_to_all(pieces, axis, 0, 0, axis_index_groups=groups)


def spread(block, count, axis, groups=None):
    return exchange(jnp.broadcast_to(block[None], (count,) + block.shape), axis, groups)


def swap(block, k):
    pairs = [(r * 8 + t, (r ^ (k >> 1)) * 8 + (t ^ (k & 1))) for r in range(N_REP) for t in range(N_TAB)]
    return lax.ppermute(block, ZT, pairs)


def pooled_kernel(left_ref, right_ref, *out_refs):
    samples = left_ref.shape[0]
    half = samples // 2

    def step(i, _):
        both = []
        for sample in (i, i + half):
            grads = jnp.dot(left_ref[sample], right_ref[sample], preferred_element_type=F32).astype(BF)
            rows = pl.ds(pl.multiple_of(sample * 16, 16), 16)
            for k, out_ref in enumerate(out_refs):
                out_ref[rows, :] = grads[16 * k : 16 * k + 16, :128]
            both.append(grads[:, 128:])
        tail = jnp.concatenate(both, axis=1)
        rows = pl.ds(pl.multiple_of(samples * 16 + i * 16, 16), 16)
        for k, out_ref in enumerate(out_refs):
            out_ref[rows, :] = tail[16 * k : 16 * k + 16, :]
        return 0

    lax.fori_loop(0, half, step, 0)


def pooled_grads(left, right):
    samples = left.shape[0]
    return pl.pallas_call(
        pooled_kernel,
        out_shape=[jax.ShapeDtypeStruct((samples * 24, 128), BF)] * 8,
        in_specs=[pl.BlockSpec(memory_space=pltpu.VMEM)] * 2,
        out_specs=[pl.BlockSpec(memory_space=pltpu.VMEM)] * 8,
        compiler_params=pltpu.CompilerParams(vmem_limit_bytes=16 * 1024 * 1024),
        cost_estimate=pl.CostEstimate(flops=2 * samples * 128 * 256 * 128, bytes_accessed=4 << 20, transcendentals=0),
        name="pooled_grads",
    )(left, right)


def counts_kernel(index_ref, slots_ref, out_ref):
    rows = out_ref.shape[1]
    base = pl.program_id(1) * rows
    ids = lax.broadcasted_iota(jnp.int32, (rows, out_ref.shape[2]), 0) + base
    total = jnp.zeros(ids.shape, F32)
    for bag in range(4):
        total = total + jnp.where(ids == slots_ref[0, bag : bag + 1, :], 1.0, 0.0)
    out_ref[0] = total.astype(BF)


def slot_counts(index, slots):
    sources, _, width = slots.shape
    return pl.pallas_call(
        counts_kernel,
        grid_spec=pltpu.PrefetchScalarGridSpec(
            num_scalar_prefetch=1,
            grid=(sources, 4),
            in_specs=[pl.BlockSpec((1, 4, width), lambda s, m, index: (index[s], 0, 0))],
            out_specs=pl.BlockSpec((1, DEDUP // 4, width), lambda s, m, index: (s, m, 0)),
        ),
        out_shape=jax.ShapeDtypeStruct((sources, DEDUP, width), BF),
        compiler_params=pltpu.CompilerParams(vmem_limit_bytes=16 * 1024 * 1024),
        cost_estimate=pl.CostEstimate(flops=20 << 20, bytes_accessed=16 << 20, transcendentals=0),
        name="slot_counts",
    )(index, slots)


def segment_kernel(counts_ref, *refs):
    value_refs, (out_ref, total_ref) = refs[:8], refs[8:]
    source = pl.program_id(0)
    half = counts_ref.shape[2] // 2

    @pl.when(source == 0)
    def _():
        total_ref[...] = jnp.zeros_like(total_ref)

    for k, values_ref in enumerate(value_refs):

        @pl.when(source == k)
        def _(values_ref=values_ref):
            tail = values_ref[2 * half :, :]
            for part in range(2):
                head = values_ref[part * half : (part + 1) * half, :]
                total_ref[part] += jnp.dot(
                    counts_ref[0, :, part * half : (part + 1) * half],
                    jnp.concatenate([head, tail], axis=1),
                    preferred_element_type=F32,
                )

    @pl.when(source == pl.num_programs(0) - 1)
    def _():
        out_ref[:, :128] = (total_ref[0, :, :128] + total_ref[1, :, :128]).astype(BF)
        out_ref[:, 128:] = (total_ref[0, :, 128:192] + total_ref[1, :, 192:]).astype(BF)


def segment_sums(counts, values):
    sources, _, width = counts.shape
    return pl.pallas_call(
        segment_kernel,
        grid=(sources,),
        out_shape=jax.ShapeDtypeStruct((DEDUP, 192), BF),
        in_specs=[pl.BlockSpec((1, DEDUP, width), lambda s: (s, 0, 0))]
        + [pl.BlockSpec(memory_space=pltpu.VMEM)] * 8,
        out_specs=pl.BlockSpec((DEDUP, 192), lambda s: (0, 0)),
        scratch_shapes=[pltpu.VMEM((2, DEDUP, 256), F32)],
        compiler_params=pltpu.CompilerParams(vmem_limit_bytes=16 * 1024 * 1024),
        cost_estimate=pl.CostEstimate(flops=2 << 30, bytes_accessed=10 << 20, transcendentals=0),
        name="segment_sums",
    )(counts, *values)


def body(pooled, projection, w_inner, w_outer, upstream, feature_order, bag_slots, bag_lengths):
    samples, features, emb_width = pooled.shape
    rank = projection.shape[1]
    shards = lax.axis_size("fsdp")
    in_rows, units = w_inner.shape
    out_cols = w_outer.shape[1]
    flat, width = in_rows * shards, out_cols * shards
    grad_rows = in_rows + out_cols
    quarter = units // 4
    rep, tab = lax.axis_index("rep"), lax.axis_index("tab")
    far, core = tab // 2, tab % 2
    place = 2 * rep + core
    mine = place % 4

    weights = jnp.concatenate(
        [
            lax.dynamic_slice(w_inner, (0, mine * quarter), (in_rows, quarter)),
            lax.dynamic_slice(w_outer.T, (0, mine * quarter), (out_cols, quarter)),
        ]
    )
    weights = spread(weights, shards, "fsdp")
    inner = weights[:, :in_rows].reshape(flat, quarter)
    outer = weights[:, in_rows:].reshape(width, quarter)

    compress = jnp.einsum("bfe,fk->bek", pooled, projection, preferred_element_type=F32).astype(BF)
    zed = jnp.einsum("bfe,bek->bfk", pooled, compress, preferred_element_type=F32).astype(BF)
    joined = jnp.concatenate([zed.reshape(samples, flat), upstream], axis=1)

    bag = bag_slots.shape[-1]
    live = jnp.where(jnp.arange(bag) < bag_lengths[..., None], bag_slots, -1)
    live = live.reshape(4, 2, samples * 16, bag).transpose(0, 1, 3, 2)
    live, _ = lax.optimization_barrier((live, joined))
    near = []
    for k in range(4):
        piece = lax.dynamic_index_in_dim(live, rep ^ k, 0, False)
        near.append(lax.ppermute(piece, "rep", [(r, r ^ k) for r in range(4)]) if k else piece)
    across = [(r * 8 + 2 * f + c, f * 8 + 2 * r + c) for r in range(4) for f in range(4) for c in range(2)]
    slots = lax.ppermute(jnp.concatenate(near), ZT, across)
    sources = place ^ jnp.arange(8, dtype=jnp.int32)
    slot_index = (far ^ (sources // 2)) * 2 + sources % 2

    joined = jnp.concatenate([joined] + [swap(joined, k) for k in (1, 2, 3)], axis=0)
    joined, slots = lax.optimization_barrier((joined, slots))
    zed_all, up_all = joined[:, :flat], joined[:, flat:]

    preact = jnp.dot(zed_all, inner, preferred_element_type=F32)
    logistic = jax.nn.sigmoid(preact)
    activated = (preact * logistic).astype(BF)
    grad_act = jnp.dot(up_all, outer, preferred_element_type=F32)
    grad_pre = (grad_act * (logistic * (1.0 + preact * (1.0 - logistic)))).astype(BF)

    partial_zed = lax.dot_general(grad_pre, inner, (((1,), (1,)), ((), ())), preferred_element_type=F32).astype(BF)
    partial_zed = partial_zed.reshape(4, samples, flat)
    grad_zed = partial_zed[0].astype(F32)
    for k in (1, 2, 3):
        grad_zed = grad_zed + swap(partial_zed[k], k).astype(F32)
    grad_zed = grad_zed.astype(BF).reshape(samples, features, rank)

    grad_comp = jnp.einsum("bfe,bfk->bek", pooled, grad_zed, preferred_element_type=F32).astype(BF)
    order = feature_order.reshape(8, 16)
    order = jnp.concatenate([lax.dynamic_index_in_dim(order, place ^ k, 0, False) for k in range(8)])
    order = (order[:, None] == jnp.arange(features)[None, :]).astype(BF)
    ordered_zed = jnp.einsum("jf,bfk->bjk", order, grad_zed, preferred_element_type=F32).astype(BF)
    ordered_proj = jnp.dot(order, projection, preferred_element_type=F32).astype(BF)
    left = jnp.concatenate(
        [ordered_zed, jnp.broadcast_to(ordered_proj[None], (samples, features, rank))], axis=2
    )
    right = jnp.concatenate([compress, grad_comp], axis=2).transpose(0, 2, 1)
    routed = pooled_grads(left, right)
    slots, _ = lax.optimization_barrier((slots, routed[0]))
    counts = slot_counts(slot_index, slots)
    own_rows = routed[0]
    routed = [routed[0]] + [swap(routed[k], k) for k in range(1, 8)]
    sums = segment_sums(counts, routed).reshape(4, DEDUP // 4, emb_width)
    row_share = jnp.zeros((DEDUP // 4, emb_width), F32)
    for k in range(4):
        pairs = [
            (r * 8 + 2 * f + c, ((f + k) % 4) * 8 + 2 * r + c) for r in range(4) for f in range(4) for c in range(2)
        ]
        piece = lax.dynamic_index_in_dim(sums, (far + k) % 4, 0, False)
        row_share = row_share + lax.ppermute(piece, ZT, pairs).astype(F32)

    over_samples = (((0,), (0,)), ((), ()))
    part_inner = lax.dot_general(zed_all, grad_pre, over_samples, preferred_element_type=F32).astype(BF)
    part_outer = lax.dot_general(up_all, activated, over_samples, preferred_element_type=F32).astype(BF)
    parts = jnp.concatenate(
        [part_inner.reshape(shards, in_rows, quarter), part_outer.reshape(shards, out_cols, quarter)], axis=1
    )
    parts, _ = lax.optimization_barrier((exchange(parts, "fsdp"), own_rows))
    parts = jnp.sum(parts.astype(F32), axis=0).astype(BF)
    part_proj = jnp.einsum("bfe,bek->kf", pooled, grad_comp, preferred_element_type=F32)
    part_proj, _ = lax.optimization_barrier((part_proj, parts))
    proj_rows = jnp.sum(spread(part_proj, shards, "fsdp"), axis=0).reshape(8, 1, -1)
    proj_high = proj_rows.astype(BF)
    proj_low = (proj_rows - proj_high.astype(F32)).astype(BF)
    pieces = jnp.concatenate([parts.reshape(8, grad_rows // 8, quarter), proj_high, proj_low], axis=1)
    share = jnp.sum(exchange(pieces, ZT, PEERS).astype(F32), axis=0)
    proj_share = share[-2:-1] + share[-1:]
    share_high = proj_share.astype(BF)
    share_low = (proj_share - share_high.astype(F32)).astype(BF)
    share = spread(jnp.concatenate([share[:-2].astype(BF), share_high, share_low]), 8, ZT, PEERS)
    quarters = lax.all_gather(share, ZT, axis_index_groups=TEAM)
    proj_sum = jnp.sum(quarters[:, :, -2, :].astype(F32) + quarters[:, :, -1, :].astype(F32), axis=0)
    proj_sum = proj_sum.reshape(rank, features).T
    grads = quarters[:, :, :-2, :].reshape(4, grad_rows, quarter).transpose(1, 0, 2).reshape(grad_rows, units)

    all_samples = samples * lax.axis_size("rep") * lax.axis_size("tab") * lax.axis_size("fsdp")
    loss_scale = 1.0 / math.sqrt(all_samples)
    grad_inner = grads[:in_rows].astype(F32) * loss_scale
    grad_outer = (grads[in_rows:].astype(F32) * loss_scale).T
    grad_proj = proj_sum * loss_scale
    row_grads = row_share.reshape(1, 1, DEDUP // 4, emb_width)
    return (grad_inner, grad_outer, grad_proj, row_grads)


def solution(mesh):
    in_specs = (
        P(("rep", "tab", "fsdp"), None, None),
        P(),
        P("fsdp", None),
        P(None, "fsdp"),
        P(("rep", "tab", "fsdp"), None),
        P(),
        P("rep", None, "fsdp", "tab", None),
        P("rep", None, "fsdp", "tab"),
    )
    out_specs = (P("fsdp", None), P(None, "fsdp"), P(), P("tab", "fsdp", "rep", None))
    return jax.shard_map(body, mesh=mesh, in_specs=in_specs, out_specs=out_specs, check_vma=False)
```

time: 560 us -> 229 us (0.41)
  waiting for transfers between devices: 262 us -> 24.8 us
  starting transfers between devices: 26.8 us -> 135 us
  blocking collectives: 105 us -> 8.25 us
  other arithmetic: 107 us -> 11.7 us
  Pallas kernels: 0 us -> 15.9 us
  matrix products: 19 us -> 5.76 us
  between operations: 14.4 us -> 1.46 us
    all_gather x4 -> x0, waiting for transfers between devices: 237 us -> none  [the longest x1 62.1 us: body(): lax.all_gather(w_outer, 'fsdp', axis=1, tiled=True)]
    psum x1 -> x0, blocking collectives: 105 us -> none  [body(): proj_sum = lax.psum(part_proj, ('rep', 'tab', 'fsdp'))]
    scatter-add x4 -> x0, other arithmetic: 94.8 us -> none  [body(): running = running + jax.ops.segment_sum(values, row_ids, num_segments=DEDUP)]
    ppermute x0 -> x21, starting transfers between devices: none -> 83.4 us  [the longest x13 53.6 us: swap(): return lax.ppermute(block, ZT, pairs)]
    all_to_all x3 -> x5, starting transfers between devices: 26.4 us -> 51.9 us  [exchange(): return lax.all_to_all(pieces, axis, 0, 0, axis_index_groups=groups)]
    ppermute x0 -> x21, waiting for transfers between devices: none -> 24.8 us  [the longest x4 12.3 us: body(): row_share = row_share + lax.ppermute(piece, ZT, pairs).astype(F32)]
    reduce_scatter x1 -> x0, waiting for transfers between devices: 18.6 us -> none  [body(): lax.psum_scatter(running.astype(jnp.bfloat16), 'rep', scatter_dimension=0...]
    pallas_call x0 -> x3, Pallas kernels: none -> 15.9 us  [the longest x1 7.52 us: slot_counts(): pl.pallas_call(counts_kernel, grid_spec=pltpu.PrefetchScalarGridSpec(num_...]
  transfers between devices with their start and end apart: 9 -> 26, of which waited for: 6 -> 6; matrix products, arithmetic and copies ran while one was open for 26% -> 9% of each run, Pallas kernels for 0% -> 7%
where the time goes in v1:
time: 229 us; the launch traced here: 225 us
  starting transfers between devices  135 us (59%)
  waiting for transfers between devices  24.8 us (11%)
  local copies, waits for them, and re-layouts  22.3 us (10%)
  Pallas kernels  15.9 us (7%)
  other arithmetic  11.7 us (5%)
  blocking collectives  8.25 us (4%)
  matrix products  5.76 us (3%)
    ppermute x13, starting transfers between devices, swap(): return lax.ppermute(block, ZT, pairs)  53.6 us
    all_to_all x5, starting transfers between devices, exchange(): return lax.all_to_all(pieces, axis, 0, 0, axis_index_groups=groups)  51.9 us
    ppermute x4, starting transfers between devices, body(): row_share = row_share + lax.ppermute(piece, ZT, pairs).astype(F32)  17.9 us
    ppermute x4, waiting for transfers between devices, body(): row_share = row_share + lax.ppermute(piece, ZT, pairs).astype(F32)  12.3 us
    ppermute x3, starting transfers between devices, body(): lax.ppermute(piece, 'rep', [(r, r ^ k) for r in range(4)])  11.3 us
    ppermute x13, waiting for transfers between devices, swap(): return lax.ppermute(block, ZT, pairs)  10.7 us
    all_gather x1, blocking collectives, body(): quarters = lax.all_gather(share, ZT, axis_index_groups=TEAM)  8.25 us
    pallas_call x1, Pallas kernels, slot_counts(): pl.pallas_call(counts_kernel, grid_spec=pltpu.PrefetchScalarGridSpec(num_...  7.52 us
  transfers between devices with their start and end apart: 26, of which 6 were waited for; matrix products, arithmetic and copies ran while one was open for 9% of the time, Pallas kernels for 7%

profile of v1, /device:TPU:1, one launch (start us, length us, event | category | flops | bytes accessed | tf_op | source)
XLA Modules:
  0.0 225.5 jit_solution(7094041447606896134)
XLA Ops:
  3.9 7.7 %all-to-all-start = ((bf16[16,224,256]{2,1,0:T(8,128)(2,1)}), bf16[16,224,256]{2,1,0:T(8,128)(2,1)S(1)}, u32[]{:S(2)}, u32[]{:S(2)}) async-start(bf16[16,224,256]{2,1,0:T(8,128)(2,1)} %broadcast_in_dim.13), calls=%async_computation | async-start | bytes 3670016 | tf_op jit(solution)/shard_map/all_to_all | solution.py:20
  14.5 2.2 copy.58
  20.3 2.0 copy.60
  25.3 6.2 %collective-permute-start.5 = (s32[2,4,512]{2,1,0:T(4,128)S(1)}, s32[2,4,512]{2,1,0:T(4,128)S(1)}, u32[]{:S(2)}, u32[]{:S(2)}) collective-permute-start(s32[2,4,512]{2,1,0:T(4,128)S(1)} %get-tuple-element.40), channel_id=1, source_target_pairs={{0,384},{128,256},{256,128},{384,0},{1,385},{129,257},{257,129},{3... | collective-permute-start | bytes 49160 | tf_op jit(solution)/shard_map/ppermute | solution.py:172
  31.5 2.0 collective-permute-start.2
  33.5 4.4 %collective-permute-start.1 = (bf16[32,3584]{1,0:T(8,128)(2,1)}, bf16[32,3584]{1,0:T(8,128)(2,1)}, u32[]{:S(2)}, u32[]{:S(2)}) collective-permute-start(bf16[32,3584]{1,0:T(8,128)(2,1)} %pad_maximum_fusion.3), channel_id=1, source_target_pairs={{0,128},{16,144},{32,160},{48,176},{64,192},{80,208},{96,224},{112... | collective-permute-start | bytes 688136 | tf_op jit(solution)/shard_map/ppermute | solution.py:29
  37.9 1.9 collective-permute-start
  39.9 2.1 collective-permute-start.4
  42.1 3.0 %collective-permute-start.3 = (s32[2,4,512]{2,1,0:T(4,128)S(1)}, s32[2,4,512]{2,1,0:T(4,128)S(1)}, u32[]{:S(2)}, u32[]{:S(2)}) collective-permute-start(s32[2,4,512]{2,1,0:T(4,128)S(1)} %get-tuple-element.42), channel_id=1, source_target_pairs={{0,128},{128,0},{256,384},{384,256},{1,129},{129,1},{257,385},{385... | collective-permute-start | bytes 49160 | tf_op jit(solution)/shard_map/ppermute | solution.py:172
  47.7 2.3 %pad_maximum_fusion.1 = bf16[128,3584]{1,0:T(8,128)(2,1)} fusion(bf16[32,3584]{1,0:T(8,128)(2,1)} %collective-permute-done.2, bf16[32,3584]{1,0:T(8,128)(2,1)} %collective-permute-done.1, bf16[32,3584]{1,0:T(8,128)(2,1)} %collective-permute-done, bf16[32,1536]{1,0:T(8,128)(2,1)} %param.12, bf16[32,2048]{1,0:T(8,128)(2,1)} %copy.59), kind=kLoop, calls=%fused_computation.15 | loop fusion | flops 4587520 | bytes 1835008 | tf_op jit(solution)/shard_map/concatenate | solution.py:178
  54.5 6.7 %all-to-all-start.1 = ((bf16[16,224,256]{2,1,0:T(8,128)(2,1)}), bf16[16,224,256]{2,1,0:T(8,128)(2,1)}, u32[]{:S(2)}, u32[]{:S(2)}) async-start(bf16[16,224,256]{2,1,0:T(8,128)(2,1)} %pad_maximum_fusion), calls=%async_computation.1 | async-start | bytes 3670016 | tf_op jit(solution)/shard_map/all_to_all | solution.py:20
  61.2 12.4 %collective-permute-start.9 = (bf16[32,2048]{1,0:T(8,128)(2,1)S(1)}, bf16[32,2048]{1,0:T(8,128)(2,1)S(1)}, u32[]{:S(2)}, u32[]{:S(2)}) collective-permute-start(bf16[32,2048]{1,0:T(8,128)(2,1)S(1)} %get-tuple-element.37), channel_id=1, source_target_pairs={{0,144},{16,128},{32,176},{48,160},{64,208},{80,192},{96,240},{112... | collective-permute-start | bytes 393224 | tf_op jit(solution)/shard_map/ppermute | solution.py:29
  75.5 2.3 %collective-permute-start.7 = (bf16[32,2048]{1,0:T(8,128)(2,1)S(1)}, bf16[32,2048]{1,0:T(8,128)(2,1)S(1)}, u32[]{:S(2)}, u32[]{:S(2)}) collective-permute-start(bf16[32,2048]{1,0:T(8,128)(2,1)S(1)} %get-tuple-element.36), channel_id=1, source_target_pairs={{0,16},{16,0},{32,48},{48,32},{64,80},{80,64},{96,112},{112,96},{1... | collective-permute-start | bytes 393224 | tf_op jit(solution)/shard_map/ppermute | solution.py:29
  78.0 1.9 collective-permute-done.8
  82.7 4.6 %pooled_grads.1 = (bf16[768,128]{1,0:T(8,128)(2,1)S(1)}, bf16[768,128]{1,0:T(8,128)(2,1)S(1)}, bf16[768,128]{1,0:T(8,128)(2,1)S(1)}, bf16[768,128]{1,0:T(8,128)(...) custom-call(bf16[32,128,32]{2,1,0:T(8,128)(2,1)S(1)} %copy.64.left_r, ...), custom_call_target="tpu_custom_call" | custom-call | flops 268435456 | bytes 4194304 | tf_op jit(solution)/shard_map/pooled_grads/pallas_call | solution.py:55
  90.7 6.9 %all-to-all-start.2 = ((f32[16,16,128]{2,1,0:T(8,128)}), f32[16,16,128]{2,1,0:T(8,128)S(1)}, u32[]{:S(2)}, u32[]{:S(2)}) async-start(f32[16,16,128]{2,1,0:T(8,128)} %broadcast_in_dim.15), calls=%async_computation.2 | async-start | bytes 262144 | tf_op jit(solution)/shard_map/all_to_all | solution.py:20
  99.6 7.8 %collective-permute-start.11 = (bf16[768,128]{1,0:T(8,128)(2,1)S(1)}, bf16[768,128]{1,0:T(8,128)(2,1)S(1)}, u32[]{:S(2)}, u32[]{:S(2)}) collective-permute-start(bf16[768,128]{1,0:T(8,128)(2,1)S(1)} %get-tuple-element.26), channel_id=1, source_target_pairs={{0,128},{16,144},{32,160},{48,176},{64,192},{80,208},{96,224},{112... | collective-permute-start | bytes 589832 | tf_op jit(solution)/shard_map/ppermute | solution.py:29
  108.2 15.1 %all-to-all-start.3 = ((bf16[8,30,256]{2,1,0:T(8,128)(2,1)}), bf16[8,30,256]{2,1,0:T(8,128)(2,1)}, u32[]{:S(2)}, u32[]{:S(2)}) async-start(bf16[8,30,256]{2,1,0:T(8,128)(2,1)} %pad_maximum_fusion.4), calls=%async_computation.3 | async-start | bytes 262144 | tf_op jit(solution)/shard_map/all_to_all | solution.py:20
  123.3 2.3 %collective-permute-start.12 = (bf16[768,128]{1,0:T(8,128)(2,1)}, bf16[768,128]{1,0:T(8,128)(2,1)S(1)}, u32[]{:S(2)}, u32[]{:S(2)}) collective-permute-start(bf16[768,128]{1,0:T(8,128)(2,1)} %get-tuple-element.27), channel_id=1, source_target_pairs={{0,144},{16,128},{32,176},{48,160},{64,208},{80,192},{96,240},{112... | collective-permute-start | bytes 589832 | tf_op jit(solution)/shard_map/ppermute | solution.py:29
  125.6 4.5 %collective-permute-start.13 = (bf16[768,128]{1,0:T(8,128)(2,1)}, bf16[768,128]{1,0:T(8,128)(2,1)S(1)}, u32[]{:S(2)}, u32[]{:S(2)}) collective-permute-start(bf16[768,128]{1,0:T(8,128)(2,1)} %get-tuple-element.28), channel_id=1, source_target_pairs={{0,256},{16,272},{32,288},{48,304},{64,320},{80,336},{96,352},{112... | collective-permute-start | bytes 589832 | tf_op jit(solution)/shard_map/ppermute | solution.py:29
  130.2 4.2 %collective-permute-start.14 = (bf16[768,128]{1,0:T(8,128)(2,1)}, bf16[768,128]{1,0:T(8,128)(2,1)S(1)}, u32[]{:S(2)}, u32[]{:S(2)}) collective-permute-start(bf16[768,128]{1,0:T(8,128)(2,1)} %get-tuple-element.29), channel_id=1, source_target_pairs={{0,272},{16,256},{32,304},{48,288},{64,336},{80,320},{96,368},{112... | collective-permute-start | bytes 589832 | tf_op jit(solution)/shard_map/ppermute | solution.py:29
  134.4 3.1 %collective-permute-start.15 = (bf16[768,128]{1,0:T(8,128)(2,1)}, bf16[768,128]{1,0:T(8,128)(2,1)S(1)}, u32[]{:S(2)}, u32[]{:S(2)}) collective-permute-start(bf16[768,128]{1,0:T(8,128)(2,1)} %get-tuple-element.30), channel_id=1, source_target_pairs={{0,384},{16,400},{32,416},{48,432},{64,448},{80,464},{96,480},{112... | collective-permute-start | bytes 589832 | tf_op jit(solution)/shard_map/ppermute | solution.py:29
  137.5 4.7 %collective-permute-start.16 = (bf16[768,128]{1,0:T(8,128)(2,1)S(1)}, bf16[768,128]{1,0:T(8,128)(2,1)S(1)}, u32[]{:S(2)}, u32[]{:S(2)}) collective-permute-start(bf16[768,128]{1,0:T(8,128)(2,1)S(1)} %get-tuple-element.31), channel_id=1, source_target_pairs={{0,400},{16,384},{32,432},{48,416},{64,464},{80,448},{96,496},{112... | collective-permute-start | bytes 589832 | tf_op jit(solution)/shard_map/ppermute | solution.py:29
  142.4 7.5 %slot_counts.1.counts_ref = bf16[8,1024,512]{2,1,0:T(8,128)(2,1)S(1)} custom-call(s32[8]{0:T(128)S(1)} %fusion.16.index_ref, s32[8,4,512]{2,1,0:T(4,128)S(1)} %collective-permute-done.6.slots_ref), custom_call_target="tpu_custom_call" | custom-call | flops 20971520 | bytes 16777216 | tf_op jit(solution)/shard_map/slot_counts/pallas_call | solution.py:78
  150.0 8.8 %collective-permute-done.14.refs_5_ = bf16[768,128]{1,0:T(8,128)(2,1)S(1)} collective-permute-done((bf16[768,128]{1,0:T(8,128)(2,1)}, bf16[768,128]{1,0:T(8,128)(2,1)S(1)}, u32[]{:S(2)}, u32[]{:S(2)}) %collective-permute-start.14) | collective-permute-done | bytes 196640 | tf_op jit(solution)/shard_map/ppermute | solution.py:29
  161.9 3.9 %segment_sums.1 = bf16[1024,192]{1,0:T(8,128)(2,1)S(1)} custom-call(bf16[8,1024,512]{2,1,0:T(8,128)(2,1)S(1)} %slot_counts.1.counts_ref, bf16[768,128]{1,0:T(8,128)(2,1)S(1)} %get-tuple-element.20.refs_0_, bf16[768,128]{1,0:T(8,128)(2,1)S(1)} %collective-permute-done.10.refs_1_, bf16[768,128]{1,0:T(8,128)(2,1)S(1)} %collective-permute-done.11.refs_2_, ...), custom_call_target="tpu_custom_call" | custom-call | flops 2147483648 | bytes 10485760 | tf_op jit(solution)/shard_map/segment_sums/pallas_call | solution.py:123
  167.5 15.5 %all-to-all-start.4 = ((bf16[8,30,256]{2,1,0:T(8,128)(2,1)}), bf16[8,30,256]{2,1,0:T(8,128)(2,1)S(1)}, u32[]{:S(2)}, u32[]{:S(2)}) async-start(bf16[8,30,256]{2,1,0:T(8,128)(2,1)} %broadcast_in_dim.16), calls=%async_computation.4 | async-start | bytes 262144 | tf_op jit(solution)/shard_map/all_to_all | solution.py:20
  183.1 6.2 %collective-permute-start.20 = (bf16[256,192]{0,1:T(8,128)(2,1)S(1)}, bf16[256,192]{0,1:T(8,128)(2,1)S(1)}, u32[]{:S(2)}, u32[]{:S(2)}) collective-permute-start(bf16[256,192]{0,1:T(8,128)(2,1)S(1)} %bitcast.105), channel_id=1, source_target_pairs={{0,384},{16,400},{32,0},{48,16},{64,128},{80,144},{96,256},{112,27... | collective-permute-start | bytes 294920 | tf_op jit(solution)/shard_map/ppermute | solution.py:217
  189.4 9.1 %collective-permute-start.19 = (bf16[256,192]{0,1:T(8,128)(2,1)S(1)}, bf16[256,192]{0,1:T(8,128)(2,1)S(1)}, u32[]{:S(2)}, u32[]{:S(2)}) collective-permute-start(bf16[256,192]{0,1:T(8,128)(2,1)S(1)} %bitcast.106), channel_id=1, source_target_pairs={{0,256},{16,272},{32,384},{48,400},{64,0},{80,16},{96,128},{112,14... | collective-permute-start | bytes 294920 | tf_op jit(solution)/shard_map/ppermute | solution.py:217
  201.4 5.5 %collective-permute-done.19 = bf16[256,192]{0,1:T(8,128)(2,1)S(1)} collective-permute-done((bf16[256,192]{0,1:T(8,128)(2,1)S(1)}, bf16[256,192]{0,1:T(8,128)(2,1)S(1)}, u32[]{:S(2)}, u32[]{:S(2)}) %collective-permute-start.19) | collective-permute-done | bytes 98336 | tf_op jit(solution)/shard_map/ppermute | solution.py:217
  206.9 6.7 %collective-permute-done.18 = bf16[256,192]{0,1:T(8,128)(2,1)S(1)} collective-permute-done((bf16[256,192]{0,1:T(8,128)(2,1)S(1)}, bf16[256,192]{0,1:T(8,128)(2,1)S(1)}, u32[]{:S(2)}, u32[]{:S(2)}) %collective-permute-start.18) | collective-permute-done | bytes 98336 | tf_op jit(solution)/shard_map/ppermute | solution.py:217
  214.5 8.2 %all-gather = bf16[32,30,256]{2,0,1:T(8,128)(2,1)S(1)} all-gather(bf16[8,30,256]{2,0,1:T(8,128)(2,1)S(1)} %copy.67), channel_id=2, replica_groups={{0,16,128,144},{32,48,160,176},{64,80,192,208},{96,112,224,240},{256,27..., dimensions={0}, use_global_device_ids=true | all-gather | bytes 614400 | tf_op jit(solution)/shard_map/all_gather | solution.py:238
  (117 shorter events, 42.2 us)
Async XLA Ops:
  0.6 11.0 %copy-start = (bf16[32,128,192]{1,2,0:T(8,128)(2,1)S(1)}, bf16[32,128,192]{1,2,0:T(8,128)(2,1)}, u32[]{:S(2)}) copy-start(bf16[32,128,192]{1,2,0:T(8,128)(2,1)} %param.8) | copy-start | bytes 4718596
  3.9 7.8 %copy-start.11 = (bf16[128,16]{0,1:T(8,128)(2,1)S(1)}, bf16[128,16]{0,1:T(8,128)(2,1)}, u32[]{:S(2)}) copy-start(bf16[128,16]{0,1:T(8,128)(2,1)} %param.9) | copy-start | bytes 12292
  3.9 46.0 %all-to-all-start = ((bf16[16,224,256]{2,1,0:T(8,128)(2,1)}), bf16[16,224,256]{2,1,0:T(8,128)(2,1)S(1)}, u32[]{:S(2)}, u32[]{:S(2)}) async-start(bf16[16,224,256]{2,1,0:T(8,128)(2,1)} %broadcast_in_dim.13), calls=%async_computation | async-start | bytes 3670016 | tf_op jit(solution)/shard_map/all_to_all | solution.py:20
  13.3 5.3 %copy-start.10 = (s32[1,8,32,16]{2,3,1,0:T(8,128)S(1)}, s32[1,8,32,16]{2,3,1,0:T(8,128)}, u32[]{:S(2)}) copy-start(s32[1,8,32,16]{2,3,1,0:T(8,128)} %param.15) | copy-start | bytes 49156
  14.5 27.5 %copy-start.12 = (s32[128]{0:T(128)S(1)}, s32[128]{0:T(128)}, u32[]{:S(2)}) copy-start(s32[128]{0:T(128)} %param.13) | copy-start | bytes 1540
  25.3 16.8 %collective-permute-start.5 = (s32[2,4,512]{2,1,0:T(4,128)S(1)}, s32[2,4,512]{2,1,0:T(4,128)S(1)}, u32[]{:S(2)}, u32[]{:S(2)}) collective-permute-start(s32[2,4,512]{2,1,0:T(4,128)S(1)} %get-tuple-element.40), channel_id=1, source_target_pairs={{0,384},{128,256},{256,128},{384,0},{1,385},{129,257},{257,129},{3... | collective-permute-start | bytes 49160 | tf_op jit(solution)/shard_map/ppermute | solution.py:172
  31.5 16.1 %collective-permute-start.2 = (bf16[32,3584]{1,0:T(8,128)(2,1)}, bf16[32,3584]{1,0:T(8,128)(2,1)}, u32[]{:S(2)}, u32[]{:S(2)}) collective-permute-start(bf16[32,3584]{1,0:T(8,128)(2,1)} %pad_maximum_fusion.3), channel_id=1, source_target_pairs={{0,144},{16,128},{32,176},{48,160},{64,208},{80,192},{96,240},{112... | collective-permute-start | bytes 688136 | tf_op jit(solution)/shard_map/ppermute | solution.py:29
  33.5 14.2 %collective-permute-start.1 = (bf16[32,3584]{1,0:T(8,128)(2,1)}, bf16[32,3584]{1,0:T(8,128)(2,1)}, u32[]{:S(2)}, u32[]{:S(2)}) collective-permute-start(bf16[32,3584]{1,0:T(8,128)(2,1)} %pad_maximum_fusion.3), channel_id=1, source_target_pairs={{0,128},{16,144},{32,160},{48,176},{64,192},{80,208},{96,224},{112... | collective-permute-start | bytes 688136 | tf_op jit(solution)/shard_map/ppermute | solution.py:29
  37.9 9.7 %collective-permute-start = (bf16[32,3584]{1,0:T(8,128)(2,1)}, bf16[32,3584]{1,0:T(8,128)(2,1)}, u32[]{:S(2)}, u32[]{:S(2)}) collective-permute-start(bf16[32,3584]{1,0:T(8,128)(2,1)} %pad_maximum_fusion.3), channel_id=1, source_target_pairs={{0,16},{16,0},{32,48},{48,32},{64,80},{80,64},{96,112},{112,96},{1... | collective-permute-start | bytes 688136 | tf_op jit(solution)/shard_map/ppermute | solution.py:29
  39.9 5.5 %collective-permute-start.4 = (s32[2,4,512]{2,1,0:T(4,128)S(1)}, s32[2,4,512]{2,1,0:T(4,128)S(1)}, u32[]{:S(2)}, u32[]{:S(2)}) collective-permute-start(s32[2,4,512]{2,1,0:T(4,128)S(1)} %get-tuple-element.41), channel_id=1, source_target_pairs={{0,256},{128,384},{256,0},{384,128},{1,257},{129,385},{257,1},{385... | collective-permute-start | bytes 49160 | tf_op jit(solution)/shard_map/ppermute | solution.py:172
  42.1 4.9 %collective-permute-start.3 = (s32[2,4,512]{2,1,0:T(4,128)S(1)}, s32[2,4,512]{2,1,0:T(4,128)S(1)}, u32[]{:S(2)}, u32[]{:S(2)}) collective-permute-start(s32[2,4,512]{2,1,0:T(4,128)S(1)} %get-tuple-element.42), channel_id=1, source_target_pairs={{0,128},{128,0},{256,384},{384,256},{1,129},{129,1},{257,385},{385... | collective-permute-start | bytes 49160 | tf_op jit(solution)/shard_map/ppermute | solution.py:172
  47.0 3.0 %collective-permute-start.6 = (s32[8,4,512]{2,1,0:T(4,128)S(1)}, s32[8,4,512]{2,1,0:T(4,128)S(1)}, u32[]{:S(2)}, u32[]{:S(2)}) collective-permute-start(s32[8,4,512]{2,1,0:T(4,128)S(1)} %pad_add_fusion), channel_id=1, source_target_pairs={{0,0},{16,16},{32,128},{48,144},{64,256},{80,272},{96,384},{112,40... | collective-permute-start | bytes 196616 | tf_op jit(solution)/shard_map/ppermute | solution.py:174
  54.5 33.8 %all-to-all-start.1 = ((bf16[16,224,256]{2,1,0:T(8,128)(2,1)}), bf16[16,224,256]{2,1,0:T(8,128)(2,1)}, u32[]{:S(2)}, u32[]{:S(2)}) async-start(bf16[16,224,256]{2,1,0:T(8,128)(2,1)} %pad_maximum_fusion), calls=%async_computation.1 | async-start | bytes 3670016 | tf_op jit(solution)/shard_map/all_to_all | solution.py:20
  61.2 16.8 %collective-permute-start.9 = (bf16[32,2048]{1,0:T(8,128)(2,1)S(1)}, bf16[32,2048]{1,0:T(8,128)(2,1)S(1)}, u32[]{:S(2)}, u32[]{:S(2)}) collective-permute-start(bf16[32,2048]{1,0:T(8,128)(2,1)S(1)} %get-tuple-element.37), channel_id=1, source_target_pairs={{0,144},{16,128},{32,176},{48,160},{64,208},{80,192},{96,240},{112... | collective-permute-start | bytes 393224 | tf_op jit(solution)/shard_map/ppermute | solution.py:29
  73.6 6.4 %collective-permute-start.8 = (bf16[32,2048]{1,0:T(8,128)(2,1)S(1)}, bf16[32,2048]{1,0:T(8,128)(2,1)S(1)}, u32[]{:S(2)}, u32[]{:S(2)}) collective-permute-start(bf16[32,2048]{1,0:T(8,128)(2,1)S(1)} %get-tuple-element.38), channel_id=1, source_target_pairs={{0,128},{16,144},{32,160},{48,176},{64,192},{80,208},{96,224},{112... | collective-permute-start | bytes 393224 | tf_op jit(solution)/shard_map/ppermute | solution.py:29
  75.5 4.4 %collective-permute-start.7 = (bf16[32,2048]{1,0:T(8,128)(2,1)S(1)}, bf16[32,2048]{1,0:T(8,128)(2,1)S(1)}, u32[]{:S(2)}, u32[]{:S(2)}) collective-permute-start(bf16[32,2048]{1,0:T(8,128)(2,1)S(1)} %get-tuple-element.36), channel_id=1, source_target_pairs={{0,16},{16,0},{32,48},{48,32},{64,80},{80,64},{96,112},{112,96},{1... | collective-permute-start | bytes 393224 | tf_op jit(solution)/shard_map/ppermute | solution.py:29
  81.1 1.4 copy-start.9
  88.3 9.4 %copy-start.6 = (bf16[768,128]{1,0:T(8,128)(2,1)S(1)}, bf16[768,128]{1,0:T(8,128)(2,1)}, u32[]{:S(2)}) copy-start(bf16[768,128]{1,0:T(8,128)(2,1)} %copy-done.5) | copy-start | bytes 589828
  90.7 16.7 %all-to-all-start.2 = ((f32[16,16,128]{2,1,0:T(8,128)}), f32[16,16,128]{2,1,0:T(8,128)S(1)}, u32[]{:S(2)}, u32[]{:S(2)}) async-start(f32[16,16,128]{2,1,0:T(8,128)} %broadcast_in_dim.15), calls=%async_computation.2 | async-start | bytes 262144 | tf_op jit(solution)/shard_map/all_to_all | solution.py:20
  97.7 36.8 %collective-permute-start.10 = (bf16[768,128]{1,0:T(8,128)(2,1)S(1)}, bf16[768,128]{1,0:T(8,128)(2,1)S(1)}, u32[]{:S(2)}, u32[]{:S(2)}) collective-permute-start(bf16[768,128]{1,0:T(8,128)(2,1)S(1)} %copy-done.6), channel_id=1, source_target_pairs={{0,16},{16,0},{32,48},{48,32},{64,80},{80,64},{96,112},{112,96},{1... | collective-permute-start | bytes 589832 | tf_op jit(solution)/shard_map/ppermute | solution.py:29
  99.6 38.0 %collective-permute-start.11 = (bf16[768,128]{1,0:T(8,128)(2,1)S(1)}, bf16[768,128]{1,0:T(8,128)(2,1)S(1)}, u32[]{:S(2)}, u32[]{:S(2)}) collective-permute-start(bf16[768,128]{1,0:T(8,128)(2,1)S(1)} %get-tuple-element.26), channel_id=1, source_target_pairs={{0,128},{16,144},{32,160},{48,176},{64,192},{80,208},{96,224},{112... | collective-permute-start | bytes 589832 | tf_op jit(solution)/shard_map/ppermute | solution.py:29
  108.2 57.6 %all-to-all-start.3 = ((bf16[8,30,256]{2,1,0:T(8,128)(2,1)}), bf16[8,30,256]{2,1,0:T(8,128)(2,1)}, u32[]{:S(2)}, u32[]{:S(2)}) async-start(bf16[8,30,256]{2,1,0:T(8,128)(2,1)} %pad_maximum_fusion.4), calls=%async_computation.3 | async-start | bytes 262144 | tf_op jit(solution)/shard_map/all_to_all | solution.py:20
  123.3 26.6 %collective-permute-start.12 = (bf16[768,128]{1,0:T(8,128)(2,1)}, bf16[768,128]{1,0:T(8,128)(2,1)S(1)}, u32[]{:S(2)}, u32[]{:S(2)}) collective-permute-start(bf16[768,128]{1,0:T(8,128)(2,1)} %get-tuple-element.27), channel_id=1, source_target_pairs={{0,144},{16,128},{32,176},{48,160},{64,208},{80,192},{96,240},{112... | collective-permute-start | bytes 589832 | tf_op jit(solution)/shard_map/ppermute | solution.py:29
  125.6 24.3 %collective-permute-start.13 = (bf16[768,128]{1,0:T(8,128)(2,1)}, bf16[768,128]{1,0:T(8,128)(2,1)S(1)}, u32[]{:S(2)}, u32[]{:S(2)}) collective-permute-start(bf16[768,128]{1,0:T(8,128)(2,1)} %get-tuple-element.28), channel_id=1, source_target_pairs={{0,256},{16,272},{32,288},{48,304},{64,320},{80,336},{96,352},{112... | collective-permute-start | bytes 589832 | tf_op jit(solution)/shard_map/ppermute | solution.py:29
  130.2 28.5 %collective-permute-start.14 = (bf16[768,128]{1,0:T(8,128)(2,1)}, bf16[768,128]{1,0:T(8,128)(2,1)S(1)}, u32[]{:S(2)}, u32[]{:S(2)}) collective-permute-start(bf16[768,128]{1,0:T(8,128)(2,1)} %get-tuple-element.29), channel_id=1, source_target_pairs={{0,272},{16,256},{32,304},{48,288},{64,336},{80,320},{96,368},{112... | collective-permute-start | bytes 589832 | tf_op jit(solution)/shard_map/ppermute | solution.py:29
  134.4 24.3 %collective-permute-start.15 = (bf16[768,128]{1,0:T(8,128)(2,1)}, bf16[768,128]{1,0:T(8,128)(2,1)S(1)}, u32[]{:S(2)}, u32[]{:S(2)}) collective-permute-start(bf16[768,128]{1,0:T(8,128)(2,1)} %get-tuple-element.30), channel_id=1, source_target_pairs={{0,384},{16,400},{32,416},{48,432},{64,448},{80,464},{96,480},{112... | collective-permute-start | bytes 589832 | tf_op jit(solution)/shard_map/ppermute | solution.py:29
  137.5 21.9 %collective-permute-start.16 = (bf16[768,128]{1,0:T(8,128)(2,1)S(1)}, bf16[768,128]{1,0:T(8,128)(2,1)S(1)}, u32[]{:S(2)}, u32[]{:S(2)}) collective-permute-start(bf16[768,128]{1,0:T(8,128)(2,1)S(1)} %get-tuple-element.31), channel_id=1, source_target_pairs={{0,400},{16,384},{32,432},{48,416},{64,464},{80,448},{96,496},{112... | collective-permute-start | bytes 589832 | tf_op jit(solution)/shard_map/ppermute | solution.py:29
  167.5 46.9 %all-to-all-start.4 = ((bf16[8,30,256]{2,1,0:T(8,128)(2,1)}), bf16[8,30,256]{2,1,0:T(8,128)(2,1)S(1)}, u32[]{:S(2)}, u32[]{:S(2)}) async-start(bf16[8,30,256]{2,1,0:T(8,128)(2,1)} %broadcast_in_dim.16), calls=%async_computation.4 | async-start | bytes 262144 | tf_op jit(solution)/shard_map/all_to_all | solution.py:20
  183.1 18.2 %collective-permute-start.20 = (bf16[256,192]{0,1:T(8,128)(2,1)S(1)}, bf16[256,192]{0,1:T(8,128)(2,1)S(1)}, u32[]{:S(2)}, u32[]{:S(2)}) collective-permute-start(bf16[256,192]{0,1:T(8,128)(2,1)S(1)} %bitcast.105), channel_id=1, source_target_pairs={{0,384},{16,400},{32,0},{48,16},{64,128},{80,144},{96,256},{112,27... | collective-permute-start | bytes 294920 | tf_op jit(solution)/shard_map/ppermute | solution.py:217
  189.4 17.5 %collective-permute-start.19 = (bf16[256,192]{0,1:T(8,128)(2,1)S(1)}, bf16[256,192]{0,1:T(8,128)(2,1)S(1)}, u32[]{:S(2)}, u32[]{:S(2)}) collective-permute-start(bf16[256,192]{0,1:T(8,128)(2,1)S(1)} %bitcast.106), channel_id=1, source_target_pairs={{0,256},{16,272},{32,384},{48,400},{64,0},{80,16},{96,128},{112,14... | collective-permute-start | bytes 294920 | tf_op jit(solution)/shard_map/ppermute | solution.py:217
  198.7 15.0 %collective-permute-start.18 = (bf16[256,192]{0,1:T(8,128)(2,1)S(1)}, bf16[256,192]{0,1:T(8,128)(2,1)S(1)}, u32[]{:S(2)}, u32[]{:S(2)}) collective-permute-start(bf16[256,192]{0,1:T(8,128)(2,1)S(1)} %bitcast.107), channel_id=1, source_target_pairs={{0,128},{16,144},{32,256},{48,272},{64,384},{80,400},{96,0},{112,1... | collective-permute-start | bytes 294920 | tf_op jit(solution)/shard_map/ppermute | solution.py:217
  200.7 13.0 %collective-permute-start.17 = (bf16[256,192]{0,1:T(8,128)(2,1)S(1)}, bf16[256,192]{0,1:T(8,128)(2,1)S(1)}, u32[]{:S(2)}, u32[]{:S(2)}) collective-permute-start(bf16[256,192]{0,1:T(8,128)(2,1)S(1)} %bitcast.108), channel_id=1, source_target_pairs={{0,0},{16,16},{32,128},{48,144},{64,256},{80,272},{96,384},{112,40... | collective-permute-start | bytes 294920 | tf_op jit(solution)/shard_map/ppermute | solution.py:217
  (7 other events, 5.8 us)

commit v2 on v0

v2 whole, which is shorter than its diff:
```python
import functools
import math

import jax
import jax.numpy as jnp
from jax import lax
from jax.experimental import pallas as pl
from jax.experimental.pallas import tpu as pltpu
from jax.sharding import PartitionSpec as P

DEDUP = 1024
BF = jnp.bfloat16
F32 = jnp.float32
ZT = ("rep", "tab")
N_REP, N_TAB = 4, 8
TEAM = [[(2 * a + b) * 8 + 2 * h + c for b in range(2) for c in range(2)] for a in range(2) for h in range(4)]
QUAD = [[r * 8 + 2 * h + c for r in range(4) for c in range(2)] for h in range(4)]
FAR = [[r * 8 + 2 * h + c for h in range(4)] for r in range(4) for c in range(2)]


def target(quad, rep, core):
    middle = 0 if (rep == 1) == (core == 0) else 2
    return (quad + {0: 3, 3: 1}.get(rep, middle)) % 4


OWNERS = [[2 * target(h, r, c) + c for r in range(4) for c in range(2)] for h in range(4)]
DEVICES = [(h, r, c) for h in range(4) for r in range(4) for c in range(2)]


def flat_id(quad, rep, core):
    return rep * 8 + 2 * quad + core


def exchange(pieces, axis, groups=None):
    return lax.all_to_all(pieces, axis, 0, 0, axis_index_groups=groups)


def spread(block, count, axis, groups=None):
    return exchange(jnp.broadcast_to(block[None], (count,) + block.shape), axis, groups)


def high_low(values, axis):
    high = values.astype(BF)
    return jnp.concatenate([high, (values - high.astype(F32)).astype(BF)], axis=axis)


def swap(block, k):
    pairs = [(r * 8 + t, (r ^ (k >> 1)) * 8 + (t ^ (k & 1))) for r in range(N_REP) for t in range(N_TAB)]
    return lax.ppermute(block, ZT, pairs)


def pooled_kernel(grads_ref, compress_ref, comp_ref, order_ref, proj_ref, out_ref, ordered_ref):
    samples = compress_ref.shape[0]
    half = samples // 2
    rank = proj_ref.shape[0]
    down = (((0,), (0,)), ((), ()))
    whole = grads_ref[...].reshape(samples * rank, 128)
    ordered = jnp.dot(whole, order_ref[...], preferred_element_type=F32).astype(BF)
    ordered_ref[...] = ordered.reshape(samples, rank, 128)

    def step(i, _):
        both = []
        for sample in (i, i + half):
            left = jnp.concatenate([ordered_ref[sample], proj_ref[...]], axis=0)
            right = jnp.concatenate([compress_ref[sample], comp_ref[sample]], axis=0)
            grads = lax.dot_general(left, right, down, preferred_element_type=F32).astype(BF)
            rows = pl.ds(pl.multiple_of(sample * 16, 16), 16)
            for p in range(8):
                out_ref[p, rows, :] = grads[16 * p : 16 * p + 16, :128]
            both.append(grads[:, 128:])
        tail = jnp.concatenate(both, axis=1)
        rows = pl.ds(pl.multiple_of(samples * 16 + i * 16, 16), 16)
        for p in range(8):
            out_ref[p, rows, :] = tail[16 * p : 16 * p + 16, :]
        return _

    lax.fori_loop(0, half, step, jnp.int32(0), unroll=4)
    first = samples * 24
    out_ref[:, first:, :] = jnp.zeros((8, out_ref.shape[1] - first, 128), BF)


def pooled_grads(grad_zed, compress, grad_comp, order, proj, grad_rows):
    samples, rank, _ = grad_zed.shape
    chunk = chunk_rows(grad_rows, samples * 24)
    whole = pl.BlockSpec(memory_space=pltpu.VMEM)
    return pl.pallas_call(
        pooled_kernel,
        out_shape=jax.ShapeDtypeStruct((8, samples * 24 + 2 * chunk, 128), BF),
        in_specs=[whole] * 5,
        out_specs=whole,
        scratch_shapes=[pltpu.VMEM((samples, rank, 128), BF)],
        compiler_params=pltpu.CompilerParams(vmem_limit_bytes=12 * 1024 * 1024),
        cost_estimate=pl.CostEstimate(flops=2 * samples * 128 * 256 * 128, bytes_accessed=6 << 20, transcendentals=0),
        name="pooled_grads",
    )(grad_zed, compress, grad_comp, order, proj)


def chunk_rows(grad_rows, first):
    return next(c for c in range(16, first, 16) if 8 * c >= grad_rows and first % (2 * c) == 0)


def chunk_kernel(parts_ref, routed_ref, out_ref):
    del routed_ref
    grad_rows = parts_ref.shape[1]
    chunk = out_ref.shape[1] // 2
    for p in range(8):
        rows = min(chunk, grad_rows - p * chunk)
        if rows <= 0:
            out_ref[p] = jnp.zeros((2 * chunk, 128), BF)
            continue
        total = jnp.sum(parts_ref[:, p * chunk : p * chunk + rows, :].astype(F32), axis=0).astype(BF)
        out_ref[p, :rows, :] = total[:, :128]
        out_ref[p, chunk : chunk + rows, :] = total[:, 128:]


def with_chunks(routed, parts, first):
    chunk = chunk_rows(parts.shape[1], first)
    return pl.pallas_call(
        chunk_kernel,
        grid=(1,),
        out_shape=jax.ShapeDtypeStruct(routed.shape, BF),
        in_specs=[pl.BlockSpec(parts.shape, lambda i: (0, 0, 0)), pl.BlockSpec(memory_space=pl.ANY)],
        out_specs=pl.BlockSpec((8, 2 * chunk, 128), lambda i: (0, first // (2 * chunk), 0)),
        input_output_aliases={1: 0},
        compiler_params=pltpu.CompilerParams(vmem_limit_bytes=10 * 1024 * 1024),
        cost_estimate=pl.CostEstimate(flops=1 << 20, bytes_accessed=2 << 20, transcendentals=0),
        name="with_chunks",
    )(parts, routed)


def middle_kernel(shards, in_rows, weights_ref, *refs):
    pieces, (parts_ref, *partial_refs), joined = refs[:4], refs[4:9], refs[9]
    samples = pieces[0].shape[0]
    flat = shards * in_rows
    out_cols = weights_ref.shape[1] - in_rows
    step = 4 if shards % 4 == 0 else 1
    for k, piece in enumerate(pieces):
        joined[k * samples : (k + 1) * samples, :] = piece[...]

    def inner(g):
        return weights_ref[g : g + step, :in_rows, :].reshape(step * in_rows, -1)

    preact = jnp.zeros((4 * samples, weights_ref.shape[2]), F32)
    grad_act = jnp.zeros_like(preact)
    for g in range(0, shards, step):
        preact += jnp.dot(joined[:, g * in_rows : (g + step) * in_rows], inner(g), preferred_element_type=F32)
        grad_act += jnp.dot(
            joined[:, flat + g * out_cols : flat + (g + step) * out_cols],
            weights_ref[g : g + step, in_rows:, :].reshape(step * out_cols, -1),
            preferred_element_type=F32,
        )
    logistic = jax.nn.sigmoid(preact)
    activated = (preact * logistic).astype(BF)
    grad_pre = (grad_act * (logistic * (1.0 + preact * (1.0 - logistic)))).astype(BF)
    over_samples = (((0,), (0,)), ((), ()))
    for g in range(0, shards, step):
        rows = slice(g * in_rows, (g + step) * in_rows)
        partial = lax.dot_general(grad_pre, inner(g), (((1,), (1,)), ((), ())), preferred_element_type=F32).astype(BF)
        for k, ref in enumerate(partial_refs):
            ref[:, rows] = partial[k * samples : (k + 1) * samples]
        part = lax.dot_general(joined[:, rows], grad_pre, over_samples, preferred_element_type=F32).astype(BF)
        parts_ref[g : g + step, :in_rows, :] = part.reshape(step, in_rows, -1)
        part = lax.dot_general(
            joined[:, flat + g * out_cols : flat + (g + step) * out_cols],
            activated,
            over_samples,
            preferred_element_type=F32,
        ).astype(BF)
        parts_ref[g : g + step, in_rows:, :] = part.reshape(step, out_cols, -1)


def middle(weights, pieces, in_rows):
    shards = weights.shape[0]
    samples, wide = pieces[0].shape
    whole = pl.BlockSpec(memory_space=pltpu.VMEM)
    out = pl.pallas_call(
        functools.partial(middle_kernel, shards, in_rows),
        out_shape=[jax.ShapeDtypeStruct(weights.shape, BF)]
        + [jax.ShapeDtypeStruct((samples, shards * in_rows), BF)] * 4,
        in_specs=[whole] * 5,
        out_specs=[whole] * 5,
        scratch_shapes=[pltpu.VMEM((4 * samples, wide), BF)],
        compiler_params=pltpu.CompilerParams(vmem_limit_bytes=14 * 1024 * 1024),
        cost_estimate=pl.CostEstimate(flops=1 << 30, bytes_accessed=6 << 20, transcendentals=1 << 15),
        name="middle",
    )(weights, *pieces)
    return out[0], out[1:]


def count_slots(slots, out_ref):
    width = slots.shape[1]
    high, low = slots >> 7, slots & 127
    ids = lax.broadcasted_iota(jnp.int32, (128, width), 0)
    lows = [jnp.where(ids == low[b : b + 1], 1.0, 0.0).astype(BF) for b in range(4)]
    for block in range(DEDUP // 128):
        counts = jnp.zeros((128, width), BF)
        for b in range(4):
            counts += lows[b] * jnp.where(high[b : b + 1] == block, 1.0, 0.0).astype(BF)
        out_ref[block * 128 : (block + 1) * 128, :] = counts


def segment_kernel(slots_ref, values_ref, out_ref, total_ref, even_ref, odd_ref):
    sources, _, width = slots_ref.shape
    half = width // 2

    def add(source, counts_ref):
        tail = values_ref[source, width : width + half, :]
        left = lax.broadcasted_iota(jnp.int32, tail.shape, 1) < 64
        zero = jnp.zeros_like(tail)
        values = jnp.concatenate(
            [
                jnp.concatenate([values_ref[source, :half, :], jnp.where(left, tail, zero)], axis=1),
                jnp.concatenate([values_ref[source, half:width, :], jnp.where(left, zero, tail)], axis=1),
            ]
        )
        total_ref[...] += jnp.dot(counts_ref[...], values, preferred_element_type=F32)

    total_ref[...] = jnp.zeros_like(total_ref)
    count_slots(slots_ref[0], even_ref)

    def step(j, _):
        count_slots(slots_ref[2 * j + 1], odd_ref)
        add(2 * j, even_ref)
        count_slots(slots_ref[jnp.minimum(2 * j + 2, sources - 1)], even_ref)
        add(2 * j + 1, odd_ref)
        return _

    lax.fori_loop(0, sources // 2, step, jnp.int32(0))
    out_ref[:, :128] = total_ref[:, :128].astype(BF)
    out_ref[:, 128:] = (total_ref[:, 128:192] + total_ref[:, 192:]).astype(BF)


def segment_sums(slots, values):
    width = slots.shape[2]
    whole = pl.BlockSpec(memory_space=pltpu.VMEM)
    return pl.pallas_call(
        segment_kernel,
        in_specs=[whole] * 2,
        out_specs=whole,
        scratch_shapes=[pltpu.VMEM((DEDUP, 256), F32)] + [pltpu.VMEM((DEDUP, width), BF)] * 2,
        out_shape=jax.ShapeDtypeStruct((DEDUP, 192), BF),
        compiler_params=pltpu.CompilerParams(vmem_limit_bytes=12 * 1024 * 1024),
        cost_estimate=pl.CostEstimate(flops=2 << 30, bytes_accessed=10 << 20, transcendentals=0),
        name="segment_sums",
    )(slots, values)


def add_kernel(*refs):
    total = refs[0][...].astype(F32)
    for ref in refs[1:-1]:
        total = total + ref[...].astype(F32)
    refs[-1][...] = total.astype(refs[-1].dtype)


def add_pieces(pieces, dtype):
    return pl.pallas_call(
        add_kernel,
        out_shape=jax.ShapeDtypeStruct(pieces[0].shape, dtype),
        compiler_params=pltpu.CompilerParams(vmem_limit_bytes=4 * 1024 * 1024),
        cost_estimate=pl.CostEstimate(flops=1 << 18, bytes_accessed=1 << 20, transcendentals=0),
        name="add_pieces",
    )(*pieces)


def body(pooled, projection, w_inner, w_outer, upstream, feature_order, bag_slots, bag_lengths):
    samples, features, emb_width = pooled.shape
    rank = projection.shape[1]
    shards = lax.axis_size("fsdp")
    in_rows, units = w_inner.shape
    out_cols = w_outer.shape[1]
    flat, width = in_rows * shards, out_cols * shards
    grad_rows = in_rows + out_cols
    quarter = units // 4
    rep, tab = lax.axis_index("rep"), lax.axis_index("tab")
    far, core = tab // 2, tab % 2
    place = 2 * rep + core
    mine = place % 4

    weights = jnp.concatenate(
        [
            lax.dynamic_slice(w_inner, (0, mine * quarter), (in_rows, quarter)),
            lax.dynamic_slice(w_outer.T, (0, mine * quarter), (out_cols, quarter)),
        ]
    )
    weights = spread(weights, shards, "fsdp")

    compress = jnp.einsum("bfe,fk->bek", pooled, projection, preferred_element_type=F32).astype(BF)
    zed = jnp.einsum("bfe,bek->bfk", pooled, compress, preferred_element_type=F32).astype(BF)
    joined = jnp.concatenate([zed.reshape(samples, flat), upstream], axis=1)

    bag = bag_slots.shape[-1]
    live = jnp.where(jnp.arange(bag) < bag_lengths[..., None], bag_slots, -1)
    live = live.reshape(4, 2, samples * 16, bag).transpose(0, 1, 3, 2)
    near = []
    for k in range(4):
        piece = lax.dynamic_index_in_dim(live, rep ^ k, 0, False)
        near.append(lax.ppermute(piece, "rep", [(r, r ^ k) for r in range(4)]) if k else piece)
    pieces = [joined] + [swap(joined, k) for k in (1, 2, 3)]
    slots = lax.all_gather(live, ZT)
    pieces, near = lax.optimization_barrier((pieces, near))
    parts, partial_zed = middle(weights, pieces, in_rows)
    parts = exchange(parts, "fsdp")
    slots = lax.ppermute(
        jnp.concatenate(near), ZT, [(flat_id(target(h, r, c), h, c), flat_id(h, r, c)) for h, r, c in DEVICES]
    )
    grad_zed = add_pieces([partial_zed[0]] + [swap(partial_zed[k], k) for k in (1, 2, 3)], BF)
    grad_zed = grad_zed.reshape(samples, features, rank).transpose(0, 2, 1)
    grad_comp = jnp.einsum("bfe,bkf->bke", pooled, grad_zed, preferred_element_type=F32).astype(BF)
    owners = jnp.take(jnp.array(OWNERS, jnp.int32).reshape(-1), far * 8 + jnp.arange(8))
    order = jnp.take(feature_order.reshape(8, 16), owners, axis=0).reshape(-1)
    order = (jnp.arange(features)[:, None] == order[None, :]).astype(BF)
    proj = jnp.dot(projection.T, order, preferred_element_type=F32).astype(BF)
    routed = pooled_grads(grad_zed, compress.transpose(0, 2, 1), grad_comp, order, proj, grad_rows)
    part_proj = jnp.einsum("bfe,bke->kf", pooled, grad_comp, preferred_element_type=F32)
    slots, routed, part_proj = lax.optimization_barrier((slots, routed, part_proj))
    routed = exchange(with_chunks(routed, parts, samples * 24), ZT, QUAD)
    for bit in range(shards.bit_length() - 1):
        part_proj = part_proj + lax.ppermute(part_proj, "fsdp", [(s, s ^ (1 << bit)) for s in range(shards)])
    index = jnp.arange(8, dtype=jnp.int32)
    slots = jnp.take(slots, (far ^ (index // 2)) * 2 + index % 2, axis=0)
    part_proj, routed, slots = lax.optimization_barrier((part_proj, routed, slots))

    share = routed[:, samples * 24 :].reshape(2, -1, 128).astype(F32)
    chunks = jnp.concatenate([(share[0] + share[1]).astype(BF), high_low(part_proj, 0)])
    chunks = jnp.sum(spread(chunks, 4, ZT, FAR).astype(F32), axis=0)
    proj_rows = high_low(chunks[-32:-16] + chunks[-16:], 0)
    chunks = lax.all_gather(jnp.concatenate([chunks[:-32].astype(BF), proj_rows]), ZT, axis_index_groups=QUAD)

    sums = segment_sums(slots, routed).reshape(4, DEDUP // 4, emb_width)
    landed = []
    for k in range(4):
        pairs = [(flat_id(h, r, c), flat_id(target(h, r, c), (h + k) % 4, c)) for h, r, c in DEVICES]
        landed.append(lax.ppermute(lax.dynamic_index_in_dim(sums, (far + k) % 4, 0, False), ZT, pairs))
    chunks, landed = lax.optimization_barrier((chunks, landed))
    row_share = jnp.zeros((DEDUP // 4, emb_width), F32)
    for piece in landed:
        row_share = row_share + piece.astype(F32)

    proj_sum = jnp.sum(chunks[:, -32:].astype(F32), axis=0)
    proj_sum = (proj_sum[:16] + proj_sum[16:]).T
    grads = chunks[:, :-32].reshape(8, 8, -1, 128).transpose(0, 2, 1, 3).reshape(-1, units)[:grad_rows]

    all_samples = samples * lax.axis_size("rep") * lax.axis_size("tab") * lax.axis_size("fsdp")
    loss_scale = 1.0 / math.sqrt(all_samples)
    grad_inner = grads[:in_rows].astype(F32) * loss_scale
    grad_outer = (grads[in_rows:].astype(F32) * loss_scale).T
    grad_proj = proj_sum * loss_scale
    row_grads = row_share.reshape(1, 1, DEDUP // 4, emb_width)
    return (grad_inner, grad_outer, grad_proj, row_grads)


def solution(mesh):
    in_specs = (
        P(("rep", "tab", "fsdp"), None, None),
        P(),
        P("fsdp", None),
        P(None, "fsdp"),
        P(("rep", "tab", "fsdp"), None),
        P(),
        P("rep", None, "fsdp", "tab", None),
        P("rep", None, "fsdp", "tab"),
    )
    out_specs = (P("fsdp", None), P(None, "fsdp"), P(), P("tab", "fsdp", "rep", None))
    return jax.shard_map(body, mesh=mesh, in_specs=in_specs, out_specs=out_specs, check_vma=False)
```

time: 560 us -> 198 us (0.35)
  waiting for transfers between devices: 262 us -> 27.1 us
  other arithmetic: 107 us -> 9.9 us
  blocking collectives: 105 us -> 19.4 us
  starting transfers between devices: 26.8 us -> 99.9 us
  matrix products: 19 us -> 2.88 us
  between operations: 14.4 us -> 1.31 us
  Pallas kernels: 0 us -> 12.4 us
    all_gather x4 -> x0, waiting for transfers between devices: 237 us -> none  [the longest x1 62.1 us: body(): lax.all_gather(w_outer, 'fsdp', axis=1, tiled=True)]
    psum x1 -> x0, blocking collectives: 105 us -> none  [body(): proj_sum = lax.psum(part_proj, ('rep', 'tab', 'fsdp'))]
    scatter-add x4 -> x0, other arithmetic: 94.8 us -> none  [body(): running = running + jax.ops.segment_sum(values, row_ids, num_segments=DEDUP)]
    ppermute x0 -> x18, starting transfers between devices: none -> 68.1 us  [the longest x4 20.5 us: body(): lax.ppermute(lax.dynamic_index_in_dim(sums, (far + k) % 4, 0, False), ZT,...]
    all_gather x0 -> x1, blocking collectives: none -> 19.4 us  [body(): lax.all_gather(jnp.concatenate([chunks[:-32].astype(BF), proj_rows]), ZT,...]
    reduce_scatter x1 -> x0, waiting for transfers between devices: 18.6 us -> none  [body(): lax.psum_scatter(running.astype(jnp.bfloat16), 'rep', scatter_dimension=0...]
    dot_general x11 -> x5, matrix products: 19 us -> 2.88 us  [the longest x1 0.91 us: body(): jnp.einsum('bfe,fk->bek', pooled, projection, preferred_element_type=F32)]
    all_to_all x3 -> x4, waiting for transfers between devices: 3.73 us -> 18.1 us  [exchange(): return lax.all_to_all(pieces, axis, 0, 0, axis_index_groups=groups)]
  transfers between devices with their start and end apart: 9 -> 22, of which waited for: 6 -> 7; matrix products, arithmetic and copies ran while one was open for 26% -> 12% of each run, Pallas kernels for 0% -> 5%
where the time goes in v2:
time: 198 us; the launch traced here: 197 us
  starting transfers between devices  99.9 us (50%)
  waiting for transfers between devices  27.1 us (14%)
  local copies, waits for them, and re-layouts  23.8 us (12%)
  blocking collectives  19.4 us (10%)
  Pallas kernels  12.4 us (6%)
  other arithmetic  9.9 us (5%)
  matrix products  2.88 us (1%)
    all_to_all x4, starting transfers between devices, exchange(): return lax.all_to_all(pieces, axis, 0, 0, axis_index_groups=groups)  31.9 us
    ppermute x4, starting transfers between devices, body(): lax.ppermute(lax.dynamic_index_in_dim(sums, (far + k) % 4, 0, False), ZT,...  20.5 us
    ppermute x6, starting transfers between devices, swap(): return lax.ppermute(block, ZT, pairs)  19.9 us
    all_gather x1, blocking collectives, body(): lax.all_gather(jnp.concatenate([chunks[:-32].astype(BF), proj_rows]), ZT,...  19.4 us
    all_to_all x4, waiting for transfers between devices, exchange(): return lax.all_to_all(pieces, axis, 0, 0, axis_index_groups=groups)  18.1 us
    ppermute x4, starting transfers between devices, body(): lax.ppermute(part_proj, 'fsdp', [(s, s ^ 1 << bit) for s in range(shards)])  16.5 us
    ppermute x3, starting transfers between devices, body(): lax.ppermute(piece, 'rep', [(r, r ^ k) for r in range(4)])  9.26 us
    unnamed x34, local copies, waits for them, and re-layouts  7.15 us
  transfers between devices with their start and end apart: 22, of which 7 were waited for; matrix products, arithmetic and copies ran while one was open for 12% of the time, Pallas kernels for 5%

profile of v2, /device:TPU:1, one launch (start us, length us, event | category | flops | bytes accessed | tf_op | source)
XLA Modules:
  0.0 196.8 jit_solution(5598123653240987322)
XLA Ops:
  3.9 7.7 %all-to-all-start = ((bf16[16,224,256]{2,1,0:T(8,128)(2,1)}), bf16[16,224,256]{2,1,0:T(8,128)(2,1)S(1)}, u32[]{:S(2)}, u32[]{:S(2)}) async-start(bf16[16,224,256]{2,1,0:T(8,128)(2,1)} %broadcast_in_dim.42), calls=%async_computation | async-start | bytes 3670016 | tf_op jit(solution)/shard_map/all_to_all | solution.py:35
  16.3 1.6 pad_maximum_fusion.refs_0_
  17.9 4.9 %collective-permute-start = (bf16[32,3584]{1,0:T(8,128)(2,1)}, bf16[32,3584]{1,0:T(8,128)(2,1)}, u32[]{:S(2)}, u32[]{:S(2)}) collective-permute-start(bf16[32,3584]{1,0:T(8,128)(2,1)} %pad_maximum_fusion.refs_0_), channel_id=1, source_target_pairs={{0,16},{16,0},{32,48},{48,32},{64,80},{80,64},{96,112},{112,96},{1... | collective-permute-start | bytes 688136 | tf_op jit(solution)/shard_map/ppermute | solution.py:49
  22.8 1.9 collective-permute-start.1
  24.7 3.5 %collective-permute-start.2 = (bf16[32,3584]{1,0:T(8,128)(2,1)}, bf16[32,3584]{1,0:T(8,128)(2,1)}, u32[]{:S(2)}, u32[]{:S(2)}) collective-permute-start(bf16[32,3584]{1,0:T(8,128)(2,1)} %pad_maximum_fusion.refs_0_), channel_id=1, source_target_pairs={{0,144},{16,128},{32,176},{48,160},{64,208},{80,192},{96,240},{112... | collective-permute-start | bytes 688136 | tf_op jit(solution)/shard_map/ppermute | solution.py:49
  28.3 1.7 fusion.2
  30.0 2.0 copy.43
  34.0 1.9 collective-permute-start.3
  35.9 4.5 %collective-permute-start.4 = (s32[2,4,512]{2,1,0:T(4,128)S(1)}, s32[2,4,512]{2,1,0:T(4,128)S(1)}, u32[]{:S(2)}, u32[]{:S(2)}) collective-permute-start(s32[2,4,512]{2,1,0:T(4,128)S(1)} %get-tuple-element.61), channel_id=1, source_target_pairs={{0,256},{128,384},{256,0},{384,128},{1,257},{129,385},{257,1},{385... | collective-permute-start | bytes 49160 | tf_op jit(solution)/shard_map/ppermute | solution.py:297
  40.4 2.9 %collective-permute-start.5 = (s32[2,4,512]{2,1,0:T(4,128)S(1)}, s32[2,4,512]{2,1,0:T(4,128)S(1)}, u32[]{:S(2)}, u32[]{:S(2)}) collective-permute-start(s32[2,4,512]{2,1,0:T(4,128)S(1)} %get-tuple-element.60), channel_id=1, source_target_pairs={{0,384},{128,256},{256,128},{384,0},{1,385},{129,257},{257,129},{3... | collective-permute-start | bytes 49160 | tf_op jit(solution)/shard_map/ppermute | solution.py:297
  44.0 2.7 %collective-permute-done.5 = s32[2,4,512]{2,1,0:T(4,128)S(1)} collective-permute-done((s32[2,4,512]{2,1,0:T(4,128)S(1)}, s32[2,4,512]{2,1,0:T(4,128)S(1)}, u32[]{:S(2)}, u32[]{:S(2)}) %collective-permute-start.5) | collective-permute-done | bytes 16416 | tf_op jit(solution)/shard_map/ppermute | solution.py:297
  47.3 2.5 %middle.1 = (bf16[16,224,256]{2,1,0:T(8,128)(2,1)S(1)}, bf16[32,2048]{1,0:T(8,128)(2,1)S(1)}, bf16[32,2048]{1,0:T(8,128)(2,1)S(1)}, bf16[32,2048]{1,0:T(8,128)(2,1)S(1)}, bf16[32,2048]{1,0:T(8,128)(2,1)S(1)}) custom-call(bf16[16,224,256]{2,1,0:T(8,128)(2,1)S(1)} %all-to-all-done.weights_ref, bf16[32,3584]{1,0:T(8,128)(2,1)} %pad_maximum_fusion.refs_0_, ...), custom_call_target="tpu_custom_call" | custom-call | flops 1073741824 | bytes 6291456 | tf_op jit(solution)/shard_map/middle/pallas_call | solution.py:176
  53.0 7.1 %all-to-all-start.1 = ((bf16[16,224,256]{2,1,0:T(8,128)(2,1)}), bf16[16,224,256]{2,1,0:T(8,128)(2,1)S(1)}, u32[]{:S(2)}, u32[]{:S(2)}) async-start(bf16[16,224,256]{2,1,0:T(8,128)(2,1)} %copy-done.3), calls=%async_computation.1 | async-start | bytes 3670016 | tf_op jit(solution)/shard_map/all_to_all | solution.py:35
  63.3 4.1 %collective-permute-start.7 = (bf16[32,2048]{1,0:T(8,128)(2,1)}, bf16[32,2048]{1,0:T(8,128)(2,1)S(1)}, u32[]{:S(2)}, u32[]{:S(2)}) collective-permute-start(bf16[32,2048]{1,0:T(8,128)(2,1)} %copy-done.8), channel_id=1, source_target_pairs={{0,16},{16,0},{32,48},{48,32},{64,80},{80,64},{96,112},{112,96},{1... | collective-permute-start | bytes 393224 | tf_op jit(solution)/shard_map/ppermute | solution.py:49
  67.4 1.9 collective-permute-start.8
  69.3 3.5 %collective-permute-start.9 = (bf16[32,2048]{1,0:T(8,128)(2,1)S(1)}, bf16[32,2048]{1,0:T(8,128)(2,1)S(1)}, u32[]{:S(2)}, u32[]{:S(2)}) collective-permute-start(bf16[32,2048]{1,0:T(8,128)(2,1)S(1)} %get-tuple-element.39), channel_id=1, source_target_pairs={{0,144},{16,128},{32,176},{48,160},{64,208},{80,192},{96,240},{112... | collective-permute-start | bytes 393224 | tf_op jit(solution)/shard_map/ppermute | solution.py:49
  74.4 1.9 collective-permute-start.6
  79.8 1.5 copy.45
  82.7 2.9 %pooled_grads.1.routed_ref = bf16[8,832,128]{2,1,0:T(8,128)(2,1)} custom-call(bf16[32,16,128]{2,1,0:T(8,128)(2,1)S(1)} %bitcast.82, bf16[32,16,192]{2,1,0:T(8,128)(2,1)S(1)} %bitcast.81, bf16[32,16,192]{2,1,0:T(8,128)(2,1)S(1)} %convolution_convert_fusion.comp_ref, bf16[128,128]{1,0:T(8,128)(2,1)S(1)} %copy-done.4, bf16[16,128]{1,0:T(8,128)(2,1)S(1)} %fusion.1.proj_ref), custom_call_target="tpu_custom_call" | custom-call | flops 268435456 | bytes 6291456 | tf_op jit(solution)/shard_map/pooled_grads/pallas_call | solution.py:86
  87.7 10.7 %all-to-all-start.2 = ((bf16[8,832,128]{2,1,0:T(8,128)(2,1)}), bf16[8,832,128]{2,1,0:T(8,128)(2,1)S(1)}, u32[]{:S(2)}, u32[]{:S(2)}) async-start(bf16[8,832,128]{2,1,0:T(8,128)(2,1)} %with_chunks.1), calls=%async_computation.2 | async-start | bytes 3407872 | tf_op jit(solution)/shard_map/all_to_all | solution.py:35
  98.4 3.5 %collective-permute-start.10 = (f32[16,128]{1,0:T(8,128)S(1)}, f32[16,128]{1,0:T(8,128)S(1)}, u32[]{:S(2)}, u32[]{:S(2)}) collective-permute-start(f32[16,128]{1,0:T(8,128)S(1)} %convolution_bitcast_fusion), channel_id=1, source_target_pairs={{0,1},{1,0},{2,3},{3,2},{4,5},{5,4},{6,7},{7,6},{8,9},{9,8},{10,11... | collective-permute-start | bytes 24584 | tf_op jit(solution)/shard_map/ppermute | solution.py:318
  103.3 4.9 %collective-permute-start.11 = (f32[16,128]{1,0:T(8,128)S(1)}, f32[16,128]{1,0:T(8,128)S(1)}, u32[]{:S(2)}, u32[]{:S(2)}) collective-permute-start(f32[16,128]{1,0:T(8,128)S(1)} %add.227), channel_id=1, source_target_pairs={{0,2},{1,3},{2,0},{3,1},{4,6},{5,7},{6,4},{7,5},{8,10},{9,11},{10,... | collective-permute-start | bytes 24584 | tf_op jit(solution)/shard_map/ppermute | solution.py:318
  109.2 3.4 %collective-permute-start.12 = (f32[16,128]{1,0:T(8,128)S(1)}, f32[16,128]{1,0:T(8,128)S(1)}, u32[]{:S(2)}, u32[]{:S(2)}) collective-permute-start(f32[16,128]{1,0:T(8,128)S(1)} %add.228), channel_id=1, source_target_pairs={{0,4},{1,5},{2,6},{3,7},{4,0},{5,1},{6,2},{7,3},{8,12},{9,13},{10,... | collective-permute-start | bytes 24584 | tf_op jit(solution)/shard_map/ppermute | solution.py:318
  114.0 4.7 %collective-permute-start.13 = (f32[16,128]{1,0:T(8,128)S(1)}, f32[16,128]{1,0:T(8,128)S(1)}, u32[]{:S(2)}, u32[]{:S(2)}) collective-permute-start(f32[16,128]{1,0:T(8,128)S(1)} %add.229), channel_id=1, source_target_pairs={{0,8},{1,9},{2,10},{3,11},{4,12},{5,13},{6,14},{7,15},{8,0},{9,1},... | collective-permute-start | bytes 24584 | tf_op jit(solution)/shard_map/ppermute | solution.py:318
  120.1 18.1 %all-to-all-done.2.values_ref = bf16[8,832,128]{2,1,0:T(8,128)(2,1)S(1)} async-done(((bf16[8,832,128]{2,1,0:T(8,128)(2,1)}), bf16[8,832,128]{2,1,0:T(8,128)(2,1)S(1)}, u32[]{:S(2)}, u32[]{:S(2)}) %all-to-all-start.2) | async-done | bytes 1703968 | tf_op jit(solution)/shard_map/all_to_all | solution.py:35
  139.0 6.4 %all-to-all-start.3 = ((bf16[4,288,128]{2,1,0:T(8,128)(2,1)}), bf16[4,288,128]{2,1,0:T(8,128)(2,1)}, u32[]{:S(2)}, u32[]{:S(2)}) async-start(bf16[4,288,128]{2,1,0:T(8,128)(2,1)} %broadcast_in_dim.47), calls=%async_computation.3 | async-start | bytes 589824 | tf_op jit(solution)/shard_map/all_to_all | solution.py:35
  145.4 6.1 %segment_sums.1 = bf16[1024,192]{1,0:T(8,128)(2,1)S(1)} custom-call(s32[8,4,512]{2,1,0:T(4,128)S(1)} %broadcast_select_fusion.slots_ref, bf16[8,832,128]{2,1,0:T(8,128)(2,1)S(1)} %all-to-all-done.2.values_ref), custom_call_target="tpu_custom_call" | custom-call | flops 2147483648 | bytes 10485760 | tf_op jit(solution)/shard_map/segment_sums/pallas_call | solution.py:236
  151.7 7.3 %collective-permute-start.14 = (bf16[256,192]{0,1:T(8,128)(2,1)S(1)}, bf16[256,192]{0,1:T(8,128)(2,1)S(1)}, u32[]{:S(2)}, u32[]{:S(2)}) collective-permute-start(bf16[256,192]{0,1:T(8,128)(2,1)S(1)} %bitcast.95), channel_id=1, source_target_pairs={{0,96},{16,112},{128,0},{144,80},{256,64},{272,16},{384,32},{400,4... | collective-permute-start | bytes 294920 | tf_op jit(solution)/shard_map/ppermute | solution.py:333
  159.1 5.4 %collective-permute-start.15 = (bf16[256,192]{0,1:T(8,128)(2,1)S(1)}, bf16[256,192]{0,1:T(8,128)(2,1)S(1)}, u32[]{:S(2)}, u32[]{:S(2)}) collective-permute-start(bf16[256,192]{0,1:T(8,128)(2,1)S(1)} %bitcast.96), channel_id=1, source_target_pairs={{0,224},{16,240},{128,128},{144,208},{256,192},{272,144},{384,160}... | collective-permute-start | bytes 294920 | tf_op jit(solution)/shard_map/ppermute | solution.py:333
  164.6 2.2 %collective-permute-start.16 = (bf16[256,192]{0,1:T(8,128)(2,1)S(1)}, bf16[256,192]{0,1:T(8,128)(2,1)S(1)}, u32[]{:S(2)}, u32[]{:S(2)}) collective-permute-start(bf16[256,192]{0,1:T(8,128)(2,1)S(1)} %bitcast.97), channel_id=1, source_target_pairs={{0,352},{16,368},{128,256},{144,336},{256,320},{272,272},{384,288}... | collective-permute-start | bytes 294920 | tf_op jit(solution)/shard_map/ppermute | solution.py:333
  166.9 5.6 %collective-permute-start.17 = (bf16[256,192]{0,1:T(8,128)(2,1)S(1)}, bf16[256,192]{0,1:T(8,128)(2,1)S(1)}, u32[]{:S(2)}, u32[]{:S(2)}) collective-permute-start(bf16[256,192]{0,1:T(8,128)(2,1)S(1)} %bitcast.98), channel_id=1, source_target_pairs={{0,480},{16,496},{128,384},{144,464},{256,448},{272,400},{384,416}... | collective-permute-start | bytes 294920 | tf_op jit(solution)/shard_map/ppermute | solution.py:333
  173.6 19.4 %all-gather = bf16[2304,128]{1,0:T(8,128)(2,1)S(1)} all-gather(bf16[288,128]{1,0:T(8,128)(2,1)S(1)} %pad_maximum_fusion.3), channel_id=2, replica_groups={{0,16,128,144,256,272,384,400},{32,48,160,176,288,304,416,432},{64,80,1..., dimensions={0}, use_global_device_ids=true | all-gather | bytes 663552 | tf_op jit(solution)/shard_map/all_gather | solution.py:327
  (113 shorter events, 37.0 us)
Async XLA Ops:
  0.6 11.0 %copy-start = (bf16[32,128,192]{1,2,0:T(8,128)(2,1)S(1)}, bf16[32,128,192]{1,2,0:T(8,128)(2,1)}, u32[]{:S(2)}) copy-start(bf16[32,128,192]{1,2,0:T(8,128)(2,1)} %param.9) | copy-start | bytes 4718596
  3.9 7.7 %copy-start.13 = (bf16[128,16]{0,1:T(8,128)(2,1)S(1)}, bf16[128,16]{0,1:T(8,128)(2,1)}, u32[]{:S(2)}) copy-start(bf16[128,16]{0,1:T(8,128)(2,1)} %param.10) | copy-start | bytes 12292
  3.9 43.4 %all-to-all-start = ((bf16[16,224,256]{2,1,0:T(8,128)(2,1)}), bf16[16,224,256]{2,1,0:T(8,128)(2,1)S(1)}, u32[]{:S(2)}, u32[]{:S(2)}) async-start(bf16[16,224,256]{2,1,0:T(8,128)(2,1)} %broadcast_in_dim.42), calls=%async_computation | async-start | bytes 3670016 | tf_op jit(solution)/shard_map/all_to_all | solution.py:35
  15.0 28.3 %copy-start.9 = (s32[32]{0:T(128)S(1)}, s32[32]{0:T(128)}, u32[]{:S(2)}) copy-start(s32[32]{0:T(128)} %constant.170) | copy-start | bytes 388
  17.9 28.8 %collective-permute-start = (bf16[32,3584]{1,0:T(8,128)(2,1)}, bf16[32,3584]{1,0:T(8,128)(2,1)}, u32[]{:S(2)}, u32[]{:S(2)}) collective-permute-start(bf16[32,3584]{1,0:T(8,128)(2,1)} %pad_maximum_fusion.refs_0_), channel_id=1, source_target_pairs={{0,16},{16,0},{32,48},{48,32},{64,80},{80,64},{96,112},{112,96},{1... | collective-permute-start | bytes 688136 | tf_op jit(solution)/shard_map/ppermute | solution.py:49
  22.8 23.9 %collective-permute-start.1 = (bf16[32,3584]{1,0:T(8,128)(2,1)}, bf16[32,3584]{1,0:T(8,128)(2,1)}, u32[]{:S(2)}, u32[]{:S(2)}) collective-permute-start(bf16[32,3584]{1,0:T(8,128)(2,1)} %pad_maximum_fusion.refs_0_), channel_id=1, source_target_pairs={{0,128},{16,144},{32,160},{48,176},{64,192},{80,208},{96,224},{112... | collective-permute-start | bytes 688136 | tf_op jit(solution)/shard_map/ppermute | solution.py:49
  24.7 22.0 %collective-permute-start.2 = (bf16[32,3584]{1,0:T(8,128)(2,1)}, bf16[32,3584]{1,0:T(8,128)(2,1)}, u32[]{:S(2)}, u32[]{:S(2)}) collective-permute-start(bf16[32,3584]{1,0:T(8,128)(2,1)} %pad_maximum_fusion.refs_0_), channel_id=1, source_target_pairs={{0,144},{16,128},{32,176},{48,160},{64,208},{80,192},{96,240},{112... | collective-permute-start | bytes 688136 | tf_op jit(solution)/shard_map/ppermute | solution.py:49
  34.0 6.4 %collective-permute-start.3 = (s32[2,4,512]{2,1,0:T(4,128)S(1)}, s32[2,4,512]{2,1,0:T(4,128)S(1)}, u32[]{:S(2)}, u32[]{:S(2)}) collective-permute-start(s32[2,4,512]{2,1,0:T(4,128)S(1)} %get-tuple-element.62), channel_id=1, source_target_pairs={{0,128},{128,0},{256,384},{384,256},{1,129},{129,1},{257,385},{385... | collective-permute-start | bytes 49160 | tf_op jit(solution)/shard_map/ppermute | solution.py:297
  35.9 8.1 %collective-permute-start.4 = (s32[2,4,512]{2,1,0:T(4,128)S(1)}, s32[2,4,512]{2,1,0:T(4,128)S(1)}, u32[]{:S(2)}, u32[]{:S(2)}) collective-permute-start(s32[2,4,512]{2,1,0:T(4,128)S(1)} %get-tuple-element.61), channel_id=1, source_target_pairs={{0,256},{128,384},{256,0},{384,128},{1,257},{129,385},{257,1},{385... | collective-permute-start | bytes 49160 | tf_op jit(solution)/shard_map/ppermute | solution.py:297
  40.4 6.3 %copy-start.10 = (s32[2,4,512]{2,1,0:T(4,128)}, s32[2,4,512]{2,1,0:T(4,128)S(1)}, u32[]{:S(2)}) copy-start(s32[2,4,512]{2,1,0:T(4,128)S(1)} %collective-permute-done.3) | copy-start | bytes 49156
  40.4 6.3 %collective-permute-start.5 = (s32[2,4,512]{2,1,0:T(4,128)S(1)}, s32[2,4,512]{2,1,0:T(4,128)S(1)}, u32[]{:S(2)}, u32[]{:S(2)}) collective-permute-start(s32[2,4,512]{2,1,0:T(4,128)S(1)} %get-tuple-element.60), channel_id=1, source_target_pairs={{0,384},{128,256},{256,128},{384,0},{1,385},{129,257},{257,129},{3... | collective-permute-start | bytes 49160 | tf_op jit(solution)/shard_map/ppermute | solution.py:297
  44.0 16.1 %copy-start.15 = (s32[8]{0:T(128)}, s32[8]{0:T(128)S(1)}, u32[]{:S(2)}) copy-start(s32[8]{0:T(128)S(1)} %gather_fusion) | copy-start | bytes 100
  44.0 2.7 %copy-start.11 = (s32[2,4,512]{2,1,0:T(4,128)}, s32[2,4,512]{2,1,0:T(4,128)S(1)}, u32[]{:S(2)}) copy-start(s32[2,4,512]{2,1,0:T(4,128)S(1)} %collective-permute-done.4) | copy-start | bytes 49156
  49.8 1.3 copy-start.3
  53.0 7.6 %copy-start.14 = (s32[128]{0:T(128)S(1)}, s32[128]{0:T(128)}, u32[]{:S(2)}) copy-start(s32[128]{0:T(128)} %param.14) | copy-start | bytes 1540
  53.0 33.8 %all-to-all-start.1 = ((bf16[16,224,256]{2,1,0:T(8,128)(2,1)}), bf16[16,224,256]{2,1,0:T(8,128)(2,1)S(1)}, u32[]{:S(2)}, u32[]{:S(2)}) async-start(bf16[16,224,256]{2,1,0:T(8,128)(2,1)} %copy-done.3), calls=%async_computation.1 | async-start | bytes 3670016 | tf_op jit(solution)/shard_map/all_to_all | solution.py:35
  63.3 13.1 %collective-permute-start.7 = (bf16[32,2048]{1,0:T(8,128)(2,1)}, bf16[32,2048]{1,0:T(8,128)(2,1)S(1)}, u32[]{:S(2)}, u32[]{:S(2)}) collective-permute-start(bf16[32,2048]{1,0:T(8,128)(2,1)} %copy-done.8), channel_id=1, source_target_pairs={{0,16},{16,0},{32,48},{48,32},{64,80},{80,64},{96,112},{112,96},{1... | collective-permute-start | bytes 393224 | tf_op jit(solution)/shard_map/ppermute | solution.py:49
  67.4 9.0 %collective-permute-start.8 = (bf16[32,2048]{1,0:T(8,128)(2,1)}, bf16[32,2048]{1,0:T(8,128)(2,1)S(1)}, u32[]{:S(2)}, u32[]{:S(2)}) collective-permute-start(bf16[32,2048]{1,0:T(8,128)(2,1)} %copy-done.7), channel_id=1, source_target_pairs={{0,128},{16,144},{32,160},{48,176},{64,192},{80,208},{96,224},{112... | collective-permute-start | bytes 393224 | tf_op jit(solution)/shard_map/ppermute | solution.py:49
  69.3 8.5 %collective-permute-start.9 = (bf16[32,2048]{1,0:T(8,128)(2,1)S(1)}, bf16[32,2048]{1,0:T(8,128)(2,1)S(1)}, u32[]{:S(2)}, u32[]{:S(2)}) collective-permute-start(bf16[32,2048]{1,0:T(8,128)(2,1)S(1)} %get-tuple-element.39), channel_id=1, source_target_pairs={{0,144},{16,128},{32,176},{48,160},{64,208},{80,192},{96,240},{112... | collective-permute-start | bytes 393224 | tf_op jit(solution)/shard_map/ppermute | solution.py:49
  74.4 12.4 %collective-permute-start.6 = (s32[8,4,512]{2,1,0:T(4,128)}, s32[8,4,512]{2,1,0:T(4,128)}, u32[]{:S(2)}, u32[]{:S(2)}) collective-permute-start(s32[8,4,512]{2,1,0:T(4,128)} %pad_add_fusion), channel_id=1, source_target_pairs={{96,0},{112,16},{0,128},{80,144},{64,256},{16,272},{32,384},{48,40... | collective-permute-start | bytes 196616 | tf_op jit(solution)/shard_map/ppermute | solution.py:303
  81.4 1.3 copy-start.2
  81.4 1.3 copy-start.4
  87.7 50.5 %all-to-all-start.2 = ((bf16[8,832,128]{2,1,0:T(8,128)(2,1)}), bf16[8,832,128]{2,1,0:T(8,128)(2,1)S(1)}, u32[]{:S(2)}, u32[]{:S(2)}) async-start(bf16[8,832,128]{2,1,0:T(8,128)(2,1)} %with_chunks.1), calls=%async_computation.2 | async-start | bytes 3407872 | tf_op jit(solution)/shard_map/all_to_all | solution.py:35
  98.4 4.9 %collective-permute-start.10 = (f32[16,128]{1,0:T(8,128)S(1)}, f32[16,128]{1,0:T(8,128)S(1)}, u32[]{:S(2)}, u32[]{:S(2)}) collective-permute-start(f32[16,128]{1,0:T(8,128)S(1)} %convolution_bitcast_fusion), channel_id=1, source_target_pairs={{0,1},{1,0},{2,3},{3,2},{4,5},{5,4},{6,7},{7,6},{8,9},{9,8},{10,11... | collective-permute-start | bytes 24584 | tf_op jit(solution)/shard_map/ppermute | solution.py:318
  103.3 5.9 %collective-permute-start.11 = (f32[16,128]{1,0:T(8,128)S(1)}, f32[16,128]{1,0:T(8,128)S(1)}, u32[]{:S(2)}, u32[]{:S(2)}) collective-permute-start(f32[16,128]{1,0:T(8,128)S(1)} %add.227), channel_id=1, source_target_pairs={{0,2},{1,3},{2,0},{3,1},{4,6},{5,7},{6,4},{7,5},{8,10},{9,11},{10,... | collective-permute-start | bytes 24584 | tf_op jit(solution)/shard_map/ppermute | solution.py:318
  109.2 4.8 %collective-permute-start.12 = (f32[16,128]{1,0:T(8,128)S(1)}, f32[16,128]{1,0:T(8,128)S(1)}, u32[]{:S(2)}, u32[]{:S(2)}) collective-permute-start(f32[16,128]{1,0:T(8,128)S(1)} %add.228), channel_id=1, source_target_pairs={{0,4},{1,5},{2,6},{3,7},{4,0},{5,1},{6,2},{7,3},{8,12},{9,13},{10,... | collective-permute-start | bytes 24584 | tf_op jit(solution)/shard_map/ppermute | solution.py:318
  114.0 6.0 %collective-permute-start.13 = (f32[16,128]{1,0:T(8,128)S(1)}, f32[16,128]{1,0:T(8,128)S(1)}, u32[]{:S(2)}, u32[]{:S(2)}) collective-permute-start(f32[16,128]{1,0:T(8,128)S(1)} %add.229), channel_id=1, source_target_pairs={{0,8},{1,9},{2,10},{3,11},{4,12},{5,13},{6,14},{7,15},{8,0},{9,1},... | collective-permute-start | bytes 24584 | tf_op jit(solution)/shard_map/ppermute | solution.py:318
  139.0 33.5 %all-to-all-start.3 = ((bf16[4,288,128]{2,1,0:T(8,128)(2,1)}), bf16[4,288,128]{2,1,0:T(8,128)(2,1)}, u32[]{:S(2)}, u32[]{:S(2)}) async-start(bf16[4,288,128]{2,1,0:T(8,128)(2,1)} %broadcast_in_dim.47), calls=%async_computation.3 | async-start | bytes 589824 | tf_op jit(solution)/shard_map/all_to_all | solution.py:35
  151.7 41.3 %collective-permute-start.14 = (bf16[256,192]{0,1:T(8,128)(2,1)S(1)}, bf16[256,192]{0,1:T(8,128)(2,1)S(1)}, u32[]{:S(2)}, u32[]{:S(2)}) collective-permute-start(bf16[256,192]{0,1:T(8,128)(2,1)S(1)} %bitcast.95), channel_id=1, source_target_pairs={{0,96},{16,112},{128,0},{144,80},{256,64},{272,16},{384,32},{400,4... | collective-permute-start | bytes 294920 | tf_op jit(solution)/shard_map/ppermute | solution.py:333
  159.1 33.9 %collective-permute-start.15 = (bf16[256,192]{0,1:T(8,128)(2,1)S(1)}, bf16[256,192]{0,1:T(8,128)(2,1)S(1)}, u32[]{:S(2)}, u32[]{:S(2)}) collective-permute-start(bf16[256,192]{0,1:T(8,128)(2,1)S(1)} %bitcast.96), channel_id=1, source_target_pairs={{0,224},{16,240},{128,128},{144,208},{256,192},{272,144},{384,160}... | collective-permute-start | bytes 294920 | tf_op jit(solution)/shard_map/ppermute | solution.py:333
  164.6 28.4 %collective-permute-start.16 = (bf16[256,192]{0,1:T(8,128)(2,1)S(1)}, bf16[256,192]{0,1:T(8,128)(2,1)S(1)}, u32[]{:S(2)}, u32[]{:S(2)}) collective-permute-start(bf16[256,192]{0,1:T(8,128)(2,1)S(1)} %bitcast.97), channel_id=1, source_target_pairs={{0,352},{16,368},{128,256},{144,336},{256,320},{272,272},{384,288}... | collective-permute-start | bytes 294920 | tf_op jit(solution)/shard_map/ppermute | solution.py:333
  166.9 26.1 %collective-permute-start.17 = (bf16[256,192]{0,1:T(8,128)(2,1)S(1)}, bf16[256,192]{0,1:T(8,128)(2,1)S(1)}, u32[]{:S(2)}, u32[]{:S(2)}) collective-permute-start(bf16[256,192]{0,1:T(8,128)(2,1)S(1)} %bitcast.98), channel_id=1, source_target_pairs={{0,480},{16,496},{128,384},{144,464},{256,448},{272,400},{384,416}... | collective-permute-start | bytes 294920 | tf_op jit(solution)/shard_map/ppermute | solution.py:333
  (6 other events, 4.2 us)

commit v3 on v2

--- a/solution.py
+++ b/solution.py
@@ -23,7 +23,6 @@
     return (quad + {0: 3, 3: 1}.get(rep, middle)) % 4
 
 
-OWNERS = [[2 * target(h, r, c) + c for r in range(4) for c in range(2)] for h in range(4)]
 DEVICES = [(h, r, c) for h in range(4) for r in range(4) for c in range(2)]
 
 
@@ -129,7 +128,7 @@
 
 
 def middle_kernel(shards, in_rows, weights_ref, *refs):
-    pieces, (parts_ref, *partial_refs), joined = refs[:4], refs[4:9], refs[9]
+    pieces, (parts_ref, *partial_refs), joined = refs[:4], refs[4:7], refs[7]
     samples = pieces[0].shape[0]
     flat = shards * in_rows
     out_cols = weights_ref.shape[1] - in_rows
@@ -156,8 +155,8 @@
     for g in range(0, shards, step):
         rows = slice(g * in_rows, (g + step) * in_rows)
         partial = lax.dot_general(grad_pre, inner(g), (((1,), (1,)), ((), ())), preferred_element_type=F32).astype(BF)
-        for k, ref in enumerate(partial_refs):
-            ref[:, rows] = partial[k * samples : (k + 1) * samples]
+        for k in range(4):
+            partial_refs[k % 2][k // 2 * samples : (k // 2 + 1) * samples, rows] = partial[k * samples : (k + 1) * samples]
         part = lax.dot_general(joined[:, rows], grad_pre, over_samples, preferred_element_type=F32).astype(BF)
         parts_ref[g : g + step, :in_rows, :] = part.reshape(step, in_rows, -1)
         part = lax.dot_general(
@@ -176,9 +175,9 @@
     out = pl.pallas_call(
         functools.partial(middle_kernel, shards, in_rows),
         out_shape=[jax.ShapeDtypeStruct(weights.shape, BF)]
-        + [jax.ShapeDtypeStruct((samples, shards * in_rows), BF)] * 4,
+        + [jax.ShapeDtypeStruct((2 * samples, shards * in_rows), BF)] * 2,
         in_specs=[whole] * 5,
-        out_specs=[whole] * 5,
+        out_specs=[whole] * 3,
         scratch_shapes=[pltpu.VMEM((4 * samples, wide), BF)],
         compiler_params=pltpu.CompilerParams(vmem_limit_bytes=14 * 1024 * 1024),
         cost_estimate=pl.CostEstimate(flops=1 << 30, bytes_accessed=6 << 20, transcendentals=1 << 15),
@@ -245,21 +244,88 @@
     )(slots, values)
 
 
-def add_kernel(*refs):
-    total = refs[0][...].astype(F32)
-    for ref in refs[1:-1]:
-        total = total + ref[...].astype(F32)
-    refs[-1][...] = total.astype(refs[-1].dtype)
-
-
-def add_pieces(pieces, dtype):
+def add_kernel(mine_ref, other_ref, stay_ref, away_ref):
+    rows = stay_ref.shape[0]
+    total = mine_ref[...].astype(F32) + other_ref[...].astype(F32)
+    stay_ref[...] = total[:rows]
+    away_ref[...] = total[rows:].astype(BF)
+
+
+def add_halves(mine, other):
+    half = (mine.shape[0] // 2, mine.shape[1])
+    whole = pl.BlockSpec(memory_space=pltpu.VMEM)
     return pl.pallas_call(
         add_kernel,
-        out_shape=jax.ShapeDtypeStruct(pieces[0].shape, dtype),
+        out_shape=[jax.ShapeDtypeStruct(half, F32), jax.ShapeDtypeStruct(half, BF)],
+        in_specs=[whole] * 2,
+        out_specs=[whole] * 2,
         compiler_params=pltpu.CompilerParams(vmem_limit_bytes=4 * 1024 * 1024),
         cost_estimate=pl.CostEstimate(flops=1 << 18, bytes_accessed=1 << 20, transcendentals=0),
-        name="add_pieces",
-    )(*pieces)
+        name="add_halves",
+    )(mine, other)
+
+
+def row_ids_kernel(slots_ref, out_ref):
+    rows, samples = slots_ref.shape
+    groups, lanes = out_ref.shape
+    slots = slots_ref[...]
+    lane = lax.broadcasted_iota(jnp.int32, (samples, lanes), 1)
+    widen = (lane // 16 == lax.broadcasted_iota(jnp.int32, (samples, lanes), 0)).astype(F32).astype(BF)
+    row = lax.broadcasted_iota(jnp.int32, (rows, lanes), 0)
+    own = ((row // 4) % 16 == lax.broadcasted_iota(jnp.int32, (rows, lanes), 1) % 16).astype(F32)
+    row = lax.broadcasted_iota(jnp.int32, (groups, rows), 1)
+    group = lax.broadcasted_iota(jnp.int32, (groups, rows), 0)
+    gather = (row // 64 * 4 + row % 4 == group).astype(F32).astype(BF)
+
+    def moved(values):
+        values = jnp.dot(values.astype(F32).astype(BF), widen, preferred_element_type=F32) * own
+        return jnp.dot(gather, values.astype(BF), preferred_element_type=F32)
+
+    out_ref[...] = (moved(slots >> 5) * 32.0 + moved(slots & 31)).astype(jnp.int32)
+
+
+def row_ids(slots):
+    rows, samples = slots.shape
+    whole = pl.BlockSpec(memory_space=pltpu.VMEM)
+    return pl.pallas_call(
+        row_ids_kernel,
+        out_shape=jax.ShapeDtypeStruct((rows // 16, samples * 16), jnp.int32),
+        in_specs=[whole],
+        out_specs=whole,
+        compiler_params=pltpu.CompilerParams(vmem_limit_bytes=12 * 1024 * 1024),
+        cost_estimate=pl.CostEstimate(flops=1 << 25, bytes_accessed=1 << 20, transcendentals=0),
+        name="row_ids",
+    )(slots)
+
+
+def finish_kernel(loss_scale, chunks_ref, inner_ref, outer_ref, proj_ref):
+    in_rows, grad_rows = inner_ref.shape[0], inner_ref.shape[0] + outer_ref.shape[0]
+    chunk = (chunks_ref.shape[1] - 32) // 8
+    proj = jnp.zeros(proj_ref.shape, F32)
+    for p in range(8):
+        first, last = p * chunk, min((p + 1) * chunk, grad_rows)
+        for ref, low, high in ((inner_ref, 0, in_rows), (outer_ref, in_rows, grad_rows)):
+            a, b = max(first, low), min(last, high)
+            if a < b:
+                for m in range(8):
+                    rows = chunks_ref[p, m * chunk + a - first : m * chunk + b - first, :]
+                    ref[a - low : b - low, m * 128 : (m + 1) * 128] = rows.astype(F32) * loss_scale
+        proj = proj + (chunks_ref[p, 8 * chunk : 8 * chunk + 16, :].astype(F32) + chunks_ref[p, 8 * chunk + 16 :, :].astype(F32))
+    proj_ref[...] = proj * loss_scale
+
+
+def finish(chunks, in_rows, out_cols, units, loss_scale):
+    whole = pl.BlockSpec(memory_space=pltpu.VMEM)
+    shapes = [(in_rows, units), (out_cols, units), (16, 128)]
+    return pl.pallas_call(
+        functools.partial(finish_kernel, loss_scale),
+        out_shape=[jax.ShapeDtypeStruct(shape, F32) for shape in shapes],
+        in_specs=[whole],
+        out_specs=[whole] * 3,
+        compiler_params=pltpu.CompilerParams(vmem_limit_bytes=24 * 1024 * 1024),
+        cost_estimate=pl.CostEstimate(flops=1 << 20, bytes_accessed=2 << 20, transcendentals=0),
+        name="finish",
+    )(chunks)
 
 
 def body(pooled, projection, w_inner, w_outer, upstream, feature_order, bag_slots, bag_lengths):
@@ -273,8 +339,7 @@
     quarter = units // 4
     rep, tab = lax.axis_index("rep"), lax.axis_index("tab")
     far, core = tab // 2, tab % 2
-    place = 2 * rep + core
-    mine = place % 4
+    mine = (2 * rep + core) % 4
 
     weights = jnp.concatenate(
         [
@@ -290,26 +355,33 @@
 
     bag = bag_slots.shape[-1]
     live = jnp.where(jnp.arange(bag) < bag_lengths[..., None], bag_slots, -1)
-    live = live.reshape(4, 2, samples * 16, bag).transpose(0, 1, 3, 2)
+    live = row_ids(live.transpose(0, 1, 3, 4, 2).reshape(-1, samples)).reshape(4, 2, bag, -1)
     near = []
     for k in range(4):
         piece = lax.dynamic_index_in_dim(live, rep ^ k, 0, False)
         near.append(lax.ppermute(piece, "rep", [(r, r ^ k) for r in range(4)]) if k else piece)
     pieces = [joined] + [swap(joined, k) for k in (1, 2, 3)]
     slots = lax.all_gather(live, ZT)
-    pieces, near = lax.optimization_barrier((pieces, near))
+    base = (jnp.arange(features)[:, None] == feature_order[None, :]).astype(BF)
+    place = jnp.arange(features)[None, :] // 16
+    middle_of = jnp.where((place // 2 == 1) == (place % 2 == 0), 0, 2)
+    quad = (far + jnp.where(place < 2, 3, jnp.where(place >= 6, 1, middle_of))) % 4
+    slot = jnp.arange(features)[:, None]
+    moved = (slot == (2 * quad + place % 2) * 16 + jnp.arange(features)[None, :] % 16).astype(BF)
+    order = jnp.dot(base, moved, preferred_element_type=F32).astype(BF)
+    proj = jnp.dot(projection.T, order, preferred_element_type=F32).astype(BF)
+    pieces, near, order, proj = lax.optimization_barrier((pieces, near, order, proj))
     parts, partial_zed = middle(weights, pieces, in_rows)
     parts = exchange(parts, "fsdp")
     slots = lax.ppermute(
-        jnp.concatenate(near), ZT, [(flat_id(target(h, r, c), h, c), flat_id(h, r, c)) for h, r, c in DEVICES]
+        jnp.concatenate(near),
+        ZT, [(flat_id(target(h, r, c), h, c), flat_id(h, r, c)) for h, r, c in DEVICES],
     )
-    grad_zed = add_pieces([partial_zed[0]] + [swap(partial_zed[k], k) for k in (1, 2, 3)], BF)
+    stay, away = add_halves(partial_zed[0], swap(partial_zed[1], 1))
+    grad_zed = stay + swap(away, 2).astype(F32)
+    grad_zed = grad_zed.astype(BF)
     grad_zed = grad_zed.reshape(samples, features, rank).transpose(0, 2, 1)
     grad_comp = jnp.einsum("bfe,bkf->bke", pooled, grad_zed, preferred_element_type=F32).astype(BF)
-    owners = jnp.take(jnp.array(OWNERS, jnp.int32).reshape(-1), far * 8 + jnp.arange(8))
-    order = jnp.take(feature_order.reshape(8, 16), owners, axis=0).reshape(-1)
-    order = (jnp.arange(features)[:, None] == order[None, :]).astype(BF)
-    proj = jnp.dot(projection.T, order, preferred_element_type=F32).astype(BF)
     routed = pooled_grads(grad_zed, compress.transpose(0, 2, 1), grad_comp, order, proj, grad_rows)
     part_proj = jnp.einsum("bfe,bke->kf", pooled, grad_comp, preferred_element_type=F32)
     slots, routed, part_proj = lax.optimization_barrier((slots, routed, part_proj))
@@ -336,17 +408,11 @@
     for piece in landed:
         row_share = row_share + piece.astype(F32)
 
-    proj_sum = jnp.sum(chunks[:, -32:].astype(F32), axis=0)
-    proj_sum = (proj_sum[:16] + proj_sum[16:]).T
-    grads = chunks[:, :-32].reshape(8, 8, -1, 128).transpose(0, 2, 1, 3).reshape(-1, units)[:grad_rows]
-
     all_samples = samples * lax.axis_size("rep") * lax.axis_size("tab") * lax.axis_size("fsdp")
     loss_scale = 1.0 / math.sqrt(all_samples)
-    grad_inner = grads[:in_rows].astype(F32) * loss_scale
-    grad_outer = (grads[in_rows:].astype(F32) * loss_scale).T
-    grad_proj = proj_sum * loss_scale
+    grad_inner, grad_outer, grad_proj = finish(chunks, in_rows, out_cols, units, loss_scale)
     row_grads = row_share.reshape(1, 1, DEDUP // 4, emb_width)
-    return (grad_inner, grad_outer, grad_proj, row_grads)
+    return (grad_inner, grad_outer.T, grad_proj.T, row_grads)
 
 
 def solution(mesh):

time: 198 us -> 192 us (0.970)
  local copies, waits for them, and re-layouts: 23.8 us -> 15.8 us
  other arithmetic: 9.9 us -> 5.27 us
  starting transfers between devices: 99.9 us -> 104 us
    all_to_all x4, starting transfers between devices: 31.9 us -> 35.8 us  [exchange(): return lax.all_to_all(pieces, axis, 0, 0, axis_index_groups=groups)]
    ppermute x6 -> x5, starting transfers between devices: 19.9 us -> 16.4 us  [swap(): return lax.ppermute(block, ZT, pairs)]
    unnamed x34 -> x22, local copies, waits for them, and re-layouts: 7.15 us -> 4.35 us
    ppermute x1, starting transfers between devices: 1.91 us -> 4.53 us  [body(): lax.ppermute(jnp.concatenate(near), ZT, [(flat_id(target(h, r, c), h, c),...]
    select_n x2 -> x0, local copies, waits for them, and re-layouts: 2.05 us -> none  [the longest x1 1.97 us: body(): live = jnp.where(jnp.arange(bag) < bag_lengths[..., None], bag_slots, -1)]
  transfers between devices with their start and end apart: 22 -> 21, of which waited for: 7 -> 9; matrix products, arithmetic and copies ran while one was open for 12% -> 8% of each run, Pallas kernels for 5% -> 5%
where the time goes in v3:
time: 192 us; the launch traced here: 191 us
  starting transfers between devices  104 us (54%)
  waiting for transfers between devices  28.2 us (15%)
  blocking collectives  19.4 us (10%)
  local copies, waits for them, and re-layouts  15.8 us (8%)
  Pallas kernels  14.1 us (7%)
  other arithmetic  5.27 us (3%)
  matrix products  3.01 us (2%)
    all_to_all x4, starting transfers between devices, exchange(): return lax.all_to_all(pieces, axis, 0, 0, axis_index_groups=groups)  35.8 us
    ppermute x4, starting transfers between devices, body(): lax.ppermute(lax.dynamic_index_in_dim(sums, (far + k) % 4, 0, False), ZT,...  20.5 us
    all_gather x1, blocking collectives, body(): lax.all_gather(jnp.concatenate([chunks[:-32].astype(BF), proj_rows]), ZT,...  19.4 us
    all_to_all x4, waiting for transfers between devices, exchange(): return lax.all_to_all(pieces, axis, 0, 0, axis_index_groups=groups)  19.2 us
    ppermute x4, starting transfers between devices, body(): lax.ppermute(part_proj, 'fsdp', [(s, s ^ 1 << bit) for s in range(shards)])  16.4 us
    ppermute x5, starting transfers between devices, swap(): return lax.ppermute(block, ZT, pairs)  16.4 us
    ppermute x3, starting transfers between devices, body(): lax.ppermute(piece, 'rep', [(r, r ^ k) for r in range(4)])  10.3 us
    pallas_call x1, Pallas kernels, segment_sums(): pl.pallas_call(segment_kernel, in_specs=[whole] * 2, out_specs=whole, scr...  6.06 us
  transfers between devices with their start and end apart: 21, of which 9 were waited for; matrix products, arithmetic and copies ran while one was open for 8% of the time, Pallas kernels for 5%

profile of v3, /device:TPU:1, one launch (start us, length us, event | category | flops | bytes accessed | tf_op | source)
XLA Modules:
  0.0 191.0 jit_solution(4601355735577249267)
XLA Ops:
  2.5 1.4 broadcast_in_dim.44
  3.9 7.7 %all-to-all-start = ((bf16[16,224,256]{2,1,0:T(8,128)(2,1)}), bf16[16,224,256]{2,1,0:T(8,128)(2,1)S(1)}, u32[]{:S(2)}, u32[]{:S(2)}) async-start(bf16[16,224,256]{2,1,0:T(8,128)(2,1)} %broadcast_in_dim.44), calls=%async_computation | async-start | bytes 3670016 | tf_op jit(solution)/shard_map/all_to_all | solution.py:34
  16.3 1.6 pad_maximum_fusion.refs_0_
  17.9 4.9 %collective-permute-start = (bf16[32,3584]{1,0:T(8,128)(2,1)}, bf16[32,3584]{1,0:T(8,128)(2,1)}, u32[]{:S(2)}, u32[]{:S(2)}) collective-permute-start(bf16[32,3584]{1,0:T(8,128)(2,1)} %pad_maximum_fusion.refs_0_), channel_id=1, source_target_pairs={{0,16},{16,0},{32,48},{48,32},{64,80},{80,64},{96,112},{112,96},{1... | collective-permute-start | bytes 688136 | tf_op jit(solution)/shard_map/ppermute | solution.py:48
  22.8 1.9 %collective-permute-start.1 = (bf16[32,3584]{1,0:T(8,128)(2,1)}, bf16[32,3584]{1,0:T(8,128)(2,1)}, u32[]{:S(2)}, u32[]{:S(2)}) collective-permute-start(bf16[32,3584]{1,0:T(8,128)(2,1)} %pad_maximum_fusion.refs_0_), channel_id=1, source_target_pairs={{0,128},{16,144},{32,160},{48,176},{64,192},{80,208},{96,224},{112... | collective-permute-start | bytes 688136 | tf_op jit(solution)/shard_map/ppermute | solution.py:48
  24.7 3.5 %collective-permute-start.2 = (bf16[32,3584]{1,0:T(8,128)(2,1)}, bf16[32,3584]{1,0:T(8,128)(2,1)}, u32[]{:S(2)}, u32[]{:S(2)}) collective-permute-start(bf16[32,3584]{1,0:T(8,128)(2,1)} %pad_maximum_fusion.refs_0_), channel_id=1, source_target_pairs={{0,144},{16,128},{32,176},{48,160},{64,208},{80,192},{96,240},{112... | collective-permute-start | bytes 688136 | tf_op jit(solution)/shard_map/ppermute | solution.py:48
  30.7 1.9 collective-permute-start.3
  32.6 4.5 %collective-permute-start.4 = (s32[2,4,512]{2,1,0:T(4,128)}, s32[2,4,512]{2,1,0:T(4,128)S(1)}, u32[]{:S(2)}, u32[]{:S(2)}) collective-permute-start(s32[2,4,512]{2,1,0:T(4,128)} %get-tuple-element.71), channel_id=1, source_target_pairs={{0,256},{128,384},{256,0},{384,128},{1,257},{129,385},{257,1},{385... | collective-permute-start | bytes 49160 | tf_op jit(solution)/shard_map/ppermute | solution.py:362
  37.4 3.9 %collective-permute-start.5 = (s32[2,4,512]{2,1,0:T(4,128)}, s32[2,4,512]{2,1,0:T(4,128)S(1)}, u32[]{:S(2)}, u32[]{:S(2)}) collective-permute-start(s32[2,4,512]{2,1,0:T(4,128)} %get-tuple-element.70), channel_id=1, source_target_pairs={{0,384},{128,256},{256,128},{384,0},{1,385},{129,257},{257,129},{3... | collective-permute-start | bytes 49160 | tf_op jit(solution)/shard_map/ppermute | solution.py:362
  41.5 2.4 %collective-permute-done.5 = s32[2,4,512]{2,1,0:T(4,128)S(1)} collective-permute-done((s32[2,4,512]{2,1,0:T(4,128)}, s32[2,4,512]{2,1,0:T(4,128)S(1)}, u32[]{:S(2)}, u32[]{:S(2)}) %collective-permute-start.5) | collective-permute-done | bytes 16416 | tf_op jit(solution)/shard_map/ppermute | solution.py:362
  43.9 2.5 %middle.1 = (bf16[16,224,256]{2,1,0:T(8,128)(2,1)S(1)}, bf16[64,2048]{1,0:T(8,128)(2,1)S(1)}, bf16[64,2048]{1,0:T(8,128)(2,1)S(1)}) custom-call(bf16[16,224,256]{2,1,0:T(8,128)(2,1)S(1)} %all-to-all-done.weights_ref, bf16[32,3584]{1,0:T(8,128)(2,1)} %pad_maximum_fusion.refs_0_, bf16[32,3584]{1,0:T(8,128)(2,1)} %collective-permute-done.refs_1_, ...), custom_call_target="tpu_custom_call" | custom-call | flops 1073741824 | bytes 6291456 | tf_op jit(solution)/shard_map/middle/pallas_call | solution.py:175
  49.0 6.9 %all-to-all-start.1 = ((bf16[16,224,256]{2,1,0:T(8,128)(2,1)}), bf16[16,224,256]{2,1,0:T(8,128)(2,1)S(1)}, u32[]{:S(2)}, u32[]{:S(2)}) async-start(bf16[16,224,256]{2,1,0:T(8,128)(2,1)} %copy-done.3), calls=%async_computation.1 | async-start | bytes 3670016 | tf_op jit(solution)/shard_map/all_to_all | solution.py:34
  55.9 4.1 %collective-permute-start.7 = (bf16[64,2048]{1,0:T(8,128)(2,1)}, bf16[64,2048]{1,0:T(8,128)(2,1)S(1)}, u32[]{:S(2)}, u32[]{:S(2)}) collective-permute-start(bf16[64,2048]{1,0:T(8,128)(2,1)} %copy-done.8), channel_id=1, source_target_pairs={{0,16},{16,0},{32,48},{48,32},{64,80},{80,64},{96,112},{112,96},{1... | collective-permute-start | bytes 786440 | tf_op jit(solution)/shard_map/ppermute | solution.py:48
  62.4 1.9 %collective-permute-start.8 = (bf16[32,2048]{1,0:T(8,128)(2,1)S(1)}, bf16[32,2048]{1,0:T(8,128)(2,1)S(1)}, u32[]{:S(2)}, u32[]{:S(2)}) collective-permute-start(bf16[32,2048]{1,0:T(8,128)(2,1)S(1)} %get-tuple-element.44), channel_id=1, source_target_pairs={{0,128},{16,144},{32,160},{48,176},{64,192},{80,208},{96,224},{112... | collective-permute-start | bytes 393224 | tf_op jit(solution)/shard_map/ppermute | solution.py:48
  65.0 4.5 %collective-permute-start.6 = (s32[8,4,512]{2,1,0:T(4,128)}, s32[8,4,512]{2,1,0:T(4,128)}, u32[]{:S(2)}, u32[]{:S(2)}) collective-permute-start(s32[8,4,512]{2,1,0:T(4,128)} %pad_add_fusion), channel_id=1, source_target_pairs={{96,0},{112,16},{0,128},{80,144},{64,256},{16,272},{32,384},{48,40... | collective-permute-start | bytes 196616 | tf_op jit(solution)/shard_map/ppermute | solution.py:376
  70.6 1.5 copy.30
  73.5 2.9 %pooled_grads.1.routed_ref = bf16[8,832,128]{2,1,0:T(8,128)(2,1)} custom-call(bf16[32,16,128]{2,1,0:T(8,128)(2,1)S(1)} %bitcast.51, bf16[32,16,192]{2,1,0:T(8,128)(2,1)S(1)} %bitcast.49, bf16[32,16,192]{2,1,0:T(8,128)(2,1)S(1)} %convolution_convert_fusion.comp_ref, bf16[128,128]{1,0:T(8,128)(2,1)S(1)} %copy-done.7, bf16[16,128]{1,0:T(8,128)(2,1)S(1)} %fusion.1.proj_ref), custom_call_target="tpu_custom_call" | custom-call | flops 268435456 | bytes 6291456 | tf_op jit(solution)/shard_map/pooled_grads/pallas_call | solution.py:85
  76.4 1.6 collective-permute-done.6
  80.0 10.7 %all-to-all-start.2 = ((bf16[8,832,128]{2,1,0:T(8,128)(2,1)}), bf16[8,832,128]{2,1,0:T(8,128)(2,1)S(1)}, u32[]{:S(2)}, u32[]{:S(2)}) async-start(bf16[8,832,128]{2,1,0:T(8,128)(2,1)} %with_chunks.1), calls=%async_computation.2 | async-start | bytes 3407872 | tf_op jit(solution)/shard_map/all_to_all | solution.py:34
  90.6 3.5 %collective-permute-start.9 = (f32[16,128]{1,0:T(8,128)S(1)}, f32[16,128]{1,0:T(8,128)S(1)}, u32[]{:S(2)}, u32[]{:S(2)}) collective-permute-start(f32[16,128]{1,0:T(8,128)S(1)} %convolution_bitcast_fusion), channel_id=1, source_target_pairs={{0,1},{1,0},{2,3},{3,2},{4,5},{5,4},{6,7},{7,6},{8,9},{9,8},{10,11... | collective-permute-start | bytes 24584 | tf_op jit(solution)/shard_map/ppermute | solution.py:390
  95.5 4.9 %collective-permute-start.10 = (f32[16,128]{1,0:T(8,128)S(1)}, f32[16,128]{1,0:T(8,128)S(1)}, u32[]{:S(2)}, u32[]{:S(2)}) collective-permute-start(f32[16,128]{1,0:T(8,128)S(1)} %add.238), channel_id=1, source_target_pairs={{0,2},{1,3},{2,0},{3,1},{4,6},{5,7},{6,4},{7,5},{8,10},{9,11},{10,... | collective-permute-start | bytes 24584 | tf_op jit(solution)/shard_map/ppermute | solution.py:390
  101.4 3.3 %collective-permute-start.11 = (f32[16,128]{1,0:T(8,128)S(1)}, f32[16,128]{1,0:T(8,128)S(1)}, u32[]{:S(2)}, u32[]{:S(2)}) collective-permute-start(f32[16,128]{1,0:T(8,128)S(1)} %add.239), channel_id=1, source_target_pairs={{0,4},{1,5},{2,6},{3,7},{4,0},{5,1},{6,2},{7,3},{8,12},{9,13},{10,... | collective-permute-start | bytes 24584 | tf_op jit(solution)/shard_map/ppermute | solution.py:390
  104.8 1.4 gather_fusion
  106.2 4.7 %collective-permute-start.12 = (f32[16,128]{1,0:T(8,128)S(1)}, f32[16,128]{1,0:T(8,128)S(1)}, u32[]{:S(2)}, u32[]{:S(2)}) collective-permute-start(f32[16,128]{1,0:T(8,128)S(1)} %add.240), channel_id=1, source_target_pairs={{0,8},{1,9},{2,10},{3,11},{4,12},{5,13},{6,14},{7,15},{8,0},{9,1},... | collective-permute-start | bytes 24584 | tf_op jit(solution)/shard_map/ppermute | solution.py:390
  112.3 18.2 %all-to-all-done.2.values_ref = bf16[8,832,128]{2,1,0:T(8,128)(2,1)S(1)} async-done(((bf16[8,832,128]{2,1,0:T(8,128)(2,1)}), bf16[8,832,128]{2,1,0:T(8,128)(2,1)S(1)}, u32[]{:S(2)}, u32[]{:S(2)}) %all-to-all-start.2) | async-done | bytes 1703968 | tf_op jit(solution)/shard_map/all_to_all | solution.py:34
  131.2 10.6 %all-to-all-start.3 = ((bf16[4,288,128]{2,1,0:T(8,128)(2,1)}), bf16[4,288,128]{2,1,0:T(8,128)(2,1)}, u32[]{:S(2)}, u32[]{:S(2)}) async-start(bf16[4,288,128]{2,1,0:T(8,128)(2,1)} %broadcast_in_dim.47), calls=%async_computation.3 | async-start | bytes 589824 | tf_op jit(solution)/shard_map/all_to_all | solution.py:34
  141.8 6.1 %segment_sums.1 = bf16[1024,192]{1,0:T(8,128)(2,1)S(1)} custom-call(s32[8,4,512]{2,1,0:T(4,128)S(1)} %broadcast_select_fusion.slots_ref, bf16[8,832,128]{2,1,0:T(8,128)(2,1)S(1)} %all-to-all-done.2.values_ref), custom_call_target="tpu_custom_call" | custom-call | flops 2147483648 | bytes 10485760 | tf_op jit(solution)/shard_map/segment_sums/pallas_call | solution.py:235
  148.0 7.3 %collective-permute-start.13 = (bf16[256,192]{0,1:T(8,128)(2,1)S(1)}, bf16[256,192]{0,1:T(8,128)(2,1)S(1)}, u32[]{:S(2)}, u32[]{:S(2)}) collective-permute-start(bf16[256,192]{0,1:T(8,128)(2,1)S(1)} %bitcast.57), channel_id=1, source_target_pairs={{0,96},{16,112},{128,0},{144,80},{256,64},{272,16},{384,32},{400,4... | collective-permute-start | bytes 294920 | tf_op jit(solution)/shard_map/ppermute | solution.py:405
  155.4 5.4 %collective-permute-start.14 = (bf16[256,192]{0,1:T(8,128)(2,1)S(1)}, bf16[256,192]{0,1:T(8,128)(2,1)S(1)}, u32[]{:S(2)}, u32[]{:S(2)}) collective-permute-start(bf16[256,192]{0,1:T(8,128)(2,1)S(1)} %bitcast.58), channel_id=1, source_target_pairs={{0,224},{16,240},{128,128},{144,208},{256,192},{272,144},{384,160}... | collective-permute-start | bytes 294920 | tf_op jit(solution)/shard_map/ppermute | solution.py:405
  160.9 2.2 %collective-permute-start.15 = (bf16[256,192]{0,1:T(8,128)(2,1)S(1)}, bf16[256,192]{0,1:T(8,128)(2,1)S(1)}, u32[]{:S(2)}, u32[]{:S(2)}) collective-permute-start(bf16[256,192]{0,1:T(8,128)(2,1)S(1)} %bitcast.59), channel_id=1, source_target_pairs={{0,352},{16,368},{128,256},{144,336},{256,320},{272,272},{384,288}... | collective-permute-start | bytes 294920 | tf_op jit(solution)/shard_map/ppermute | solution.py:405
  163.2 5.6 %collective-permute-start.16 = (bf16[256,192]{0,1:T(8,128)(2,1)S(1)}, bf16[256,192]{0,1:T(8,128)(2,1)S(1)}, u32[]{:S(2)}, u32[]{:S(2)}) collective-permute-start(bf16[256,192]{0,1:T(8,128)(2,1)S(1)} %bitcast.60), channel_id=1, source_target_pairs={{0,480},{16,496},{128,384},{144,464},{256,448},{272,400},{384,416}... | collective-permute-start | bytes 294920 | tf_op jit(solution)/shard_map/ppermute | solution.py:405
  170.0 19.4 %all-gather = bf16[2304,128]{1,0:T(8,128)(2,1)S(1)} all-gather(bf16[288,128]{1,0:T(8,128)(2,1)S(1)} %pad_maximum_fusion.3), channel_id=2, replica_groups={{0,16,128,144,256,272,384,400},{32,48,160,176,288,304,416,432},{64,80,1..., dimensions={0}, use_global_device_ids=true | all-gather | bytes 663552 | tf_op jit(solution)/shard_map/all_gather | solution.py:399
  (85 shorter events, 26.8 us)
Async XLA Ops:
  0.6 11.0 %copy-start = (bf16[32,128,192]{1,2,0:T(8,128)(2,1)S(1)}, bf16[32,128,192]{1,2,0:T(8,128)(2,1)}, u32[]{:S(2)}) copy-start(bf16[32,128,192]{1,2,0:T(8,128)(2,1)} %param.8) | copy-start | bytes 4718596
  3.9 7.7 %copy-start.9 = (bf16[128,16]{0,1:T(8,128)(2,1)S(1)}, bf16[128,16]{0,1:T(8,128)(2,1)}, u32[]{:S(2)}) copy-start(bf16[128,16]{0,1:T(8,128)(2,1)} %param.9) | copy-start | bytes 12292
  3.9 40.0 %all-to-all-start = ((bf16[16,224,256]{2,1,0:T(8,128)(2,1)}), bf16[16,224,256]{2,1,0:T(8,128)(2,1)S(1)}, u32[]{:S(2)}, u32[]{:S(2)}) async-start(bf16[16,224,256]{2,1,0:T(8,128)(2,1)} %broadcast_in_dim.44), calls=%async_computation | async-start | bytes 3670016 | tf_op jit(solution)/shard_map/all_to_all | solution.py:34
  13.1 0.7 copy-start.1
  13.8 23.3 %copy-start.10 = (s32[128]{0:T(128)S(1)}, s32[128]{0:T(128)}, u32[]{:S(2)}) copy-start(s32[128]{0:T(128)} %param.13) | copy-start | bytes 1540
  17.9 26.0 %collective-permute-start = (bf16[32,3584]{1,0:T(8,128)(2,1)}, bf16[32,3584]{1,0:T(8,128)(2,1)}, u32[]{:S(2)}, u32[]{:S(2)}) collective-permute-start(bf16[32,3584]{1,0:T(8,128)(2,1)} %pad_maximum_fusion.refs_0_), channel_id=1, source_target_pairs={{0,16},{16,0},{32,48},{48,32},{64,80},{80,64},{96,112},{112,96},{1... | collective-permute-start | bytes 688136 | tf_op jit(solution)/shard_map/ppermute | solution.py:48
  22.8 21.1 %collective-permute-start.1 = (bf16[32,3584]{1,0:T(8,128)(2,1)}, bf16[32,3584]{1,0:T(8,128)(2,1)}, u32[]{:S(2)}, u32[]{:S(2)}) collective-permute-start(bf16[32,3584]{1,0:T(8,128)(2,1)} %pad_maximum_fusion.refs_0_), channel_id=1, source_target_pairs={{0,128},{16,144},{32,160},{48,176},{64,192},{80,208},{96,224},{112... | collective-permute-start | bytes 688136 | tf_op jit(solution)/shard_map/ppermute | solution.py:48
  24.7 19.2 %collective-permute-start.2 = (bf16[32,3584]{1,0:T(8,128)(2,1)}, bf16[32,3584]{1,0:T(8,128)(2,1)}, u32[]{:S(2)}, u32[]{:S(2)}) collective-permute-start(bf16[32,3584]{1,0:T(8,128)(2,1)} %pad_maximum_fusion.refs_0_), channel_id=1, source_target_pairs={{0,144},{16,128},{32,176},{48,160},{64,208},{80,192},{96,240},{112... | collective-permute-start | bytes 688136 | tf_op jit(solution)/shard_map/ppermute | solution.py:48
  30.7 6.7 %collective-permute-start.3 = (s32[2,4,512]{2,1,0:T(4,128)}, s32[2,4,512]{2,1,0:T(4,128)S(1)}, u32[]{:S(2)}, u32[]{:S(2)}) collective-permute-start(s32[2,4,512]{2,1,0:T(4,128)} %get-tuple-element.72), channel_id=1, source_target_pairs={{0,128},{128,0},{256,384},{384,256},{1,129},{129,1},{257,385},{385... | collective-permute-start | bytes 49160 | tf_op jit(solution)/shard_map/ppermute | solution.py:362
  32.6 8.8 %collective-permute-start.4 = (s32[2,4,512]{2,1,0:T(4,128)}, s32[2,4,512]{2,1,0:T(4,128)S(1)}, u32[]{:S(2)}, u32[]{:S(2)}) collective-permute-start(s32[2,4,512]{2,1,0:T(4,128)} %get-tuple-element.71), channel_id=1, source_target_pairs={{0,256},{128,384},{256,0},{384,128},{1,257},{129,385},{257,1},{385... | collective-permute-start | bytes 49160 | tf_op jit(solution)/shard_map/ppermute | solution.py:362
  37.3 6.6 %copy-start.6 = (bf16[128,128]{1,0:T(8,128)(2,1)}, bf16[128,128]{1,0:T(8,128)(2,1)S(1)}, u32[]{:S(2)}) copy-start(bf16[128,128]{1,0:T(8,128)(2,1)S(1)} %convolution_convert_fusion.3.order_ref) | copy-start | bytes 98308
  37.4 6.5 %collective-permute-start.5 = (s32[2,4,512]{2,1,0:T(4,128)}, s32[2,4,512]{2,1,0:T(4,128)S(1)}, u32[]{:S(2)}, u32[]{:S(2)}) collective-permute-start(s32[2,4,512]{2,1,0:T(4,128)} %get-tuple-element.70), channel_id=1, source_target_pairs={{0,384},{128,256},{256,128},{384,0},{1,385},{129,257},{257,129},{3... | collective-permute-start | bytes 49160 | tf_op jit(solution)/shard_map/ppermute | solution.py:362
  46.4 1.3 copy-start.3
  47.6 0.7 copy-start.4
  48.3 0.7 copy-start.8
  49.0 30.0 %all-to-all-start.1 = ((bf16[16,224,256]{2,1,0:T(8,128)(2,1)}), bf16[16,224,256]{2,1,0:T(8,128)(2,1)S(1)}, u32[]{:S(2)}, u32[]{:S(2)}) async-start(bf16[16,224,256]{2,1,0:T(8,128)(2,1)} %copy-done.3), calls=%async_computation.1 | async-start | bytes 3670016 | tf_op jit(solution)/shard_map/all_to_all | solution.py:34
  55.9 5.5 %collective-permute-start.7 = (bf16[64,2048]{1,0:T(8,128)(2,1)}, bf16[64,2048]{1,0:T(8,128)(2,1)S(1)}, u32[]{:S(2)}, u32[]{:S(2)}) collective-permute-start(bf16[64,2048]{1,0:T(8,128)(2,1)} %copy-done.8), channel_id=1, source_target_pairs={{0,16},{16,0},{32,48},{48,32},{64,80},{80,64},{96,112},{112,96},{1... | collective-permute-start | bytes 786440 | tf_op jit(solution)/shard_map/ppermute | solution.py:48
  61.4 0.9 copy-start.5
  62.4 7.1 %collective-permute-start.8 = (bf16[32,2048]{1,0:T(8,128)(2,1)S(1)}, bf16[32,2048]{1,0:T(8,128)(2,1)S(1)}, u32[]{:S(2)}, u32[]{:S(2)}) collective-permute-start(bf16[32,2048]{1,0:T(8,128)(2,1)S(1)} %get-tuple-element.44), channel_id=1, source_target_pairs={{0,128},{16,144},{32,160},{48,176},{64,192},{80,208},{96,224},{112... | collective-permute-start | bytes 393224 | tf_op jit(solution)/shard_map/ppermute | solution.py:48
  65.0 13.0 %collective-permute-start.6 = (s32[8,4,512]{2,1,0:T(4,128)}, s32[8,4,512]{2,1,0:T(4,128)}, u32[]{:S(2)}, u32[]{:S(2)}) collective-permute-start(s32[8,4,512]{2,1,0:T(4,128)} %pad_add_fusion), channel_id=1, source_target_pairs={{96,0},{112,16},{0,128},{80,144},{64,256},{16,272},{32,384},{48,40... | collective-permute-start | bytes 196616 | tf_op jit(solution)/shard_map/ppermute | solution.py:376
  72.1 1.3 copy-start.2
  72.1 1.3 copy-start.7
  80.0 50.5 %all-to-all-start.2 = ((bf16[8,832,128]{2,1,0:T(8,128)(2,1)}), bf16[8,832,128]{2,1,0:T(8,128)(2,1)S(1)}, u32[]{:S(2)}, u32[]{:S(2)}) async-start(bf16[8,832,128]{2,1,0:T(8,128)(2,1)} %with_chunks.1), calls=%async_computation.2 | async-start | bytes 3407872 | tf_op jit(solution)/shard_map/all_to_all | solution.py:34
  90.6 4.9 %collective-permute-start.9 = (f32[16,128]{1,0:T(8,128)S(1)}, f32[16,128]{1,0:T(8,128)S(1)}, u32[]{:S(2)}, u32[]{:S(2)}) collective-permute-start(f32[16,128]{1,0:T(8,128)S(1)} %convolution_bitcast_fusion), channel_id=1, source_target_pairs={{0,1},{1,0},{2,3},{3,2},{4,5},{5,4},{6,7},{7,6},{8,9},{9,8},{10,11... | collective-permute-start | bytes 24584 | tf_op jit(solution)/shard_map/ppermute | solution.py:390
  95.5 5.9 %collective-permute-start.10 = (f32[16,128]{1,0:T(8,128)S(1)}, f32[16,128]{1,0:T(8,128)S(1)}, u32[]{:S(2)}, u32[]{:S(2)}) collective-permute-start(f32[16,128]{1,0:T(8,128)S(1)} %add.238), channel_id=1, source_target_pairs={{0,2},{1,3},{2,0},{3,1},{4,6},{5,7},{6,4},{7,5},{8,10},{9,11},{10,... | collective-permute-start | bytes 24584 | tf_op jit(solution)/shard_map/ppermute | solution.py:390
  101.4 4.8 %collective-permute-start.11 = (f32[16,128]{1,0:T(8,128)S(1)}, f32[16,128]{1,0:T(8,128)S(1)}, u32[]{:S(2)}, u32[]{:S(2)}) collective-permute-start(f32[16,128]{1,0:T(8,128)S(1)} %add.239), channel_id=1, source_target_pairs={{0,4},{1,5},{2,6},{3,7},{4,0},{5,1},{6,2},{7,3},{8,12},{9,13},{10,... | collective-permute-start | bytes 24584 | tf_op jit(solution)/shard_map/ppermute | solution.py:390
  106.2 6.0 %collective-permute-start.12 = (f32[16,128]{1,0:T(8,128)S(1)}, f32[16,128]{1,0:T(8,128)S(1)}, u32[]{:S(2)}, u32[]{:S(2)}) collective-permute-start(f32[16,128]{1,0:T(8,128)S(1)} %add.240), channel_id=1, source_target_pairs={{0,8},{1,9},{2,10},{3,11},{4,12},{5,13},{6,14},{7,15},{8,0},{9,1},... | collective-permute-start | bytes 24584 | tf_op jit(solution)/shard_map/ppermute | solution.py:390
  131.2 37.6 %all-to-all-start.3 = ((bf16[4,288,128]{2,1,0:T(8,128)(2,1)}), bf16[4,288,128]{2,1,0:T(8,128)(2,1)}, u32[]{:S(2)}, u32[]{:S(2)}) async-start(bf16[4,288,128]{2,1,0:T(8,128)(2,1)} %broadcast_in_dim.47), calls=%async_computation.3 | async-start | bytes 589824 | tf_op jit(solution)/shard_map/all_to_all | solution.py:34
  148.0 41.3 %collective-permute-start.13 = (bf16[256,192]{0,1:T(8,128)(2,1)S(1)}, bf16[256,192]{0,1:T(8,128)(2,1)S(1)}, u32[]{:S(2)}, u32[]{:S(2)}) collective-permute-start(bf16[256,192]{0,1:T(8,128)(2,1)S(1)} %bitcast.57), channel_id=1, source_target_pairs={{0,96},{16,112},{128,0},{144,80},{256,64},{272,16},{384,32},{400,4... | collective-permute-start | bytes 294920 | tf_op jit(solution)/shard_map/ppermute | solution.py:405
  155.4 33.9 %collective-permute-start.14 = (bf16[256,192]{0,1:T(8,128)(2,1)S(1)}, bf16[256,192]{0,1:T(8,128)(2,1)S(1)}, u32[]{:S(2)}, u32[]{:S(2)}) collective-permute-start(bf16[256,192]{0,1:T(8,128)(2,1)S(1)} %bitcast.58), channel_id=1, source_target_pairs={{0,224},{16,240},{128,128},{144,208},{256,192},{272,144},{384,160}... | collective-permute-start | bytes 294920 | tf_op jit(solution)/shard_map/ppermute | solution.py:405
  160.9 28.4 %collective-permute-start.15 = (bf16[256,192]{0,1:T(8,128)(2,1)S(1)}, bf16[256,192]{0,1:T(8,128)(2,1)S(1)}, u32[]{:S(2)}, u32[]{:S(2)}) collective-permute-start(bf16[256,192]{0,1:T(8,128)(2,1)S(1)} %bitcast.59), channel_id=1, source_target_pairs={{0,352},{16,368},{128,256},{144,336},{256,320},{272,272},{384,288}... | collective-permute-start | bytes 294920 | tf_op jit(solution)/shard_map/ppermute | solution.py:405
  163.2 26.1 %collective-permute-start.16 = (bf16[256,192]{0,1:T(8,128)(2,1)S(1)}, bf16[256,192]{0,1:T(8,128)(2,1)S(1)}, u32[]{:S(2)}, u32[]{:S(2)}) collective-permute-start(bf16[256,192]{0,1:T(8,128)(2,1)S(1)} %bitcast.60), channel_id=1, source_target_pairs={{0,480},{16,496},{128,384},{144,464},{256,448},{272,400},{384,416}... | collective-permute-start | bytes 294920 | tf_op jit(solution)/shard_map/ppermute | solution.py:405

commit v4 on v3

--- a/solution.py
+++ b/solution.py
@@ -361,7 +361,6 @@
         piece = lax.dynamic_index_in_dim(live, rep ^ k, 0, False)
         near.append(lax.ppermute(piece, "rep", [(r, r ^ k) for r in range(4)]) if k else piece)
     pieces = [joined] + [swap(joined, k) for k in (1, 2, 3)]
-    slots = lax.all_gather(live, ZT)
     base = (jnp.arange(features)[:, None] == feature_order[None, :]).astype(BF)
     place = jnp.arange(features)[None, :] // 16
     middle_of = jnp.where((place // 2 == 1) == (place % 2 == 0), 0, 2)
@@ -370,7 +369,7 @@
     moved = (slot == (2 * quad + place % 2) * 16 + jnp.arange(features)[None, :] % 16).astype(BF)
     order = jnp.dot(base, moved, preferred_element_type=F32).astype(BF)
     proj = jnp.dot(projection.T, order, preferred_element_type=F32).astype(BF)
-    pieces, near, order, proj = lax.optimization_barrier((pieces, near, order, proj))
+    pieces, near[:3], order, proj = lax.optimization_barrier((pieces, near[:3], order, proj))
     parts, partial_zed = middle(weights, pieces, in_rows)
     parts = exchange(parts, "fsdp")
     slots = lax.ppermute(

time: 192 us -> 189 us (0.984)
  starting transfers between devices: 104 us -> 99.2 us
  waiting for transfers between devices: 28.2 us -> 30.3 us
    all_to_all x4, starting transfers between devices: 35.8 us -> 32.4 us  [exchange(): return lax.all_to_all(pieces, axis, 0, 0, axis_index_groups=groups)]
    ppermute x1, starting transfers between devices: 4.53 us -> 1.91 us  [body(): lax.ppermute(jnp.concatenate(near), ZT, [(flat_id(target(h, r, c), h, c),...]
    ppermute x1, waiting for transfers between devices: 1.61 us -> 3.63 us  [body(): lax.ppermute(jnp.concatenate(near), ZT, [(flat_id(target(h, r, c), h, c),...]
  transfers between devices with their start and end apart: 21 -> 21, of which waited for: 9 -> 8; matrix products, arithmetic and copies ran while one was open for 8% -> 8% of each run, Pallas kernels for 5% -> 5%
where the time goes in v4:
time: 189 us; the launch traced here: 188 us
  starting transfers between devices  99.2 us (52%)
  waiting for transfers between devices  30.3 us (16%)
  blocking collectives  19.4 us (10%)
  local copies, waits for them, and re-layouts  15.8 us (8%)
  Pallas kernels  14.1 us (7%)
  other arithmetic  5.26 us (3%)
  matrix products  3.01 us (2%)
    all_to_all x4, starting transfers between devices, exchange(): return lax.all_to_all(pieces, axis, 0, 0, axis_index_groups=groups)  32.4 us
    ppermute x4, starting transfers between devices, body(): lax.ppermute(lax.dynamic_index_in_dim(sums, (far + k) % 4, 0, False), ZT,...  20.5 us
    all_gather x1, blocking collectives, body(): lax.all_gather(jnp.concatenate([chunks[:-32].astype(BF), proj_rows]), ZT,...  19.4 us
    all_to_all x4, waiting for transfers between devices, exchange(): return lax.all_to_all(pieces, axis, 0, 0, axis_index_groups=groups)  18.1 us
    ppermute x5, starting transfers between devices, swap(): return lax.ppermute(block, ZT, pairs)  17.3 us
    ppermute x4, starting transfers between devices, body(): lax.ppermute(part_proj, 'fsdp', [(s, s ^ 1 << bit) for s in range(shards)])  16.4 us
    ppermute x3, starting transfers between devices, body(): lax.ppermute(piece, 'rep', [(r, r ^ k) for r in range(4)])  10.6 us
    pallas_call x1, Pallas kernels, segment_sums(): pl.pallas_call(segment_kernel, in_specs=[whole] * 2, out_specs=whole, scr...  6.06 us
  transfers between devices with their start and end apart: 21, of which 8 were waited for; matrix products, arithmetic and copies ran while one was open for 8% of the time, Pallas kernels for 5%

profile of v4, /device:TPU:1, one launch (start us, length us, event | category | flops | bytes accessed | tf_op | source)
XLA Modules:
  0.0 188.3 jit_solution(3022791438970668556)
XLA Ops:
  2.5 1.4 broadcast_in_dim.44
  3.9 7.7 %all-to-all-start = ((bf16[16,224,256]{2,1,0:T(8,128)(2,1)}), bf16[16,224,256]{2,1,0:T(8,128)(2,1)S(1)}, u32[]{:S(2)}, u32[]{:S(2)}) async-start(bf16[16,224,256]{2,1,0:T(8,128)(2,1)} %broadcast_in_dim.44), calls=%async_computation | async-start | bytes 3670016 | tf_op jit(solution)/shard_map/all_to_all | solution.py:34
  16.3 1.6 pad_maximum_fusion.refs_0_
  17.9 4.9 %collective-permute-start = (bf16[32,3584]{1,0:T(8,128)(2,1)}, bf16[32,3584]{1,0:T(8,128)(2,1)}, u32[]{:S(2)}, u32[]{:S(2)}) collective-permute-start(bf16[32,3584]{1,0:T(8,128)(2,1)} %pad_maximum_fusion.refs_0_), channel_id=1, source_target_pairs={{0,16},{16,0},{32,48},{48,32},{64,80},{80,64},{96,112},{112,96},{1... | collective-permute-start | bytes 688136 | tf_op jit(solution)/shard_map/ppermute | solution.py:48
  22.8 1.9 %collective-permute-start.1 = (bf16[32,3584]{1,0:T(8,128)(2,1)}, bf16[32,3584]{1,0:T(8,128)(2,1)}, u32[]{:S(2)}, u32[]{:S(2)}) collective-permute-start(bf16[32,3584]{1,0:T(8,128)(2,1)} %pad_maximum_fusion.refs_0_), channel_id=1, source_target_pairs={{0,128},{16,144},{32,160},{48,176},{64,192},{80,208},{96,224},{112... | collective-permute-start | bytes 688136 | tf_op jit(solution)/shard_map/ppermute | solution.py:48
  24.7 3.5 %collective-permute-start.2 = (bf16[32,3584]{1,0:T(8,128)(2,1)}, bf16[32,3584]{1,0:T(8,128)(2,1)}, u32[]{:S(2)}, u32[]{:S(2)}) collective-permute-start(bf16[32,3584]{1,0:T(8,128)(2,1)} %pad_maximum_fusion.refs_0_), channel_id=1, source_target_pairs={{0,144},{16,128},{32,176},{48,160},{64,208},{80,192},{96,240},{112... | collective-permute-start | bytes 688136 | tf_op jit(solution)/shard_map/ppermute | solution.py:48
  30.7 1.9 %collective-permute-start.3 = (s32[2,4,512]{2,1,0:T(4,128)}, s32[2,4,512]{2,1,0:T(4,128)S(1)}, u32[]{:S(2)}, u32[]{:S(2)}) collective-permute-start(s32[2,4,512]{2,1,0:T(4,128)} %get-tuple-element.70), channel_id=1, source_target_pairs={{0,128},{128,0},{256,384},{384,256},{1,129},{129,1},{257,385},{385... | collective-permute-start | bytes 49160 | tf_op jit(solution)/shard_map/ppermute | solution.py:362
  32.6 4.5 %collective-permute-start.4 = (s32[2,4,512]{2,1,0:T(4,128)}, s32[2,4,512]{2,1,0:T(4,128)S(1)}, u32[]{:S(2)}, u32[]{:S(2)}) collective-permute-start(s32[2,4,512]{2,1,0:T(4,128)} %get-tuple-element.68), channel_id=1, source_target_pairs={{0,256},{128,384},{256,0},{384,128},{1,257},{129,385},{257,1},{385... | collective-permute-start | bytes 49160 | tf_op jit(solution)/shard_map/ppermute | solution.py:362
  38.7 2.5 %middle.1 = (bf16[16,224,256]{2,1,0:T(8,128)(2,1)S(1)}, bf16[64,2048]{1,0:T(8,128)(2,1)S(1)}, bf16[64,2048]{1,0:T(8,128)(2,1)S(1)}) custom-call(bf16[16,224,256]{2,1,0:T(8,128)(2,1)S(1)} %all-to-all-done.weights_ref, bf16[32,3584]{1,0:T(8,128)(2,1)} %pad_maximum_fusion.refs_0_, bf16[32,3584]{1,0:T(8,128)(2,1)} %collective-permute-done.refs_1_, ...), custom_call_target="tpu_custom_call" | custom-call | flops 1073741824 | bytes 6291456 | tf_op jit(solution)/shard_map/middle/pallas_call | solution.py:175
  43.9 6.6 %all-to-all-start.1 = ((bf16[16,224,256]{2,1,0:T(8,128)(2,1)}), bf16[16,224,256]{2,1,0:T(8,128)(2,1)S(1)}, u32[]{:S(2)}, u32[]{:S(2)}) async-start(bf16[16,224,256]{2,1,0:T(8,128)(2,1)} %copy-done.3), calls=%async_computation.1 | async-start | bytes 3670016 | tf_op jit(solution)/shard_map/all_to_all | solution.py:34
  50.5 3.6 %collective-permute-start.7 = (bf16[64,2048]{1,0:T(8,128)(2,1)}, bf16[64,2048]{1,0:T(8,128)(2,1)S(1)}, u32[]{:S(2)}, u32[]{:S(2)}) collective-permute-start(bf16[64,2048]{1,0:T(8,128)(2,1)} %copy-done.8), channel_id=1, source_target_pairs={{0,16},{16,0},{32,48},{48,32},{64,80},{80,64},{96,112},{112,96},{1... | collective-permute-start | bytes 786440 | tf_op jit(solution)/shard_map/ppermute | solution.py:48
  56.5 3.4 %collective-permute-start.8 = (bf16[32,2048]{1,0:T(8,128)(2,1)S(1)}, bf16[32,2048]{1,0:T(8,128)(2,1)S(1)}, u32[]{:S(2)}, u32[]{:S(2)}) collective-permute-start(bf16[32,2048]{1,0:T(8,128)(2,1)S(1)} %get-tuple-element.42), channel_id=1, source_target_pairs={{0,128},{16,144},{32,160},{48,176},{64,192},{80,208},{96,224},{112... | collective-permute-start | bytes 393224 | tf_op jit(solution)/shard_map/ppermute | solution.py:48
  59.8 4.3 %collective-permute-start.5 = (s32[2,4,512]{2,1,0:T(4,128)S(1)}, s32[2,4,512]{2,1,0:T(4,128)S(1)}, u32[]{:S(2)}, u32[]{:S(2)}) collective-permute-start(s32[2,4,512]{2,1,0:T(4,128)S(1)} %get-tuple-element.69), channel_id=1, source_target_pairs={{0,384},{128,256},{256,128},{384,0},{1,385},{129,257},{257,129},{3... | collective-permute-start | bytes 49160 | tf_op jit(solution)/shard_map/ppermute | solution.py:362
  64.1 2.3 %collective-permute-done.5 = s32[2,4,512]{2,1,0:T(4,128)S(1)} collective-permute-done((s32[2,4,512]{2,1,0:T(4,128)S(1)}, s32[2,4,512]{2,1,0:T(4,128)S(1)}, u32[]{:S(2)}, u32[]{:S(2)}) %collective-permute-start.5) | collective-permute-done | bytes 16416 | tf_op jit(solution)/shard_map/ppermute | solution.py:362
  67.0 1.9 %collective-permute-start.6 = (s32[8,4,512]{2,1,0:T(4,128)}, s32[8,4,512]{2,1,0:T(4,128)}, u32[]{:S(2)}, u32[]{:S(2)}) collective-permute-start(s32[8,4,512]{2,1,0:T(4,128)} %pad_add_fusion), channel_id=1, source_target_pairs={{96,0},{112,16},{0,128},{80,144},{64,256},{16,272},{32,384},{48,40... | collective-permute-start | bytes 196616 | tf_op jit(solution)/shard_map/ppermute | solution.py:375
  70.0 1.5 copy.30
  72.9 2.9 %pooled_grads.1.routed_ref = bf16[8,832,128]{2,1,0:T(8,128)(2,1)} custom-call(bf16[32,16,128]{2,1,0:T(8,128)(2,1)S(1)} %bitcast.51, bf16[32,16,192]{2,1,0:T(8,128)(2,1)S(1)} %bitcast.49, bf16[32,16,192]{2,1,0:T(8,128)(2,1)S(1)} %convolution_convert_fusion.comp_ref, bf16[128,128]{1,0:T(8,128)(2,1)S(1)} %copy-done.7, bf16[16,128]{1,0:T(8,128)(2,1)S(1)} %fusion.1.proj_ref), custom_call_target="tpu_custom_call" | custom-call | flops 268435456 | bytes 6291456 | tf_op jit(solution)/shard_map/pooled_grads/pallas_call | solution.py:85
  75.8 3.6 %collective-permute-done.6 = s32[8,4,512]{2,1,0:T(4,128)} collective-permute-done((s32[8,4,512]{2,1,0:T(4,128)}, s32[8,4,512]{2,1,0:T(4,128)}, u32[]{:S(2)}, u32[]{:S(2)}) %collective-permute-start.6) | collective-permute-done | bytes 65568 | tf_op jit(solution)/shard_map/ppermute | solution.py:375
  80.4 10.6 %all-to-all-start.2 = ((bf16[8,832,128]{2,1,0:T(8,128)(2,1)}), bf16[8,832,128]{2,1,0:T(8,128)(2,1)S(1)}, u32[]{:S(2)}, u32[]{:S(2)}) async-start(bf16[8,832,128]{2,1,0:T(8,128)(2,1)} %with_chunks.1), calls=%async_computation.2 | async-start | bytes 3407872 | tf_op jit(solution)/shard_map/all_to_all | solution.py:34
  91.0 3.5 %collective-permute-start.9 = (f32[16,128]{1,0:T(8,128)S(1)}, f32[16,128]{1,0:T(8,128)S(1)}, u32[]{:S(2)}, u32[]{:S(2)}) collective-permute-start(f32[16,128]{1,0:T(8,128)S(1)} %convolution_bitcast_fusion), channel_id=1, source_target_pairs={{0,1},{1,0},{2,3},{3,2},{4,5},{5,4},{6,7},{7,6},{8,9},{9,8},{10,11... | collective-permute-start | bytes 24584 | tf_op jit(solution)/shard_map/ppermute | solution.py:389
  95.9 4.9 %collective-permute-start.10 = (f32[16,128]{1,0:T(8,128)S(1)}, f32[16,128]{1,0:T(8,128)S(1)}, u32[]{:S(2)}, u32[]{:S(2)}) collective-permute-start(f32[16,128]{1,0:T(8,128)S(1)} %add.238), channel_id=1, source_target_pairs={{0,2},{1,3},{2,0},{3,1},{4,6},{5,7},{6,4},{7,5},{8,10},{9,11},{10,... | collective-permute-start | bytes 24584 | tf_op jit(solution)/shard_map/ppermute | solution.py:389
  101.8 3.4 %collective-permute-start.11 = (f32[16,128]{1,0:T(8,128)S(1)}, f32[16,128]{1,0:T(8,128)S(1)}, u32[]{:S(2)}, u32[]{:S(2)}) collective-permute-start(f32[16,128]{1,0:T(8,128)S(1)} %add.239), channel_id=1, source_target_pairs={{0,4},{1,5},{2,6},{3,7},{4,0},{5,1},{6,2},{7,3},{8,12},{9,13},{10,... | collective-permute-start | bytes 24584 | tf_op jit(solution)/shard_map/ppermute | solution.py:389
  105.2 1.4 gather_fusion
  106.6 4.7 %collective-permute-start.12 = (f32[16,128]{1,0:T(8,128)S(1)}, f32[16,128]{1,0:T(8,128)S(1)}, u32[]{:S(2)}, u32[]{:S(2)}) collective-permute-start(f32[16,128]{1,0:T(8,128)S(1)} %add.240), channel_id=1, source_target_pairs={{0,8},{1,9},{2,10},{3,11},{4,12},{5,13},{6,14},{7,15},{8,0},{9,1},... | collective-permute-start | bytes 24584 | tf_op jit(solution)/shard_map/ppermute | solution.py:389
  112.7 18.1 %all-to-all-done.2.values_ref = bf16[8,832,128]{2,1,0:T(8,128)(2,1)S(1)} async-done(((bf16[8,832,128]{2,1,0:T(8,128)(2,1)}), bf16[8,832,128]{2,1,0:T(8,128)(2,1)S(1)}, u32[]{:S(2)}, u32[]{:S(2)}) %all-to-all-start.2) | async-done | bytes 1703968 | tf_op jit(solution)/shard_map/all_to_all | solution.py:34
  131.6 7.4 %all-to-all-start.3 = ((bf16[4,288,128]{2,1,0:T(8,128)(2,1)}), bf16[4,288,128]{2,1,0:T(8,128)(2,1)}, u32[]{:S(2)}, u32[]{:S(2)}) async-start(bf16[4,288,128]{2,1,0:T(8,128)(2,1)} %broadcast_in_dim.47), calls=%async_computation.3 | async-start | bytes 589824 | tf_op jit(solution)/shard_map/all_to_all | solution.py:34
  139.0 6.1 %segment_sums.1 = bf16[1024,192]{1,0:T(8,128)(2,1)S(1)} custom-call(s32[8,4,512]{2,1,0:T(4,128)S(1)} %broadcast_select_fusion.slots_ref, bf16[8,832,128]{2,1,0:T(8,128)(2,1)S(1)} %all-to-all-done.2.values_ref), custom_call_target="tpu_custom_call" | custom-call | flops 2147483648 | bytes 10485760 | tf_op jit(solution)/shard_map/segment_sums/pallas_call | solution.py:235
  145.2 7.3 %collective-permute-start.13 = (bf16[256,192]{0,1:T(8,128)(2,1)S(1)}, bf16[256,192]{0,1:T(8,128)(2,1)S(1)}, u32[]{:S(2)}, u32[]{:S(2)}) collective-permute-start(bf16[256,192]{0,1:T(8,128)(2,1)S(1)} %bitcast.57), channel_id=1, source_target_pairs={{0,96},{16,112},{128,0},{144,80},{256,64},{272,16},{384,32},{400,4... | collective-permute-start | bytes 294920 | tf_op jit(solution)/shard_map/ppermute | solution.py:404
  152.6 5.4 %collective-permute-start.14 = (bf16[256,192]{0,1:T(8,128)(2,1)S(1)}, bf16[256,192]{0,1:T(8,128)(2,1)S(1)}, u32[]{:S(2)}, u32[]{:S(2)}) collective-permute-start(bf16[256,192]{0,1:T(8,128)(2,1)S(1)} %bitcast.58), channel_id=1, source_target_pairs={{0,224},{16,240},{128,128},{144,208},{256,192},{272,144},{384,160}... | collective-permute-start | bytes 294920 | tf_op jit(solution)/shard_map/ppermute | solution.py:404
  158.2 2.2 %collective-permute-start.15 = (bf16[256,192]{0,1:T(8,128)(2,1)S(1)}, bf16[256,192]{0,1:T(8,128)(2,1)S(1)}, u32[]{:S(2)}, u32[]{:S(2)}) collective-permute-start(bf16[256,192]{0,1:T(8,128)(2,1)S(1)} %bitcast.59), channel_id=1, source_target_pairs={{0,352},{16,368},{128,256},{144,336},{256,320},{272,272},{384,288}... | collective-permute-start | bytes 294920 | tf_op jit(solution)/shard_map/ppermute | solution.py:404
  160.5 5.6 %collective-permute-start.16 = (bf16[256,192]{0,1:T(8,128)(2,1)S(1)}, bf16[256,192]{0,1:T(8,128)(2,1)S(1)}, u32[]{:S(2)}, u32[]{:S(2)}) collective-permute-start(bf16[256,192]{0,1:T(8,128)(2,1)S(1)} %bitcast.60), channel_id=1, source_target_pairs={{0,480},{16,496},{128,384},{144,464},{256,448},{272,400},{384,416}... | collective-permute-start | bytes 294920 | tf_op jit(solution)/shard_map/ppermute | solution.py:404
  167.2 19.4 %all-gather = bf16[2304,128]{1,0:T(8,128)(2,1)S(1)} all-gather(bf16[288,128]{1,0:T(8,128)(2,1)S(1)} %pad_maximum_fusion.3), channel_id=2, replica_groups={{0,16,128,144,256,272,384,400},{32,48,160,176,288,304,416,432},{64,80,1..., dimensions={0}, use_global_device_ids=true | all-gather | bytes 663552 | tf_op jit(solution)/shard_map/all_gather | solution.py:398
  (85 shorter events, 27.0 us)
Async XLA Ops:
  0.6 11.0 %copy-start = (bf16[32,128,192]{1,2,0:T(8,128)(2,1)S(1)}, bf16[32,128,192]{1,2,0:T(8,128)(2,1)}, u32[]{:S(2)}) copy-start(bf16[32,128,192]{1,2,0:T(8,128)(2,1)} %param.8) | copy-start | bytes 4718596
  3.9 7.7 %copy-start.9 = (bf16[128,16]{0,1:T(8,128)(2,1)S(1)}, bf16[128,16]{0,1:T(8,128)(2,1)}, u32[]{:S(2)}) copy-start(bf16[128,16]{0,1:T(8,128)(2,1)} %param.9) | copy-start | bytes 12292
  3.9 34.8 %all-to-all-start = ((bf16[16,224,256]{2,1,0:T(8,128)(2,1)}), bf16[16,224,256]{2,1,0:T(8,128)(2,1)S(1)}, u32[]{:S(2)}, u32[]{:S(2)}) async-start(bf16[16,224,256]{2,1,0:T(8,128)(2,1)} %broadcast_in_dim.44), calls=%async_computation | async-start | bytes 3670016 | tf_op jit(solution)/shard_map/all_to_all | solution.py:34
  13.1 0.7 copy-start.1
  13.8 23.3 %copy-start.10 = (s32[128]{0:T(128)S(1)}, s32[128]{0:T(128)}, u32[]{:S(2)}) copy-start(s32[128]{0:T(128)} %param.13) | copy-start | bytes 1540
  17.9 20.8 %collective-permute-start = (bf16[32,3584]{1,0:T(8,128)(2,1)}, bf16[32,3584]{1,0:T(8,128)(2,1)}, u32[]{:S(2)}, u32[]{:S(2)}) collective-permute-start(bf16[32,3584]{1,0:T(8,128)(2,1)} %pad_maximum_fusion.refs_0_), channel_id=1, source_target_pairs={{0,16},{16,0},{32,48},{48,32},{64,80},{80,64},{96,112},{112,96},{1... | collective-permute-start | bytes 688136 | tf_op jit(solution)/shard_map/ppermute | solution.py:48
  22.8 15.9 %collective-permute-start.1 = (bf16[32,3584]{1,0:T(8,128)(2,1)}, bf16[32,3584]{1,0:T(8,128)(2,1)}, u32[]{:S(2)}, u32[]{:S(2)}) collective-permute-start(bf16[32,3584]{1,0:T(8,128)(2,1)} %pad_maximum_fusion.refs_0_), channel_id=1, source_target_pairs={{0,128},{16,144},{32,160},{48,176},{64,192},{80,208},{96,224},{112... | collective-permute-start | bytes 688136 | tf_op jit(solution)/shard_map/ppermute | solution.py:48
  24.7 14.0 %collective-permute-start.2 = (bf16[32,3584]{1,0:T(8,128)(2,1)}, bf16[32,3584]{1,0:T(8,128)(2,1)}, u32[]{:S(2)}, u32[]{:S(2)}) collective-permute-start(bf16[32,3584]{1,0:T(8,128)(2,1)} %pad_maximum_fusion.refs_0_), channel_id=1, source_target_pairs={{0,144},{16,128},{32,176},{48,160},{64,208},{80,192},{96,240},{112... | collective-permute-start | bytes 688136 | tf_op jit(solution)/shard_map/ppermute | solution.py:48
  30.7 6.7 %collective-permute-start.3 = (s32[2,4,512]{2,1,0:T(4,128)}, s32[2,4,512]{2,1,0:T(4,128)S(1)}, u32[]{:S(2)}, u32[]{:S(2)}) collective-permute-start(s32[2,4,512]{2,1,0:T(4,128)} %get-tuple-element.70), channel_id=1, source_target_pairs={{0,128},{128,0},{256,384},{384,256},{1,129},{129,1},{257,385},{385... | collective-permute-start | bytes 49160 | tf_op jit(solution)/shard_map/ppermute | solution.py:362
  32.6 6.1 %collective-permute-start.4 = (s32[2,4,512]{2,1,0:T(4,128)}, s32[2,4,512]{2,1,0:T(4,128)S(1)}, u32[]{:S(2)}, u32[]{:S(2)}) collective-permute-start(s32[2,4,512]{2,1,0:T(4,128)} %get-tuple-element.68), channel_id=1, source_target_pairs={{0,256},{128,384},{256,0},{384,128},{1,257},{129,385},{257,1},{385... | collective-permute-start | bytes 49160 | tf_op jit(solution)/shard_map/ppermute | solution.py:362
  37.3 1.4 copy-start.6
  41.2 1.3 copy-start.3
  42.5 0.7 copy-start.4
  43.2 0.7 copy-start.8
  43.9 35.6 %all-to-all-start.1 = ((bf16[16,224,256]{2,1,0:T(8,128)(2,1)}), bf16[16,224,256]{2,1,0:T(8,128)(2,1)S(1)}, u32[]{:S(2)}, u32[]{:S(2)}) async-start(bf16[16,224,256]{2,1,0:T(8,128)(2,1)} %copy-done.3), calls=%async_computation.1 | async-start | bytes 3670016 | tf_op jit(solution)/shard_map/all_to_all | solution.py:34
  50.5 4.9 %collective-permute-start.7 = (bf16[64,2048]{1,0:T(8,128)(2,1)}, bf16[64,2048]{1,0:T(8,128)(2,1)S(1)}, u32[]{:S(2)}, u32[]{:S(2)}) collective-permute-start(bf16[64,2048]{1,0:T(8,128)(2,1)} %copy-done.8), channel_id=1, source_target_pairs={{0,16},{16,0},{32,48},{48,32},{64,80},{80,64},{96,112},{112,96},{1... | collective-permute-start | bytes 786440 | tf_op jit(solution)/shard_map/ppermute | solution.py:48
  55.4 0.9 copy-start.5
  56.5 12.5 %collective-permute-start.8 = (bf16[32,2048]{1,0:T(8,128)(2,1)S(1)}, bf16[32,2048]{1,0:T(8,128)(2,1)S(1)}, u32[]{:S(2)}, u32[]{:S(2)}) collective-permute-start(bf16[32,2048]{1,0:T(8,128)(2,1)S(1)} %get-tuple-element.42), channel_id=1, source_target_pairs={{0,128},{16,144},{32,160},{48,176},{64,192},{80,208},{96,224},{112... | collective-permute-start | bytes 393224 | tf_op jit(solution)/shard_map/ppermute | solution.py:48
  59.8 6.6 %collective-permute-start.5 = (s32[2,4,512]{2,1,0:T(4,128)S(1)}, s32[2,4,512]{2,1,0:T(4,128)S(1)}, u32[]{:S(2)}, u32[]{:S(2)}) collective-permute-start(s32[2,4,512]{2,1,0:T(4,128)S(1)} %get-tuple-element.69), channel_id=1, source_target_pairs={{0,384},{128,256},{256,128},{384,0},{1,385},{129,257},{257,129},{3... | collective-permute-start | bytes 49160 | tf_op jit(solution)/shard_map/ppermute | solution.py:362
  67.0 12.4 %collective-permute-start.6 = (s32[8,4,512]{2,1,0:T(4,128)}, s32[8,4,512]{2,1,0:T(4,128)}, u32[]{:S(2)}, u32[]{:S(2)}) collective-permute-start(s32[8,4,512]{2,1,0:T(4,128)} %pad_add_fusion), channel_id=1, source_target_pairs={{96,0},{112,16},{0,128},{80,144},{64,256},{16,272},{32,384},{48,40... | collective-permute-start | bytes 196616 | tf_op jit(solution)/shard_map/ppermute | solution.py:375
  71.6 1.3 copy-start.2
  71.6 1.3 copy-start.7
  80.4 50.4 %all-to-all-start.2 = ((bf16[8,832,128]{2,1,0:T(8,128)(2,1)}), bf16[8,832,128]{2,1,0:T(8,128)(2,1)S(1)}, u32[]{:S(2)}, u32[]{:S(2)}) async-start(bf16[8,832,128]{2,1,0:T(8,128)(2,1)} %with_chunks.1), calls=%async_computation.2 | async-start | bytes 3407872 | tf_op jit(solution)/shard_map/all_to_all | solution.py:34
  91.0 4.9 %collective-permute-start.9 = (f32[16,128]{1,0:T(8,128)S(1)}, f32[16,128]{1,0:T(8,128)S(1)}, u32[]{:S(2)}, u32[]{:S(2)}) collective-permute-start(f32[16,128]{1,0:T(8,128)S(1)} %convolution_bitcast_fusion), channel_id=1, source_target_pairs={{0,1},{1,0},{2,3},{3,2},{4,5},{5,4},{6,7},{7,6},{8,9},{9,8},{10,11... | collective-permute-start | bytes 24584 | tf_op jit(solution)/shard_map/ppermute | solution.py:389
  95.9 5.9 %collective-permute-start.10 = (f32[16,128]{1,0:T(8,128)S(1)}, f32[16,128]{1,0:T(8,128)S(1)}, u32[]{:S(2)}, u32[]{:S(2)}) collective-permute-start(f32[16,128]{1,0:T(8,128)S(1)} %add.238), channel_id=1, source_target_pairs={{0,2},{1,3},{2,0},{3,1},{4,6},{5,7},{6,4},{7,5},{8,10},{9,11},{10,... | collective-permute-start | bytes 24584 | tf_op jit(solution)/shard_map/ppermute | solution.py:389
  101.8 4.8 %collective-permute-start.11 = (f32[16,128]{1,0:T(8,128)S(1)}, f32[16,128]{1,0:T(8,128)S(1)}, u32[]{:S(2)}, u32[]{:S(2)}) collective-permute-start(f32[16,128]{1,0:T(8,128)S(1)} %add.239), channel_id=1, source_target_pairs={{0,4},{1,5},{2,6},{3,7},{4,0},{5,1},{6,2},{7,3},{8,12},{9,13},{10,... | collective-permute-start | bytes 24584 | tf_op jit(solution)/shard_map/ppermute | solution.py:389
  106.6 6.0 %collective-permute-start.12 = (f32[16,128]{1,0:T(8,128)S(1)}, f32[16,128]{1,0:T(8,128)S(1)}, u32[]{:S(2)}, u32[]{:S(2)}) collective-permute-start(f32[16,128]{1,0:T(8,128)S(1)} %add.240), channel_id=1, source_target_pairs={{0,8},{1,9},{2,10},{3,11},{4,12},{5,13},{6,14},{7,15},{8,0},{9,1},... | collective-permute-start | bytes 24584 | tf_op jit(solution)/shard_map/ppermute | solution.py:389
  131.6 34.5 %all-to-all-start.3 = ((bf16[4,288,128]{2,1,0:T(8,128)(2,1)}), bf16[4,288,128]{2,1,0:T(8,128)(2,1)}, u32[]{:S(2)}, u32[]{:S(2)}) async-start(bf16[4,288,128]{2,1,0:T(8,128)(2,1)} %broadcast_in_dim.47), calls=%async_computation.3 | async-start | bytes 589824 | tf_op jit(solution)/shard_map/all_to_all | solution.py:34
  145.2 41.3 %collective-permute-start.13 = (bf16[256,192]{0,1:T(8,128)(2,1)S(1)}, bf16[256,192]{0,1:T(8,128)(2,1)S(1)}, u32[]{:S(2)}, u32[]{:S(2)}) collective-permute-start(bf16[256,192]{0,1:T(8,128)(2,1)S(1)} %bitcast.57), channel_id=1, source_target_pairs={{0,96},{16,112},{128,0},{144,80},{256,64},{272,16},{384,32},{400,4... | collective-permute-start | bytes 294920 | tf_op jit(solution)/shard_map/ppermute | solution.py:404
  152.6 33.9 %collective-permute-start.14 = (bf16[256,192]{0,1:T(8,128)(2,1)S(1)}, bf16[256,192]{0,1:T(8,128)(2,1)S(1)}, u32[]{:S(2)}, u32[]{:S(2)}) collective-permute-start(bf16[256,192]{0,1:T(8,128)(2,1)S(1)} %bitcast.58), channel_id=1, source_target_pairs={{0,224},{16,240},{128,128},{144,208},{256,192},{272,144},{384,160}... | collective-permute-start | bytes 294920 | tf_op jit(solution)/shard_map/ppermute | solution.py:404
  158.2 28.4 %collective-permute-start.15 = (bf16[256,192]{0,1:T(8,128)(2,1)S(1)}, bf16[256,192]{0,1:T(8,128)(2,1)S(1)}, u32[]{:S(2)}, u32[]{:S(2)}) collective-permute-start(bf16[256,192]{0,1:T(8,128)(2,1)S(1)} %bitcast.59), channel_id=1, source_target_pairs={{0,352},{16,368},{128,256},{144,336},{256,320},{272,272},{384,288}... | collective-permute-start | bytes 294920 | tf_op jit(solution)/shard_map/ppermute | solution.py:404
  160.5 26.1 %collective-permute-start.16 = (bf16[256,192]{0,1:T(8,128)(2,1)S(1)}, bf16[256,192]{0,1:T(8,128)(2,1)S(1)}, u32[]{:S(2)}, u32[]{:S(2)}) collective-permute-start(bf16[256,192]{0,1:T(8,128)(2,1)S(1)} %bitcast.60), channel_id=1, source_target_pairs={{0,480},{16,496},{128,384},{144,464},{256,448},{272,400},{384,416}... | collective-permute-start | bytes 294920 | tf_op jit(solution)/shard_map/ppermute | solution.py:404

commit v5 on v4

--- a/solution.py
+++ b/solution.py
@@ -73,9 +73,7 @@
             out_ref[p, rows, :] = tail[16 * p : 16 * p + 16, :]
         return _
 
-    lax.fori_loop(0, half, step, jnp.int32(0), unroll=4)
-    first = samples * 24
-    out_ref[:, first:, :] = jnp.zeros((8, out_ref.shape[1] - first, 128), BF)
+    lax.fori_loop(0, half, step, jnp.int32(0), unroll=8)
 
 
 def pooled_grads(grad_zed, compress, grad_comp, order, proj, grad_rows):

time: 189 us -> 189 us (level)
  no operation moved by 1% of the time
where the time goes in v5:
time: 189 us; the launch traced here: 188 us
  starting transfers between devices  99.2 us (52%)
  waiting for transfers between devices  30.8 us (16%)
  blocking collectives  19.4 us (10%)
  local copies, waits for them, and re-layouts  15.8 us (8%)
  Pallas kernels  13.6 us (7%)
  other arithmetic  5.26 us (3%)
  matrix products  3.01 us (2%)
    all_to_all x4, starting transfers between devices, exchange(): return lax.all_to_all(pieces, axis, 0, 0, axis_index_groups=groups)  32.4 us
    ppermute x4, starting transfers between devices, body(): lax.ppermute(lax.dynamic_index_in_dim(sums, (far + k) % 4, 0, False), ZT,...  20.5 us
    all_gather x1, blocking collectives, body(): lax.all_gather(jnp.concatenate([chunks[:-32].astype(BF), proj_rows]), ZT,...  19.4 us
    all_to_all x4, waiting for transfers between devices, exchange(): return lax.all_to_all(pieces, axis, 0, 0, axis_index_groups=groups)  18.2 us
    ppermute x5, starting transfers between devices, swap(): return lax.ppermute(block, ZT, pairs)  17.3 us
    ppermute x4, starting transfers between devices, body(): lax.ppermute(part_proj, 'fsdp', [(s, s ^ 1 << bit) for s in range(shards)])  16.4 us
    ppermute x3, starting transfers between devices, body(): lax.ppermute(piece, 'rep', [(r, r ^ k) for r in range(4)])  10.6 us
    pallas_call x1, Pallas kernels, segment_sums(): pl.pallas_call(segment_kernel, in_specs=[whole] * 2, out_specs=whole, scr...  6.06 us
  transfers between devices with their start and end apart: 21, of which 8 were waited for; matrix products, arithmetic and copies ran while one was open for 8% of the time, Pallas kernels for 5%

profile of v5, /device:TPU:1, one launch (start us, length us, event | category | flops | bytes accessed | tf_op | source)
XLA Modules:
  0.0 188.3 jit_solution(17410539062713197754)
XLA Ops:
  2.5 1.4 broadcast_in_dim.44
  3.9 7.7 %all-to-all-start = ((bf16[16,224,256]{2,1,0:T(8,128)(2,1)}), bf16[16,224,256]{2,1,0:T(8,128)(2,1)S(1)}, u32[]{:S(2)}, u32[]{:S(2)}) async-start(bf16[16,224,256]{2,1,0:T(8,128)(2,1)} %broadcast_in_dim.44), calls=%async_computation | async-start | bytes 3670016 | tf_op jit(solution)/shard_map/all_to_all | solution.py:34
  16.3 1.6 pad_maximum_fusion.refs_0_
  17.9 4.9 %collective-permute-start = (bf16[32,3584]{1,0:T(8,128)(2,1)}, bf16[32,3584]{1,0:T(8,128)(2,1)}, u32[]{:S(2)}, u32[]{:S(2)}) collective-permute-start(bf16[32,3584]{1,0:T(8,128)(2,1)} %pad_maximum_fusion.refs_0_), channel_id=1, source_target_pairs={{0,16},{16,0},{32,48},{48,32},{64,80},{80,64},{96,112},{112,96},{1... | collective-permute-start | bytes 688136 | tf_op jit(solution)/shard_map/ppermute | solution.py:48
  22.8 1.9 %collective-permute-start.1 = (bf16[32,3584]{1,0:T(8,128)(2,1)}, bf16[32,3584]{1,0:T(8,128)(2,1)}, u32[]{:S(2)}, u32[]{:S(2)}) collective-permute-start(bf16[32,3584]{1,0:T(8,128)(2,1)} %pad_maximum_fusion.refs_0_), channel_id=1, source_target_pairs={{0,128},{16,144},{32,160},{48,176},{64,192},{80,208},{96,224},{112... | collective-permute-start | bytes 688136 | tf_op jit(solution)/shard_map/ppermute | solution.py:48
  24.7 3.5 %collective-permute-start.2 = (bf16[32,3584]{1,0:T(8,128)(2,1)}, bf16[32,3584]{1,0:T(8,128)(2,1)}, u32[]{:S(2)}, u32[]{:S(2)}) collective-permute-start(bf16[32,3584]{1,0:T(8,128)(2,1)} %pad_maximum_fusion.refs_0_), channel_id=1, source_target_pairs={{0,144},{16,128},{32,176},{48,160},{64,208},{80,192},{96,240},{112... | collective-permute-start | bytes 688136 | tf_op jit(solution)/shard_map/ppermute | solution.py:48
  30.7 1.9 %collective-permute-start.3 = (s32[2,4,512]{2,1,0:T(4,128)}, s32[2,4,512]{2,1,0:T(4,128)S(1)}, u32[]{:S(2)}, u32[]{:S(2)}) collective-permute-start(s32[2,4,512]{2,1,0:T(4,128)} %get-tuple-element.70), channel_id=1, source_target_pairs={{0,128},{128,0},{256,384},{384,256},{1,129},{129,1},{257,385},{385... | collective-permute-start | bytes 49160 | tf_op jit(solution)/shard_map/ppermute | solution.py:360
  32.6 4.5 %collective-permute-start.4 = (s32[2,4,512]{2,1,0:T(4,128)}, s32[2,4,512]{2,1,0:T(4,128)S(1)}, u32[]{:S(2)}, u32[]{:S(2)}) collective-permute-start(s32[2,4,512]{2,1,0:T(4,128)} %get-tuple-element.68), channel_id=1, source_target_pairs={{0,256},{128,384},{256,0},{384,128},{1,257},{129,385},{257,1},{385... | collective-permute-start | bytes 49160 | tf_op jit(solution)/shard_map/ppermute | solution.py:360
  38.7 2.5 %middle.1 = (bf16[16,224,256]{2,1,0:T(8,128)(2,1)S(1)}, bf16[64,2048]{1,0:T(8,128)(2,1)S(1)}, bf16[64,2048]{1,0:T(8,128)(2,1)S(1)}) custom-call(bf16[16,224,256]{2,1,0:T(8,128)(2,1)S(1)} %all-to-all-done.weights_ref, bf16[32,3584]{1,0:T(8,128)(2,1)} %pad_maximum_fusion.refs_0_, bf16[32,3584]{1,0:T(8,128)(2,1)} %collective-permute-done.refs_1_, ...), custom_call_target="tpu_custom_call" | custom-call | flops 1073741824 | bytes 6291456 | tf_op jit(solution)/shard_map/middle/pallas_call | solution.py:173
  43.9 6.6 %all-to-all-start.1 = ((bf16[16,224,256]{2,1,0:T(8,128)(2,1)}), bf16[16,224,256]{2,1,0:T(8,128)(2,1)S(1)}, u32[]{:S(2)}, u32[]{:S(2)}) async-start(bf16[16,224,256]{2,1,0:T(8,128)(2,1)} %copy-done.3), calls=%async_computation.1 | async-start | bytes 3670016 | tf_op jit(solution)/shard_map/all_to_all | solution.py:34
  50.5 3.6 %collective-permute-start.7 = (bf16[64,2048]{1,0:T(8,128)(2,1)}, bf16[64,2048]{1,0:T(8,128)(2,1)S(1)}, u32[]{:S(2)}, u32[]{:S(2)}) collective-permute-start(bf16[64,2048]{1,0:T(8,128)(2,1)} %copy-done.8), channel_id=1, source_target_pairs={{0,16},{16,0},{32,48},{48,32},{64,80},{80,64},{96,112},{112,96},{1... | collective-permute-start | bytes 786440 | tf_op jit(solution)/shard_map/ppermute | solution.py:48
  56.5 3.4 %collective-permute-start.8 = (bf16[32,2048]{1,0:T(8,128)(2,1)S(1)}, bf16[32,2048]{1,0:T(8,128)(2,1)S(1)}, u32[]{:S(2)}, u32[]{:S(2)}) collective-permute-start(bf16[32,2048]{1,0:T(8,128)(2,1)S(1)} %get-tuple-element.42), channel_id=1, source_target_pairs={{0,128},{16,144},{32,160},{48,176},{64,192},{80,208},{96,224},{112... | collective-permute-start | bytes 393224 | tf_op jit(solution)/shard_map/ppermute | solution.py:48
  59.8 4.3 %collective-permute-start.5 = (s32[2,4,512]{2,1,0:T(4,128)S(1)}, s32[2,4,512]{2,1,0:T(4,128)S(1)}, u32[]{:S(2)}, u32[]{:S(2)}) collective-permute-start(s32[2,4,512]{2,1,0:T(4,128)S(1)} %get-tuple-element.69), channel_id=1, source_target_pairs={{0,384},{128,256},{256,128},{384,0},{1,385},{129,257},{257,129},{3... | collective-permute-start | bytes 49160 | tf_op jit(solution)/shard_map/ppermute | solution.py:360
  64.1 2.3 %collective-permute-done.5 = s32[2,4,512]{2,1,0:T(4,128)S(1)} collective-permute-done((s32[2,4,512]{2,1,0:T(4,128)S(1)}, s32[2,4,512]{2,1,0:T(4,128)S(1)}, u32[]{:S(2)}, u32[]{:S(2)}) %collective-permute-start.5) | collective-permute-done | bytes 16416 | tf_op jit(solution)/shard_map/ppermute | solution.py:360
  67.0 1.9 %collective-permute-start.6 = (s32[8,4,512]{2,1,0:T(4,128)}, s32[8,4,512]{2,1,0:T(4,128)}, u32[]{:S(2)}, u32[]{:S(2)}) collective-permute-start(s32[8,4,512]{2,1,0:T(4,128)} %pad_add_fusion), channel_id=1, source_target_pairs={{96,0},{112,16},{0,128},{80,144},{64,256},{16,272},{32,384},{48,40... | collective-permute-start | bytes 196616 | tf_op jit(solution)/shard_map/ppermute | solution.py:373
  70.0 1.5 copy.30
  72.9 2.5 %pooled_grads.1.routed_ref = bf16[8,832,128]{2,1,0:T(8,128)(2,1)} custom-call(bf16[32,16,128]{2,1,0:T(8,128)(2,1)S(1)} %bitcast.51, bf16[32,16,192]{2,1,0:T(8,128)(2,1)S(1)} %bitcast.49, bf16[32,16,192]{2,1,0:T(8,128)(2,1)S(1)} %convolution_convert_fusion.comp_ref, bf16[128,128]{1,0:T(8,128)(2,1)S(1)} %copy-done.7, bf16[16,128]{1,0:T(8,128)(2,1)S(1)} %fusion.1.proj_ref), custom_call_target="tpu_custom_call" | custom-call | flops 268435456 | bytes 6291456 | tf_op jit(solution)/shard_map/pooled_grads/pallas_call | solution.py:83
  75.4 4.1 %collective-permute-done.6 = s32[8,4,512]{2,1,0:T(4,128)} collective-permute-done((s32[8,4,512]{2,1,0:T(4,128)}, s32[8,4,512]{2,1,0:T(4,128)}, u32[]{:S(2)}, u32[]{:S(2)}) %collective-permute-start.6) | collective-permute-done | bytes 65568 | tf_op jit(solution)/shard_map/ppermute | solution.py:373
  80.4 10.2 %all-to-all-start.2 = ((bf16[8,832,128]{2,1,0:T(8,128)(2,1)}), bf16[8,832,128]{2,1,0:T(8,128)(2,1)S(1)}, u32[]{:S(2)}, u32[]{:S(2)}) async-start(bf16[8,832,128]{2,1,0:T(8,128)(2,1)} %with_chunks.1), calls=%async_computation.2 | async-start | bytes 3407872 | tf_op jit(solution)/shard_map/all_to_all | solution.py:34
  90.5 3.5 %collective-permute-start.9 = (f32[16,128]{1,0:T(8,128)S(1)}, f32[16,128]{1,0:T(8,128)S(1)}, u32[]{:S(2)}, u32[]{:S(2)}) collective-permute-start(f32[16,128]{1,0:T(8,128)S(1)} %convolution_bitcast_fusion), channel_id=1, source_target_pairs={{0,1},{1,0},{2,3},{3,2},{4,5},{5,4},{6,7},{7,6},{8,9},{9,8},{10,11... | collective-permute-start | bytes 24584 | tf_op jit(solution)/shard_map/ppermute | solution.py:387
  95.4 4.8 %collective-permute-start.10 = (f32[16,128]{1,0:T(8,128)S(1)}, f32[16,128]{1,0:T(8,128)S(1)}, u32[]{:S(2)}, u32[]{:S(2)}) collective-permute-start(f32[16,128]{1,0:T(8,128)S(1)} %add.238), channel_id=1, source_target_pairs={{0,2},{1,3},{2,0},{3,1},{4,6},{5,7},{6,4},{7,5},{8,10},{9,11},{10,... | collective-permute-start | bytes 24584 | tf_op jit(solution)/shard_map/ppermute | solution.py:387
  101.3 3.3 %collective-permute-start.11 = (f32[16,128]{1,0:T(8,128)S(1)}, f32[16,128]{1,0:T(8,128)S(1)}, u32[]{:S(2)}, u32[]{:S(2)}) collective-permute-start(f32[16,128]{1,0:T(8,128)S(1)} %add.239), channel_id=1, source_target_pairs={{0,4},{1,5},{2,6},{3,7},{4,0},{5,1},{6,2},{7,3},{8,12},{9,13},{10,... | collective-permute-start | bytes 24584 | tf_op jit(solution)/shard_map/ppermute | solution.py:387
  104.7 1.4 gather_fusion
  106.1 4.7 %collective-permute-start.12 = (f32[16,128]{1,0:T(8,128)S(1)}, f32[16,128]{1,0:T(8,128)S(1)}, u32[]{:S(2)}, u32[]{:S(2)}) collective-permute-start(f32[16,128]{1,0:T(8,128)S(1)} %add.240), channel_id=1, source_target_pairs={{0,8},{1,9},{2,10},{3,11},{4,12},{5,13},{6,14},{7,15},{8,0},{9,1},... | collective-permute-start | bytes 24584 | tf_op jit(solution)/shard_map/ppermute | solution.py:387
  112.2 18.1 %all-to-all-done.2.values_ref = bf16[8,832,128]{2,1,0:T(8,128)(2,1)S(1)} async-done(((bf16[8,832,128]{2,1,0:T(8,128)(2,1)}), bf16[8,832,128]{2,1,0:T(8,128)(2,1)S(1)}, u32[]{:S(2)}, u32[]{:S(2)}) %all-to-all-start.2) | async-done | bytes 1703968 | tf_op jit(solution)/shard_map/all_to_all | solution.py:34
  131.1 7.9 %all-to-all-start.3 = ((bf16[4,288,128]{2,1,0:T(8,128)(2,1)}), bf16[4,288,128]{2,1,0:T(8,128)(2,1)}, u32[]{:S(2)}, u32[]{:S(2)}) async-start(bf16[4,288,128]{2,1,0:T(8,128)(2,1)} %broadcast_in_dim.47), calls=%async_computation.3 | async-start | bytes 589824 | tf_op jit(solution)/shard_map/all_to_all | solution.py:34
  139.0 6.1 %segment_sums.1 = bf16[1024,192]{1,0:T(8,128)(2,1)S(1)} custom-call(s32[8,4,512]{2,1,0:T(4,128)S(1)} %broadcast_select_fusion.slots_ref, bf16[8,832,128]{2,1,0:T(8,128)(2,1)S(1)} %all-to-all-done.2.values_ref), custom_call_target="tpu_custom_call" | custom-call | flops 2147483648 | bytes 10485760 | tf_op jit(solution)/shard_map/segment_sums/pallas_call | solution.py:233
  145.2 7.3 %collective-permute-start.13 = (bf16[256,192]{0,1:T(8,128)(2,1)S(1)}, bf16[256,192]{0,1:T(8,128)(2,1)S(1)}, u32[]{:S(2)}, u32[]{:S(2)}) collective-permute-start(bf16[256,192]{0,1:T(8,128)(2,1)S(1)} %bitcast.57), channel_id=1, source_target_pairs={{0,96},{16,112},{128,0},{144,80},{256,64},{272,16},{384,32},{400,4... | collective-permute-start | bytes 294920 | tf_op jit(solution)/shard_map/ppermute | solution.py:402
  152.6 5.4 %collective-permute-start.14 = (bf16[256,192]{0,1:T(8,128)(2,1)S(1)}, bf16[256,192]{0,1:T(8,128)(2,1)S(1)}, u32[]{:S(2)}, u32[]{:S(2)}) collective-permute-start(bf16[256,192]{0,1:T(8,128)(2,1)S(1)} %bitcast.58), channel_id=1, source_target_pairs={{0,224},{16,240},{128,128},{144,208},{256,192},{272,144},{384,160}... | collective-permute-start | bytes 294920 | tf_op jit(solution)/shard_map/ppermute | solution.py:402
  158.2 2.2 %collective-permute-start.15 = (bf16[256,192]{0,1:T(8,128)(2,1)S(1)}, bf16[256,192]{0,1:T(8,128)(2,1)S(1)}, u32[]{:S(2)}, u32[]{:S(2)}) collective-permute-start(bf16[256,192]{0,1:T(8,128)(2,1)S(1)} %bitcast.59), channel_id=1, source_target_pairs={{0,352},{16,368},{128,256},{144,336},{256,320},{272,272},{384,288}... | collective-permute-start | bytes 294920 | tf_op jit(solution)/shard_map/ppermute | solution.py:402
  160.5 5.6 %collective-permute-start.16 = (bf16[256,192]{0,1:T(8,128)(2,1)S(1)}, bf16[256,192]{0,1:T(8,128)(2,1)S(1)}, u32[]{:S(2)}, u32[]{:S(2)}) collective-permute-start(bf16[256,192]{0,1:T(8,128)(2,1)S(1)} %bitcast.60), channel_id=1, source_target_pairs={{0,480},{16,496},{128,384},{144,464},{256,448},{272,400},{384,416}... | collective-permute-start | bytes 294920 | tf_op jit(solution)/shard_map/ppermute | solution.py:402
  167.2 19.4 %all-gather = bf16[2304,128]{1,0:T(8,128)(2,1)S(1)} all-gather(bf16[288,128]{1,0:T(8,128)(2,1)S(1)} %pad_maximum_fusion.3), channel_id=2, replica_groups={{0,16,128,144,256,272,384,400},{32,48,160,176,288,304,416,432},{64,80,1..., dimensions={0}, use_global_device_ids=true | all-gather | bytes 663552 | tf_op jit(solution)/shard_map/all_gather | solution.py:396
  (85 shorter events, 27.0 us)
Async XLA Ops:
  0.6 11.0 %copy-start = (bf16[32,128,192]{1,2,0:T(8,128)(2,1)S(1)}, bf16[32,128,192]{1,2,0:T(8,128)(2,1)}, u32[]{:S(2)}) copy-start(bf16[32,128,192]{1,2,0:T(8,128)(2,1)} %param.8) | copy-start | bytes 4718596
  3.9 7.7 %copy-start.9 = (bf16[128,16]{0,1:T(8,128)(2,1)S(1)}, bf16[128,16]{0,1:T(8,128)(2,1)}, u32[]{:S(2)}) copy-start(bf16[128,16]{0,1:T(8,128)(2,1)} %param.9) | copy-start | bytes 12292
  3.9 34.8 %all-to-all-start = ((bf16[16,224,256]{2,1,0:T(8,128)(2,1)}), bf16[16,224,256]{2,1,0:T(8,128)(2,1)S(1)}, u32[]{:S(2)}, u32[]{:S(2)}) async-start(bf16[16,224,256]{2,1,0:T(8,128)(2,1)} %broadcast_in_dim.44), calls=%async_computation | async-start | bytes 3670016 | tf_op jit(solution)/shard_map/all_to_all | solution.py:34
  13.1 0.7 copy-start.1
  13.8 23.3 %copy-start.10 = (s32[128]{0:T(128)S(1)}, s32[128]{0:T(128)}, u32[]{:S(2)}) copy-start(s32[128]{0:T(128)} %param.13) | copy-start | bytes 1540
  17.9 20.8 %collective-permute-start = (bf16[32,3584]{1,0:T(8,128)(2,1)}, bf16[32,3584]{1,0:T(8,128)(2,1)}, u32[]{:S(2)}, u32[]{:S(2)}) collective-permute-start(bf16[32,3584]{1,0:T(8,128)(2,1)} %pad_maximum_fusion.refs_0_), channel_id=1, source_target_pairs={{0,16},{16,0},{32,48},{48,32},{64,80},{80,64},{96,112},{112,96},{1... | collective-permute-start | bytes 688136 | tf_op jit(solution)/shard_map/ppermute | solution.py:48
  22.8 15.9 %collective-permute-start.1 = (bf16[32,3584]{1,0:T(8,128)(2,1)}, bf16[32,3584]{1,0:T(8,128)(2,1)}, u32[]{:S(2)}, u32[]{:S(2)}) collective-permute-start(bf16[32,3584]{1,0:T(8,128)(2,1)} %pad_maximum_fusion.refs_0_), channel_id=1, source_target_pairs={{0,128},{16,144},{32,160},{48,176},{64,192},{80,208},{96,224},{112... | collective-permute-start | bytes 688136 | tf_op jit(solution)/shard_map/ppermute | solution.py:48
  24.7 14.0 %collective-permute-start.2 = (bf16[32,3584]{1,0:T(8,128)(2,1)}, bf16[32,3584]{1,0:T(8,128)(2,1)}, u32[]{:S(2)}, u32[]{:S(2)}) collective-permute-start(bf16[32,3584]{1,0:T(8,128)(2,1)} %pad_maximum_fusion.refs_0_), channel_id=1, source_target_pairs={{0,144},{16,128},{32,176},{48,160},{64,208},{80,192},{96,240},{112... | collective-permute-start | bytes 688136 | tf_op jit(solution)/shard_map/ppermute | solution.py:48
  30.7 6.7 %collective-permute-start.3 = (s32[2,4,512]{2,1,0:T(4,128)}, s32[2,4,512]{2,1,0:T(4,128)S(1)}, u32[]{:S(2)}, u32[]{:S(2)}) collective-permute-start(s32[2,4,512]{2,1,0:T(4,128)} %get-tuple-element.70), channel_id=1, source_target_pairs={{0,128},{128,0},{256,384},{384,256},{1,129},{129,1},{257,385},{385... | collective-permute-start | bytes 49160 | tf_op jit(solution)/shard_map/ppermute | solution.py:360
  32.6 6.1 %collective-permute-start.4 = (s32[2,4,512]{2,1,0:T(4,128)}, s32[2,4,512]{2,1,0:T(4,128)S(1)}, u32[]{:S(2)}, u32[]{:S(2)}) collective-permute-start(s32[2,4,512]{2,1,0:T(4,128)} %get-tuple-element.68), channel_id=1, source_target_pairs={{0,256},{128,384},{256,0},{384,128},{1,257},{129,385},{257,1},{385... | collective-permute-start | bytes 49160 | tf_op jit(solution)/shard_map/ppermute | solution.py:360
  37.3 1.4 copy-start.6
  41.2 1.3 copy-start.3
  42.5 0.7 copy-start.4
  43.2 0.7 copy-start.8
  43.9 35.6 %all-to-all-start.1 = ((bf16[16,224,256]{2,1,0:T(8,128)(2,1)}), bf16[16,224,256]{2,1,0:T(8,128)(2,1)S(1)}, u32[]{:S(2)}, u32[]{:S(2)}) async-start(bf16[16,224,256]{2,1,0:T(8,128)(2,1)} %copy-done.3), calls=%async_computation.1 | async-start | bytes 3670016 | tf_op jit(solution)/shard_map/all_to_all | solution.py:34
  50.5 4.9 %collective-permute-start.7 = (bf16[64,2048]{1,0:T(8,128)(2,1)}, bf16[64,2048]{1,0:T(8,128)(2,1)S(1)}, u32[]{:S(2)}, u32[]{:S(2)}) collective-permute-start(bf16[64,2048]{1,0:T(8,128)(2,1)} %copy-done.8), channel_id=1, source_target_pairs={{0,16},{16,0},{32,48},{48,32},{64,80},{80,64},{96,112},{112,96},{1... | collective-permute-start | bytes 786440 | tf_op jit(solution)/shard_map/ppermute | solution.py:48
  55.4 0.9 copy-start.5
  56.5 12.5 %collective-permute-start.8 = (bf16[32,2048]{1,0:T(8,128)(2,1)S(1)}, bf16[32,2048]{1,0:T(8,128)(2,1)S(1)}, u32[]{:S(2)}, u32[]{:S(2)}) collective-permute-start(bf16[32,2048]{1,0:T(8,128)(2,1)S(1)} %get-tuple-element.42), channel_id=1, source_target_pairs={{0,128},{16,144},{32,160},{48,176},{64,192},{80,208},{96,224},{112... | collective-permute-start | bytes 393224 | tf_op jit(solution)/shard_map/ppermute | solution.py:48
  59.8 6.6 %collective-permute-start.5 = (s32[2,4,512]{2,1,0:T(4,128)S(1)}, s32[2,4,512]{2,1,0:T(4,128)S(1)}, u32[]{:S(2)}, u32[]{:S(2)}) collective-permute-start(s32[2,4,512]{2,1,0:T(4,128)S(1)} %get-tuple-element.69), channel_id=1, source_target_pairs={{0,384},{128,256},{256,128},{384,0},{1,385},{129,257},{257,129},{3... | collective-permute-start | bytes 49160 | tf_op jit(solution)/shard_map/ppermute | solution.py:360
  67.0 12.4 %collective-permute-start.6 = (s32[8,4,512]{2,1,0:T(4,128)}, s32[8,4,512]{2,1,0:T(4,128)}, u32[]{:S(2)}, u32[]{:S(2)}) collective-permute-start(s32[8,4,512]{2,1,0:T(4,128)} %pad_add_fusion), channel_id=1, source_target_pairs={{96,0},{112,16},{0,128},{80,144},{64,256},{16,272},{32,384},{48,40... | collective-permute-start | bytes 196616 | tf_op jit(solution)/shard_map/ppermute | solution.py:373
  71.6 1.3 copy-start.2
  71.6 1.3 copy-start.7
  80.4 49.9 %all-to-all-start.2 = ((bf16[8,832,128]{2,1,0:T(8,128)(2,1)}), bf16[8,832,128]{2,1,0:T(8,128)(2,1)S(1)}, u32[]{:S(2)}, u32[]{:S(2)}) async-start(bf16[8,832,128]{2,1,0:T(8,128)(2,1)} %with_chunks.1), calls=%async_computation.2 | async-start | bytes 3407872 | tf_op jit(solution)/shard_map/all_to_all | solution.py:34
  90.5 4.9 %collective-permute-start.9 = (f32[16,128]{1,0:T(8,128)S(1)}, f32[16,128]{1,0:T(8,128)S(1)}, u32[]{:S(2)}, u32[]{:S(2)}) collective-permute-start(f32[16,128]{1,0:T(8,128)S(1)} %convolution_bitcast_fusion), channel_id=1, source_target_pairs={{0,1},{1,0},{2,3},{3,2},{4,5},{5,4},{6,7},{7,6},{8,9},{9,8},{10,11... | collective-permute-start | bytes 24584 | tf_op jit(solution)/shard_map/ppermute | solution.py:387
  95.4 5.9 %collective-permute-start.10 = (f32[16,128]{1,0:T(8,128)S(1)}, f32[16,128]{1,0:T(8,128)S(1)}, u32[]{:S(2)}, u32[]{:S(2)}) collective-permute-start(f32[16,128]{1,0:T(8,128)S(1)} %add.238), channel_id=1, source_target_pairs={{0,2},{1,3},{2,0},{3,1},{4,6},{5,7},{6,4},{7,5},{8,10},{9,11},{10,... | collective-permute-start | bytes 24584 | tf_op jit(solution)/shard_map/ppermute | solution.py:387
  101.3 4.8 %collective-permute-start.11 = (f32[16,128]{1,0:T(8,128)S(1)}, f32[16,128]{1,0:T(8,128)S(1)}, u32[]{:S(2)}, u32[]{:S(2)}) collective-permute-start(f32[16,128]{1,0:T(8,128)S(1)} %add.239), channel_id=1, source_target_pairs={{0,4},{1,5},{2,6},{3,7},{4,0},{5,1},{6,2},{7,3},{8,12},{9,13},{10,... | collective-permute-start | bytes 24584 | tf_op jit(solution)/shard_map/ppermute | solution.py:387
  106.1 6.0 %collective-permute-start.12 = (f32[16,128]{1,0:T(8,128)S(1)}, f32[16,128]{1,0:T(8,128)S(1)}, u32[]{:S(2)}, u32[]{:S(2)}) collective-permute-start(f32[16,128]{1,0:T(8,128)S(1)} %add.240), channel_id=1, source_target_pairs={{0,8},{1,9},{2,10},{3,11},{4,12},{5,13},{6,14},{7,15},{8,0},{9,1},... | collective-permute-start | bytes 24584 | tf_op jit(solution)/shard_map/ppermute | solution.py:387
  131.1 34.9 %all-to-all-start.3 = ((bf16[4,288,128]{2,1,0:T(8,128)(2,1)}), bf16[4,288,128]{2,1,0:T(8,128)(2,1)}, u32[]{:S(2)}, u32[]{:S(2)}) async-start(bf16[4,288,128]{2,1,0:T(8,128)(2,1)} %broadcast_in_dim.47), calls=%async_computation.3 | async-start | bytes 589824 | tf_op jit(solution)/shard_map/all_to_all | solution.py:34
  145.2 41.3 %collective-permute-start.13 = (bf16[256,192]{0,1:T(8,128)(2,1)S(1)}, bf16[256,192]{0,1:T(8,128)(2,1)S(1)}, u32[]{:S(2)}, u32[]{:S(2)}) collective-permute-start(bf16[256,192]{0,1:T(8,128)(2,1)S(1)} %bitcast.57), channel_id=1, source_target_pairs={{0,96},{16,112},{128,0},{144,80},{256,64},{272,16},{384,32},{400,4... | collective-permute-start | bytes 294920 | tf_op jit(solution)/shard_map/ppermute | solution.py:402
  152.6 33.9 %collective-permute-start.14 = (bf16[256,192]{0,1:T(8,128)(2,1)S(1)}, bf16[256,192]{0,1:T(8,128)(2,1)S(1)}, u32[]{:S(2)}, u32[]{:S(2)}) collective-permute-start(bf16[256,192]{0,1:T(8,128)(2,1)S(1)} %bitcast.58), channel_id=1, source_target_pairs={{0,224},{16,240},{128,128},{144,208},{256,192},{272,144},{384,160}... | collective-permute-start | bytes 294920 | tf_op jit(solution)/shard_map/ppermute | solution.py:402
  158.2 28.4 %collective-permute-start.15 = (bf16[256,192]{0,1:T(8,128)(2,1)S(1)}, bf16[256,192]{0,1:T(8,128)(2,1)S(1)}, u32[]{:S(2)}, u32[]{:S(2)}) collective-permute-start(bf16[256,192]{0,1:T(8,128)(2,1)S(1)} %bitcast.59), channel_id=1, source_target_pairs={{0,352},{16,368},{128,256},{144,336},{256,320},{272,272},{384,288}... | collective-permute-start | bytes 294920 | tf_op jit(solution)/shard_map/ppermute | solution.py:402
  160.5 26.1 %collective-permute-start.16 = (bf16[256,192]{0,1:T(8,128)(2,1)S(1)}, bf16[256,192]{0,1:T(8,128)(2,1)S(1)}, u32[]{:S(2)}, u32[]{:S(2)}) collective-permute-start(bf16[256,192]{0,1:T(8,128)(2,1)S(1)} %bitcast.60), channel_id=1, source_target_pairs={{0,480},{16,496},{128,384},{144,464},{256,448},{272,400},{384,416}... | collective-permute-start | bytes 294920 | tf_op jit(solution)/shard_map/ppermute | solution.py:402
